TPU v7x, 128 devices: a whole 4x4x4 slice. The times are simulated.
128 devices in a mesh: gx: 8 (over y_lo, z), gy: 8 (over y_hi, x), gz: 2 (over core).
Axes of the slice: x: 4, y: 4 (y_hi: 2, y_lo: 2; y = y_hi * 2 + y_lo), z: 4, core: 2. Of those that a mesh axis runs over, the one named last changes fastest.
Arguments:
- velocity: float32 [3, 128, 256, 512], P(None, 'gx', 'gy', 'gz'), may hold values from -6 to 6
- stress: float32 [6, 128, 256, 512], P(None, 'gx', 'gy', 'gz'), may hold values from -6 to 6
- material: int32 [128, 256, 512], P('gx', 'gy', 'gz'), may hold values from 0 to 15
- properties: float32 [16, 3], replicated, may hold values from 0.5 to 2
- owner_map: int32 [64, 512, 1], replicated, may hold values from 0 to 127; in each aligned block of 512 rows (0 to 511, 512 to 1023, ..., all dimensions but the last counted through in order) at most 8 rows name the same one
- cell_map: int32 [64, 512], replicated, may hold values from 0 to 4095
- height: float32 [256, 2048], P('gx', ('gy', 'gz')), may hold values from -6 to 6
- current: float32 [256, 2048], P('gx', ('gy', 'gz')), may hold values from -6 to 6
- sea_depth: float32 [256, 2048], P('gx', ('gy', 'gz')), may hold values from 120 to 240
- wet_mask: int32 [256, 2048], P('gx', ('gy', 'gz')), may hold values 0 or 1
Outputs:
- velocity_out: float32 [3, 128, 256, 512], P(None, 'gx', 'gy', 'gz')
- stress_out: float32 [6, 128, 256, 512], P(None, 'gx', 'gy', 'gz')
- height_out: float32 [256, 2048], P('gx', ('gy', 'gz'))
- current_out: float32 [256, 2048], P('gx', ('gy', 'gz'))
Inputs may be any that keep to these rules, and one draw needn't show every extreme that they name: `owner_map`: among the 512 cells of one tile at most 8 have the same owner, and in some tile exactly 8 do.
All inputs are finite; a program needn't handle non-finite values. No bound on the sum of `wet_mask` on one device may be relied on, other than what follows from the above.
Results may differ from a plain program's by a relative error of at most 0.0003.
Values sent between devices are 32-bit elements; how exact they have to be, the bound alone decides.
No kernel may reach another device: no remote copies, remote signals or barrier semaphores. Data moves between devices by JAX's collectives and lax.ppermute only.
A program may use at most 128 MiB of HBM per device.

v0:
```python
import functools

import jax
import jax.numpy as jnp
from jax import lax
from jax.experimental import pallas as pl
from jax.experimental.pallas import tpu as pltpu
from jax.sharding import PartitionSpec as P

F32 = jnp.float32
CX, CY, CZ = 16, 32, 256
LAT = 128
LON = 32
NB = 8
SX, SY, SZ = (0, 5, 4), (5, 1, 3), (4, 3, 2)
VA = (0, 1, 2)
XF = 3 * 2 * CY
OCR = 80
XR = XF + OCR
YR = 3 * 2 * CX
ZR = 3 * CX * CY
HIGH = lax.Precision.HIGHEST
VM = pl.BlockSpec(memory_space=pltpu.VMEM)
SM = pl.BlockSpec(memory_space=pltpu.SMEM)


def iotas():
    return (
        lax.broadcasted_iota(jnp.int32, (8, 128), 0),
        lax.broadcasted_iota(jnp.int32, (8, 128), 1),
    )


def tile(ref, c, x, t, h):
    return ref[c, x, t * 8 : t * 8 + 8, h * 128 : h * 128 + 128]


def call(body, outs, *args, scratch=(), limit=40):
    return pl.pallas_call(
        body,
        out_shape=outs,
        in_specs=[SM] + [VM] * (len(args) - 1),
        out_specs=[VM] * len(outs),
        scratch_shapes=list(scratch),
        compiler_params=pltpu.CompilerParams(vmem_limit_bytes=limit * 1024 * 1024),
    )(*args)


def shape(*dims):
    return jax.ShapeDtypeStruct(dims, F32)


PAYLOAD = [shape(XR, 128), shape(XR, 128), shape(YR, 128), shape(YR, 128)]


def put_x_faces(ref, comps, pxu, pxd):
    for i, c in enumerate(comps):
        for h in range(2):
            rows = slice(i * 64 + h * 32, i * 64 + h * 32 + 32)
            lanes = slice(h * 128, h * 128 + 128)
            pxu[rows, :] = ref[c, CX - 1, :, lanes]
            pxd[rows, :] = ref[c, 0, :, lanes]


def put_yz(gz, x, i, tiles, pyu, pyd, pz):
    for h in range(2):
        pyu[pl.ds(i * 32 + h * 16 + x, 1), :] = tiles[3][h][7:8, :]
        pyd[pl.ds(i * 32 + h * 16 + x, 1), :] = tiles[0][h][0:1, :]
    put_z(gz, x, i, tiles, pz)


def put_y(x, i, tiles, pyu, pyd):
    for h in range(2):
        pyu[pl.ds(i * 32 + h * 16 + x, 1), :] = tiles[3][h][7:8, :]
        pyd[pl.ds(i * 32 + h * 16 + x, 1), :] = tiles[0][h][0:1, :]


def put_z(gz, x, i, tiles, pz):
    for t in range(4):
        row = pl.multiple_of(i * 512 + x * 32 + t * 8, 8)
        pz[pl.ds(row, 8), :] = jnp.where(gz == 0, tiles[t][1], tiles[t][0])


def prepare(pos, s, depth, height, wet, pxu, pxd, pyu, pyd, pz, fac, rows):
    gz = pos[2]
    put_x_faces(s, SX, pxu, pxd)

    def plane(x, carry):
        for i, c in enumerate(SY):
            put_y(x, i, [[tile(s, c, x, t, h) for h in range(2)] for t in range(4)], pyu, pyd)
        for i, c in enumerate(SZ):
            put_z(gz, x, i, [[tile(s, c, x, t, h) for h in range(2)] for t in range(4)], pz)
        return carry

    lax.fori_loop(0, CX, plane, 0)
    factor(depth, height, wet, pxu, fac, rows)
    pxd[XF:, :] = pxu[XF:, :]


def factor(depth, height, wet, pxu, fac, rows):
    spread = depth[...] * depth[...] / 3.0
    rows[0:32, :] = spread
    w = [None] * LON
    inv = [None] * LON
    right = [None] * LON
    after = jnp.zeros((1, LAT), F32)
    link = jnp.ones((1, LAT), F32)
    for j in reversed(range(LON)):
        sp = rows[j : j + 1, :]
        inv[j] = 1.0 / (1.0 + 2.0 * sp - sp * after)
        w[j] = after = sp * inv[j]
        right[j] = link = w[j] * link
    left_run = jnp.ones((1, LAT), F32)
    right_run = jnp.zeros((1, LAT), F32)
    past = jnp.zeros((1, LAT), F32)
    weight = [None] * LON
    weight[LON - 1] = jnp.ones((1, LAT), F32)
    for j in reversed(range(LON - 1)):
        weight[j] = w[j + 1] * weight[j + 1]
    total = jnp.zeros((1, LAT), F32)
    p_before = q_before = jnp.zeros((1, LAT), F32)
    for j in range(LON):
        p_now = left_run * inv[j]
        total = weight[j] + (w[j - 1] * total if j else 0.0)
        q_now = inv[j] * total
        left_run = w[j] * left_run
        right_run = right[j] + w[j] * right_run
        fac[j : j + 1, :] = left_run
        fac[32 + j : 33 + j, :] = right_run
        fac[64 + j : 65 + j, :] = w[j]
        fac[96 + j : 97 + j, :] = inv[j]
        rows[j : j + 1, :] = p_now - p_before
        rows[32 + j : 33 + j, :] = q_now - q_before
        p_before, q_before = p_now, q_now
    wet_float = wet[...].astype(F32)
    high = height[...]
    a1 = 400.0 * rows[0:32, :] * wet_float
    a2 = 400.0 * rows[32:64, :] * wet_float
    pxu[XF : XF + 32, :] = a1
    pxu[XF + 32 : XF + 64, :] = a2
    base = XF + 64
    pxu[base : base + 1, :] = jnp.sum(a1 * high, axis=0, keepdims=True)
    pxu[base + 1 : base + 2, :] = jnp.sum(a2 * high, axis=0, keepdims=True)
    pxu[base + 2 : base + 3, :] = fac[0:1, :]
    pxu[base + 3 : base + 4, :] = fac[31:32, :]
    pxu[base + 4 : base + 5, :] = fac[32:33, :]
    pxu[base + 5 : base + 6, :] = fac[63:64, :]
    pxu[base + 6 : base + 7, :] = -400.0 * p_before
    pxu[base + 7 : base + 8, :] = -400.0 * q_before
    pxu[base + 8 : base + 9, :] = wet_float[0:1, :]
    pxu[base + 9 : base + 10, :] = wet_float[0:1, :] * high[0:1, :]
    pxu[base + 10 : base + 16, :] = jnp.zeros((6, LAT), F32)


def differences(pos, src, comps, xdn, xup, ydn, yup, zs):
    gx, gy, gz = pos[0], pos[1], pos[2]
    sub, lane = iotas()
    cx, cy, cz = comps
    zero = jnp.zeros((8, 128), F32)

    def flag(cond):
        return jnp.where(cond, 1.0, 0.0).astype(F32)

    m_xd, m_xu = flag(gx > 0), flag(gx < NB - 1)
    m_yd, m_yu = flag(gy > 0), flag(gy < NB - 1)
    m_zd, m_zu = flag(gz == 1), flag(gz == 0)
    top, bottom = sub == 7, sub == 0
    far, near = lane == 127, lane == 0

    def halo_x(ref, mask, i, t, h):
        row = i * 64 + h * 32 + t * 8
        return ref[row : row + 8, :] * mask

    def dx(x, i, t, h, place):
        c = cx[i]
        low = halo_x(xdn, m_xd, i, t, h) if place == "first" else tile(src, c, x - 1, t, h)
        high = halo_x(xup, m_xu, i, t, h) if place == "last" else tile(src, c, x + 1, t, h)
        return high - low

    def dy(x, i, tiles):
        out = [[None, None] for _ in range(4)]
        for h in range(2):
            up = [pltpu.roll(tiles[t][h], 7, 0) for t in range(4)]
            dn = [pltpu.roll(tiles[t][h], 1, 0) for t in range(4)]
            row = i * 32 + h * 16 + x
            up.append(jnp.broadcast_to(yup[pl.ds(row, 1), :] * m_yu, (8, 128)))
            dn.insert(0, jnp.broadcast_to(ydn[pl.ds(row, 1), :] * m_yd, (8, 128)))
            for t in range(4):
                out[t][h] = jnp.where(top, up[t + 1], up[t]) - jnp.where(bottom, dn[t], dn[t + 1])
        return out

    def dz(x, i, tiles):
        out = [[None, None] for _ in range(4)]
        for t in range(4):
            row = pl.multiple_of(i * 512 + x * 32 + t * 8, 8)
            slab = zs[pl.ds(row, 8), :]
            up = [pltpu.roll(tiles[t][h], 127, 1) for h in range(2)] + [pltpu.roll(slab, 127, 1) * m_zu]
            dn = [pltpu.roll(slab, 1, 1) * m_zd] + [pltpu.roll(tiles[t][h], 1, 1) for h in range(2)]
            for h in range(2):
                out[t][h] = jnp.where(far, up[h + 1], up[h]) - jnp.where(near, dn[h], dn[h + 1])
        return out

    return dx, dy, dz


def planes(body):
    body(0, "first")
    lax.fori_loop(1, CX - 1, lambda x, carry: (body(x, "inner"), carry)[1], 0)
    body(CX - 1, "last")


def grab(ref, c, x):
    return [[tile(ref, c, x, t, h) for h in range(2)] for t in range(4)]


def gather(table, index):
    return jnp.take_along_axis(table, index, axis=1, mode="promise_in_bounds")


def move(has_lift, pos, v, s, mat, tab, xdn, xup, ydn, yup, zs, *refs):
    if has_lift:
        lift_in, vo, pxu, pxd, pyu, pyd, pz = refs
    else:
        vo, pxu, pxd, pyu, pyd, pz, lift_out = refs
    gz = pos[2]
    sub, lane = iotas()
    dx, dy, dz = differences(pos, s, (SX, SY, SZ), xdn, xup, ydn, yup, zs)
    buoy = tab[0:8, :]
    lift_rows = (lambda t: slice(ZR + t * 8, ZR + t * 8 + 8)) if has_lift else (lambda t: slice(t * 8, t * 8 + 8))
    lift_ref = pz if has_lift else lift_out
    for t in range(4):
        lift_ref[lift_rows(t), :] = lift_in[t * 8 : t * 8 + 8, :] if has_lift else jnp.zeros((8, 128), F32)

    def plane(x, place):
        weight = [
            [gather(buoy, mat[x, t * 8 : t * 8 + 8, h * 128 : h * 128 + 128]) for h in range(2)]
            for t in range(4)
        ]
        for i in range(3):
            ey = dy(x, i, grab(s, SY[i], x))
            ez = dz(x, i, grab(s, SZ[i], x))
            new = [[None, None] for _ in range(4)]
            for t in range(4):
                for h in range(2):
                    force = dx(x, i, t, h, place) + ey[t][h] + ez[t][h]
                    new[t][h] = tile(v, i, x, t, h) + weight[t][h] * force
                    vo[i, x, t * 8 : t * 8 + 8, h * 128 : h * 128 + 128] = new[t][h]
            put_yz(gz, x, i, new, pyu, pyd, pz)
            if i == 2:
                for t in range(4):
                    old = lift_ref[lift_rows(t), :]
                    column = pltpu.roll(new[t][0], x, 1)
                    lift_ref[lift_rows(t), :] = jnp.where(lane == x, old - 0.25 * column, old)

    planes(plane)
    put_x_faces(vo, VA, pxu, pxd)
    pxu[XF:, :] = xdn[XF:, :]
    pxd[XF:, :] = xup[XF:, :]


def strain(last, pos, s, v, mat, tab, xdn, xup, ydn, yup, zs, *refs):
    if last:
        (so,) = refs
    else:
        so, pxu, pxd, pyu, pyd, pz = refs
    gz = pos[2]
    dx, dy, dz = differences(pos, v, (VA, VA, VA), xdn, xup, ydn, yup, zs)
    first8, second8 = tab[8:16, :], tab[16:24, :]

    def plane(x, place):
        vel = [grab(v, c, x) for c in range(3)]
        ey = [dy(x, c, vel[c]) for c in range(3)]
        ez = [dz(x, c, vel[c]) for c in range(3)]
        new = [[[None, None] for _ in range(4)] for _ in range(6)]
        for t in range(4):
            for h in range(2):
                ex = [dx(x, c, t, h, place) for c in range(3)]
                index = mat[x, t * 8 : t * 8 + 8, h * 128 : h * 128 + 128]
                mu = gather(second8, index)
                bulk = gather(first8, index) * (ex[0] + ey[1][t][h] + ez[2][t][h])
                mu2 = mu + mu
                change = (
                    bulk + mu2 * ex[0],
                    bulk + mu2 * ey[1][t][h],
                    bulk + mu2 * ez[2][t][h],
                    mu * (ez[1][t][h] + ey[2][t][h]),
                    mu * (ez[0][t][h] + ex[2]),
                    mu * (ey[0][t][h] + ex[1]),
                )
                for c in range(6):
                    new[c][t][h] = tile(s, c, x, t, h) + change[c]
                    so[c, x, t * 8 : t * 8 + 8, h * 128 : h * 128 + 128] = new[c][t][h]
        if not last:
            for i in range(3):
                put_y(x, i, new[SY[i]], pyu, pyd)
                put_z(gz, x, i, new[SZ[i]], pz)

    planes(plane)
    if not last:
        put_x_faces(so, SX, pxu, pxd)
        pxu[XF:, :] = xdn[XF:, :]
        pxd[XF:, :] = xup[XF:, :]


def as_column(row, sub, lane):
    parts = []
    for i in range(4):
        part = jnp.broadcast_to(row[:, i * 128 : i * 128 + 128], (128, 128))
        parts.append(jnp.sum(jnp.where(sub == lane, part, 0.0), axis=1, keepdims=True))
    return jnp.concatenate(parts, axis=0)


def address(pos, owner, cell, group, slot, code):
    gz = pos[2]
    sub = lax.broadcasted_iota(jnp.int32, (128, 128), 0)
    lane = lax.broadcasted_iota(jnp.int32, (128, 128), 1)
    own = owner[...]
    column = as_column(own.astype(F32), sub, lane).astype(jnp.int32)
    cells = as_column(cell[...].astype(F32) + 1.0, sub, lane)
    wide = lax.broadcasted_iota(jnp.int32, (512, 128), 1)
    same = (jnp.broadcast_to(column, (512, 128)) == wide).astype(F32)
    earlier = (
        lax.broadcasted_iota(jnp.int32, (512, 512), 1) < lax.broadcasted_iota(jnp.int32, (512, 512), 0)
    ).astype(F32)
    before = jnp.dot(earlier, same, preferred_element_type=F32)
    position = jnp.sum(same * before, axis=1, keepdims=True).astype(jnp.int32)
    place = (column >> 4) * 8 + position
    taken = (jnp.broadcast_to(place, (512, 128)) == wide).astype(F32)
    slot[...] = taken
    rows = lax.broadcasted_iota(jnp.int32, (8, 512), 0)
    mine = jnp.broadcast_to(own, (8, 512))
    chosen = ((((mine >> 1) & 7) == rows) & ((mine & 1) == gz)).astype(F32)
    group[...] = chosen
    found = jnp.dot(chosen, taken * cells, precision=HIGH, preferred_element_type=F32)
    code[...] = pltpu.roll(found, 64, 1)


def pack_lift(pos, pz, zs, group, slot, code, out, wide):
    lift = jnp.where(pos[2] == 0, pz[ZR:, :], zs[ZR:, :])
    for x in range(CX):
        rows = slice(x * 32, x * 32 + 32)
        wide[rows, :] = slot[rows, :] * jnp.broadcast_to(lift[:, x : x + 1], (32, 128))
    row = jnp.dot(group[...], wide[...], precision=HIGH, preferred_element_type=F32) + code[...]
    for i in range(8):
        out[i * 8 : i * 8 + 8, :] = row


def ocean(pos, arrived, height, current, wet, fac, own, d1, u1, d2, u2, d3, u3, d4, ho, co, oc, hot, val, pair, src, ends, sweep):
    gx = pos[0]
    b16 = jnp.bfloat16
    lane = lax.broadcasted_iota(jnp.int32, (32, 128), 1)
    half = lane < 64
    one, two = arrived[0:32, :], arrived[32:64, :]
    value = jnp.where(half, one, pltpu.roll(two, 64, 1))
    cell = jnp.where(half, pltpu.roll(one, 64, 1), two).astype(jnp.int32) - 1
    band = (lane & 63) >> 3
    pair[0:32, :] = jnp.where(cell >= 0, band * 32 + (cell >> 7), -1)
    pair[32:64, :] = cell & 127
    coarse = value.astype(b16).astype(F32)
    val[0:32, :] = coarse
    val[32:64, :] = value - coarse
    lon_rows = lax.broadcasted_iota(jnp.int32, (256, 128), 0)
    lat_rows = lax.broadcasted_iota(jnp.int32, (128, 128), 0)
    for r in range(32):
        cols = slice(r * 128, r * 128 + 128)
        hot[0:256, cols] = (lon_rows == pair[r : r + 1, :]).astype(F32).astype(b16)
        here = lat_rows == pair[32 + r : 33 + r, :]
        hot[256:384, cols] = jnp.where(here, val[r : r + 1, :], 0.0).astype(b16)
        hot[384:512, cols] = jnp.where(here, val[32 + r : 33 + r, :], 0.0).astype(b16)
    both = lax.dot_general(
        hot[0:256, :], hot[256:512, :], (((1,), (1,)), ((), ())), preferred_element_type=F32
    )
    src[...] = both[:, 0:128] + both[:, 128:256]
    for steps, ref in ((0, own), (1, u1), (2, u2), (3, u3), (4, d4), (5, d3), (6, d2), (7, d1)):
        oc[pl.ds(lax.rem(gx + steps, NB), 1), :, :] = ref[XF:, :][None]
    zero = jnp.zeros((1, LAT), F32)

    def extra(b, k):
        return oc[b, 64 + k : 65 + k, :]

    head = [extra(b, 8) * src[b * 32 : b * 32 + 1, :] + extra(b, 9) for b in range(NB)] + [zero]
    y0, yl = [], []
    for b in range(NB):
        s_b = src[b * 32 : b * 32 + 32, :]
        y0.append(jnp.sum(oc[b, 0:32, :] * s_b, axis=0, keepdims=True) + extra(b, 0) + extra(b, 6) * head[b + 1])
        yl.append(jnp.sum(oc[b, 32:64, :] * s_b, axis=0, keepdims=True) + extra(b, 1) + extra(b, 7) * head[b + 1])
    a = [zero] * (NB + 1)
    m = [zero] * (NB + 1)
    zc = [zero] * NB
    zl = [zero] * NB
    for b in reversed(range(NB)):
        scale = 1.0 / (1.0 - extra(b, 5) * m[b + 1])
        zc[b] = scale * (yl[b] + extra(b, 5) * a[b + 1])
        zl[b] = scale * extra(b, 3)
        a[b] = y0[b] + extra(b, 4) * (a[b + 1] + m[b + 1] * zc[b])
        m[b] = extra(b, 2) + extra(b, 4) * m[b + 1] * zl[b]
    z = zero
    ends[0:1, :] = zero
    ends[16 + NB : 17 + NB, :] = zero
    for b in range(NB):
        ends[16 + b : 17 + b, :] = a[b] + m[b] * z
        z = zc[b] + zl[b] * z
        ends[b + 1 : b + 2, :] = z
    left = ends[pl.ds(gx, 1), :]
    right = ends[pl.ds(gx + 17, 1), :]
    wet_float = wet[...].astype(F32)
    new_height = wet_float * (height[...] + src[pl.ds(pl.multiple_of(gx * 32, 32), 32), :])
    ho[...] = new_height
    sweep[0:32, :] = new_height
    nxt = lax.rem(gx + 1, NB)
    next_head = oc[pl.ds(nxt, 1), 72:73, :][0] * src[pl.ds(nxt * 32, 1), :] + oc[pl.ds(nxt, 1), 73:74, :][0]
    sweep[32:33, :] = jnp.where(gx == NB - 1, 0.0, next_head)
    forced = fac[96:128, :] * (-400.0 * (sweep[1:33, :] - new_height))
    sweep[40:72, :] = forced
    run = zero
    offs = [None] * LON
    for j in reversed(range(LON)):
        offs[j] = run = sweep[40 + j : 41 + j, :] + fac[64 + j : 65 + j, :] * run
    run = zero
    for j in range(LON):
        run = offs[j] + fac[64 + j : 65 + j, :] * run
        sweep[40 + j : 41 + j, :] = run
    increment = sweep[40:72, :] + fac[0:32, :] * left + fac[32:64, :] * right
    co[...] = wet_float * (current[...] + increment)


def ring(value, axis, step):
    n = lax.axis_size(axis)
    return lax.ppermute(value, axis, [(i, (i + step) % n) for i in range(n)])


def exchange(payload):
    pxu, pxd, pyu, pyd, pz = payload
    zs = ring(pz, "gz", 1)
    xdn, xup = ring(pxu, "gx", 1), ring(pxd, "gx", -1)
    ydn, yup = ring(pyu, "gy", 1), ring(pyd, "gy", -1)
    return xdn, xup, ydn, yup, zs


def local(velocity, stress, material, properties, owner_map, cell_map, height, current, sea_depth, wet_mask):
    pos = jnp.stack([lax.axis_index(a) for a in ("gx", "gy", "gz")]).astype(jnp.int32)
    scaled = 0.125 * properties.T
    tab = jnp.pad(jnp.concatenate([scaled[2:3], scaled[0:1], scaled[1:2]]), ((0, 0), (0, 112)))
    tab = jnp.repeat(tab, 8, axis=0)
    tile_here = pos[0] * NB + pos[1]
    owner = lax.dynamic_slice_in_dim(owner_map[:, :, 0], tile_here, 1, 0)
    cell = lax.dynamic_slice_in_dim(cell_map, tile_here, 1, 0)

    pz_shape, pz_lift = shape(ZR, 128), shape(ZR + 32, 128)
    v_shape, s_shape = shape(3, CX, CY, CZ), shape(6, CX, CY, CZ)
    *first, fac = call(
        prepare,
        PAYLOAD + [pz_shape, shape(128, LAT)],
        pos, stress, sea_depth, height, wet_mask,
        scratch=[pltpu.VMEM((64, LAT), F32)],
    )
    group, slot, code = call(address, [shape(8, 512), shape(512, 128), shape(8, 128)], pos, owner, cell)
    r1 = exchange(first)
    v1, *sent, lift = call(
        functools.partial(move, False),
        [v_shape] + PAYLOAD + [pz_shape, shape(32, 128)],
        pos, velocity, stress, material, tab, *r1,
    )
    r2 = exchange(sent)
    s1, *sent = call(
        functools.partial(strain, False),
        [s_shape] + PAYLOAD + [pz_shape],
        pos, stress, v1, material, tab, *r2,
    )
    r3 = exchange(sent)
    v2, *sent = call(
        functools.partial(move, True),
        [v_shape] + PAYLOAD + [pz_lift],
        pos, v1, s1, material, tab, *r3, lift,
    )
    r4 = exchange(sent)
    (out,) = call(
        pack_lift, [shape(64, 128)], pos, sent[4], r4[4], group, slot, code,
        scratch=[pltpu.VMEM((512, 128), F32)],
    )
    arrived = lax.all_to_all(out, ("gx", "gy"), split_axis=0, concat_axis=0, tiled=True)
    (s2,) = call(
        functools.partial(strain, True), [s_shape], pos, s1, v2, material, tab, *r4
    )
    height_out, current_out = call(
        ocean, [shape(LON, LAT)] * 2,
        pos, arrived, height, current, wet_mask, fac, first[0],
        r1[0], r1[1], r2[0], r2[1], r3[0], r3[1], r4[0],
        scratch=[
            pltpu.VMEM((NB, OCR, LAT), F32),
            pltpu.VMEM((512, 4096), jnp.bfloat16),
            pltpu.VMEM((64, 128), F32),
            pltpu.VMEM((64, 128), jnp.int32),
            pltpu.VMEM((256, 128), F32),
            pltpu.VMEM((32, 128), F32),
            pltpu.VMEM((72, 128), F32),
        ],
    )
    return v2, s2, height_out, current_out


def solution(mesh):
    return jax.shard_map(
        local,
        mesh=mesh,
        in_specs=(
            P(None, "gx", "gy", "gz"),
            P(None, "gx", "gy", "gz"),
            P("gx", "gy", "gz"),
            P(),
            P(),
            P(),
            P("gx", ("gy", "gz")),
            P("gx", ("gy", "gz")),
            P("gx", ("gy", "gz")),
            P("gx", ("gy", "gz")),
        ),
        out_specs=(
            P(None, "gx", "gy", "gz"),
            P(None, "gx", "gy", "gz"),
            P("gx", ("gy", "gz")),
            P("gx", ("gy", "gz")),
        ),
        check_vma=False,
    )
```

profile of v0, /device:TPU:0, one launch (start us, length us, event | category | flops | bytes accessed | tf_op | source)
XLA Modules:
  0.0 101.3 jit_solution(5217317305236404215)
XLA Ops:
  0.7 1.9 %copy-done.1 = f32[6,16,32,256]{3,2,1,0:T(8,128)S(1)} copy-done((f32[6,16,32,256]{3,2,1,0:T(8,128)S(1)}, f32[6,16,32,256]{3,2,1,0:T(8,128)}, u32[]{:S(2)}) %copy-start.1) | copy-done | bytes 3145752
  4.8 1.1 %shard_map.129 = (f32[272,128]{1,0:T(8,128)S(1)}, f32[272,128]{1,0:T(8,128)S(1)}, f32[96,128]{1,0:T(8,128)S(1)}, f32[96,128]{1,0:T(8,128)S(1)}, f32[1536,128]{1,0:T(8,128)S(1)}, /*index=5*/f32[128,128]{1,0:T(8,128)S(1)}) custom-call(s32[3]{0:T(128)S(1)} %pad_add_fusion.pos, f32[6,16,32,256]{3,2,1,0:T(8,128)S(1)} %copy-done.1, f32[32,128]{1,0:T(8,128)S(1)} %copy-done.30, ...), custom_call_target="tpu_custom_call" | custom-call | tf_op jit(solution)/shard_map/pallas_call | solution.py:39
  6.5 2.0 %collective-permute-start = (f32[272,128]{1,0:T(8,128)S(1)}, f32[272,128]{1,0:T(8,128)S(1)}, u32[]{:S(2)}, u32[]{:S(2)}) collective-permute-start(f32[272,128]{1,0:T(8,128)S(1)} %get-tuple-element.34.own), channel_id=1, source_target_pairs={{0,16},{16,32},{32,48},{48,64},{64,80},{80,96},{96,112},{112,0},{1... | collective-permute-start | bytes 417800 | tf_op jit(solution)/shard_map/ppermute | solution.py:429
  8.5 3.2 %collective-permute-start.1 = (f32[272,128]{1,0:T(8,128)S(1)}, f32[272,128]{1,0:T(8,128)S(1)}, u32[]{:S(2)}, u32[]{:S(2)}) collective-permute-start(f32[272,128]{1,0:T(8,128)S(1)} %get-tuple-element.35), channel_id=1, source_target_pairs={{0,112},{16,0},{32,16},{48,32},{64,48},{80,64},{96,80},{112,96},{1... | collective-permute-start | bytes 417800 | tf_op jit(solution)/shard_map/ppermute | solution.py:429
  11.7 1.5 %collective-permute-start.2 = (f32[96,128]{1,0:T(8,128)S(1)}, f32[96,128]{1,0:T(8,128)S(1)}, u32[]{:S(2)}, u32[]{:S(2)}) collective-permute-start(f32[96,128]{1,0:T(8,128)S(1)} %get-tuple-element.36), channel_id=1, source_target_pairs={{0,2},{2,4},{4,6},{6,8},{8,10},{10,12},{12,14},{14,0},{1,3},{3,5},... | collective-permute-start | bytes 147464 | tf_op jit(solution)/shard_map/ppermute | solution.py:429
  13.2 4.1 %collective-permute-start.3 = (f32[96,128]{1,0:T(8,128)S(1)}, f32[96,128]{1,0:T(8,128)S(1)}, u32[]{:S(2)}, u32[]{:S(2)}) collective-permute-start(f32[96,128]{1,0:T(8,128)S(1)} %get-tuple-element.37), channel_id=1, source_target_pairs={{0,14},{2,0},{4,2},{6,4},{8,6},{10,8},{12,10},{14,12},{1,15},{3,1}... | collective-permute-start | bytes 147464 | tf_op jit(solution)/shard_map/ppermute | solution.py:429
  17.4 2.0 %collective-permute-done.2.ydn = f32[96,128]{1,0:T(8,128)S(1)} collective-permute-done((f32[96,128]{1,0:T(8,128)S(1)}, f32[96,128]{1,0:T(8,128)S(1)}, u32[]{:S(2)}, u32[]{:S(2)}) %collective-permute-start.2) | collective-permute-done | bytes 49184 | tf_op jit(solution)/shard_map/ppermute | solution.py:429
  19.5 3.6 %shard_map.130 = (f32[3,16,32,256]{3,2,1,0:T(8,128)S(1)}, f32[272,128]{1,0:T(8,128)S(1)}, f32[272,128]{1,0:T(8,128)S(1)}, f32[96,128]{1,0:T(8,128)S(1)}, f32[96,...) custom-call(s32[3]{0:T(128)S(1)} %pad_add_fusion.pos, f32[3,16,32,256]{3,2,1,0:T(8,128)S(1)} %copy-done.4, ...), custom_call_target="tpu_custom_call" | custom-call | tf_op jit(solution)/shard_map/pallas_call | solution.py:39
  23.3 4.1 %collective-permute-start.6 = (f32[272,128]{1,0:T(8,128)S(1)}, f32[272,128]{1,0:T(8,128)S(1)}, u32[]{:S(2)}, u32[]{:S(2)}) collective-permute-start(f32[272,128]{1,0:T(8,128)S(1)} %get-tuple-element.41), channel_id=1, source_target_pairs={{0,112},{16,0},{32,16},{48,32},{64,48},{80,64},{96,80},{112,96},{1... | collective-permute-start | bytes 417800 | tf_op jit(solution)/shard_map/ppermute | solution.py:429
  27.4 5.6 %collective-permute-start.8 = (f32[96,128]{1,0:T(8,128)S(1)}, f32[96,128]{1,0:T(8,128)S(1)}, u32[]{:S(2)}, u32[]{:S(2)}) collective-permute-start(f32[96,128]{1,0:T(8,128)S(1)} %get-tuple-element.43), channel_id=1, source_target_pairs={{0,14},{2,0},{4,2},{6,4},{8,6},{10,8},{12,10},{14,12},{1,15},{3,1}... | collective-permute-start | bytes 147464 | tf_op jit(solution)/shard_map/ppermute | solution.py:429
  33.0 2.1 %collective-permute-done.7.ydn = f32[96,128]{1,0:T(8,128)S(1)} collective-permute-done((f32[96,128]{1,0:T(8,128)S(1)}, f32[96,128]{1,0:T(8,128)S(1)}, u32[]{:S(2)}, u32[]{:S(2)}) %collective-permute-start.7) | collective-permute-done | bytes 49184 | tf_op jit(solution)/shard_map/ppermute | solution.py:429
  35.1 3.6 %shard_map.131 = (f32[6,16,32,256]{3,2,1,0:T(8,128)S(1)}, f32[272,128]{1,0:T(8,128)S(1)}, f32[272,128]{1,0:T(8,128)S(1)}, f32[96,128]{1,0:T(8,128)S(1)}, f32[96,128]{1,0:T(8,128)S(1)}, /*index=5*/f32[1536,128]{1,0:T(8,128)S(1)}) custom-call(s32[3]{0:T(128)S(1)} %pad_add_fusion.pos, f32[6,16,32,256]{3,2,1,0:T(8,128)S(1)} %copy-done.1, ...), custom_call_target="tpu_custom_call" | custom-call | tf_op jit(solution)/shard_map/pallas_call | solution.py:39
  38.9 4.1 %collective-permute-start.11 = (f32[272,128]{1,0:T(8,128)S(1)}, f32[272,128]{1,0:T(8,128)S(1)}, u32[]{:S(2)}, u32[]{:S(2)}) collective-permute-start(f32[272,128]{1,0:T(8,128)S(1)} %get-tuple-element.47), channel_id=1, source_target_pairs={{0,112},{16,0},{32,16},{48,32},{64,48},{80,64},{96,80},{112,96},{1... | collective-permute-start | bytes 417800 | tf_op jit(solution)/shard_map/ppermute | solution.py:429
  43.0 1.3 %collective-permute-start.12 = (f32[96,128]{1,0:T(8,128)S(1)}, f32[96,128]{1,0:T(8,128)S(1)}, u32[]{:S(2)}, u32[]{:S(2)}) collective-permute-start(f32[96,128]{1,0:T(8,128)S(1)} %get-tuple-element.48), channel_id=1, source_target_pairs={{0,2},{2,4},{4,6},{6,8},{8,10},{10,12},{12,14},{14,0},{1,3},{3,5},... | collective-permute-start | bytes 147464 | tf_op jit(solution)/shard_map/ppermute | solution.py:429
  44.4 4.3 %collective-permute-start.13 = (f32[96,128]{1,0:T(8,128)S(1)}, f32[96,128]{1,0:T(8,128)S(1)}, u32[]{:S(2)}, u32[]{:S(2)}) collective-permute-start(f32[96,128]{1,0:T(8,128)S(1)} %get-tuple-element.49), channel_id=1, source_target_pairs={{0,14},{2,0},{4,2},{6,4},{8,6},{10,8},{12,10},{14,12},{1,15},{3,1}... | collective-permute-start | bytes 147464 | tf_op jit(solution)/shard_map/ppermute | solution.py:429
  48.7 2.1 %collective-permute-done.12.ydn = f32[96,128]{1,0:T(8,128)S(1)} collective-permute-done((f32[96,128]{1,0:T(8,128)S(1)}, f32[96,128]{1,0:T(8,128)S(1)}, u32[]{:S(2)}, u32[]{:S(2)}) %collective-permute-start.12) | collective-permute-done | bytes 49184 | tf_op jit(solution)/shard_map/ppermute | solution.py:429
  50.8 4.9 %shard_map.132 = (f32[3,16,32,256]{3,2,1,0:T(8,128)}, f32[272,128]{1,0:T(8,128)S(1)}, f32[272,128]{1,0:T(8,128)S(1)}, f32[96,128]{1,0:T(8,128)S(1)}, f32[96,128]{1,0:T(8,128)S(1)}, /*index=5*/f32[1568,128]{1,0:T(8,128)}) custom-call(s32[3]{0:T(128)S(1)} %pad_add_fusion.pos, f32[3,16,32,256]{3,2,1,0:T(8,128)S(1)} %get-tuple-element.39.v, ...), custom_call_target="tpu_custom_call" | custom-call | tf_op jit(solution)/shard_map/pallas_call | solution.py:39
  58.3 4.1 %collective-permute-start.16 = (f32[272,128]{1,0:T(8,128)}, f32[272,128]{1,0:T(8,128)}, u32[]{:S(2)}, u32[]{:S(2)}) collective-permute-start(f32[272,128]{1,0:T(8,128)} %copy-done.32), channel_id=1, source_target_pairs={{0,112},{16,0},{32,16},{48,32},{64,48},{80,64},{96,80},{112,96},{1... | collective-permute-start | bytes 417800 | tf_op jit(solution)/shard_map/ppermute | solution.py:429
  62.5 1.3 %collective-permute-start.17 = (f32[96,128]{1,0:T(8,128)}, f32[96,128]{1,0:T(8,128)}, u32[]{:S(2)}, u32[]{:S(2)}) collective-permute-start(f32[96,128]{1,0:T(8,128)} %copy-done.35), channel_id=1, source_target_pairs={{0,2},{2,4},{4,6},{6,8},{8,10},{10,12},{12,14},{14,0},{1,3},{3,5},... | collective-permute-start | bytes 147464 | tf_op jit(solution)/shard_map/ppermute | solution.py:429
  63.8 4.3 %collective-permute-start.18 = (f32[96,128]{1,0:T(8,128)}, f32[96,128]{1,0:T(8,128)}, u32[]{:S(2)}, u32[]{:S(2)}) collective-permute-start(f32[96,128]{1,0:T(8,128)} %copy-done.34), channel_id=1, source_target_pairs={{0,14},{2,0},{4,2},{6,4},{8,6},{10,8},{12,10},{14,12},{1,15},{3,1}... | collective-permute-start | bytes 147464 | tf_op jit(solution)/shard_map/ppermute | solution.py:429
  69.4 1.9 %shard_map.134 = (f32[8,512]{1,0:T(8,128)S(1)}, f32[512,128]{1,0:T(8,128)S(1)}, f32[8,128]{1,0:T(8,128)S(1)}) custom-call(s32[3]{0:T(128)S(1)} %copy-done.26, s32[1,512]{1,0:T(1,128)S(1)} %dynamic-slice_bitcast_fusion.owner, s32[1,512]{1,0:T(1,128)S(1)} %constant_dynamic-slice_fusion.cell), custom_call_target="tpu_custom_call" | custom-call | tf_op jit(solution)/shard_map/pallas_call | solution.py:39
  72.0 1.7 %shard_map.135 = f32[64,128]{1,0:T(8,128)S(1)} custom-call(s32[3]{0:T(128)S(1)} %copy-done.27, f32[1568,128]{1,0:T(8,128)} %get-tuple-element.57.pz, f32[1568,128]{1,0:T(8,128)} %collective-permute-done.19.zs, f32[8,512]{1,0:T(8,128)S(1)} %get-tuple-element.58.group, f32[512,128]{1,0:T(8,128)S(1)} %get-tuple-element.59.slot, f32[8,128]{1,0:T(8,128)S(1)} %get-tuple-element.60.code), custom_call_target="tpu_custom_call" | custom-call | tf_op jit(solution)/shard_map/pallas_call | solution.py:39
  74.3 5.5 %all-to-all-start = ((f32[64,1,128]{2,1,0:T(1,128)}), f32[64,1,128]{2,1,0:T(1,128)}, u32[]{:S(2)}, u32[]{:S(2)}) async-start(f32[64,1,128]{2,1,0:T(1,128)} %bitcast.13), calls=%async_computation | async-start | bytes 65536 | tf_op jit(solution)/shard_map/all_to_all | solution.py:481
  79.8 1.0 %copy-done.3 = s32[16,32,256]{2,1,0:T(8,128)S(1)} copy-done((s32[16,32,256]{2,1,0:T(8,128)S(1)}, s32[16,32,256]{2,1,0:T(8,128)}, u32[]{:S(2)}) %copy-start.3) | copy-done | bytes 524312
  80.8 1.4 %copy-done.5 = f32[3,16,32,256]{3,2,1,0:T(8,128)S(1)} copy-done((f32[3,16,32,256]{3,2,1,0:T(8,128)S(1)}, f32[3,16,32,256]{3,2,1,0:T(8,128)}, u32[]{:S(2)}) %copy-start.5) | copy-done | bytes 1572888
  83.6 6.0 %shard_map.133 = f32[6,16,32,256]{3,2,1,0:T(8,128)} custom-call(s32[3]{0:T(128)S(1)} %copy-done.28, f32[6,16,32,256]{3,2,1,0:T(8,128)S(1)} %get-tuple-element.45.s, f32[3,16,32,256]{3,2,1,0:T(8,128)S(1)} %copy-done.5, s32[16,32,256]{2,1,0:T(8,128)S(1)} %copy-done.3, f32[24,128]{1,0:T(8,128)S(1)} %copy-done.15, f32[272,128]{1,0:T(8,128)} %collective-permute-done.15.xdn.d4, ...), custom_call_target="tpu_custom_call" | custom-call | tf_op jit(solution)/shard_map/pallas_call | solution.py:39
  89.6 0.9 copy-done.7
  90.5 0.9 copy-done.9
  91.4 0.9 copy-done.11
  92.4 0.9 copy-done.13
  93.3 0.9 copy-done.17
  97.8 3.6 %shard_map.136 = (f32[32,128]{1,0:T(8,128)}, f32[32,128]{1,0:T(8,128)}) custom-call(s32[3]{0:T(128)S(1)} %copy-done.29, f32[64,128]{1,0:T(8,128)} %bitcast.8.arrived, f32[32,128]{1,0:T(8,128)S(1)} %copy-done.20, f32[32,128]{1,0:T(8,128)S(1)} %copy-done.31, s32[32,128]{1,0:T(8,128)S(1)} %copy-done.22, f32[128,128]{1,0:T(8,128)S(1)} %copy-done.24, ...), custom_call_target="tpu_custom_call" | custom-call | tf_op jit(solution)/shard_map/pallas_call | solution.py:39
  (100 shorter events, 13.4 us)
Async XLA Ops:
  0.6 57.6 %copy-start = (s32[64,512]{1,0:T(8,128)S(1)}, s32[64,512]{1,0:T(8,128)}, u32[]{:S(2)}) copy-start(s32[64,512]{1,0:T(8,128)} %param.15) | copy-start | bytes 393220
  0.6 16.7 %copy-start.36 = (f32[16,3]{0,1:T(4,128)S(1)}, f32[16,3]{0,1:T(4,128)}, u32[]{:S(2)}) copy-start(f32[16,3]{0,1:T(4,128)} %param.13) | copy-start | bytes 580
  4.8 46.0 %copy-start.25 = (s32[3]{0:T(128)}, s32[3]{0:T(128)S(1)}, u32[]{:S(2)}) copy-start(s32[3]{0:T(128)S(1)} %pad_add_fusion.pos) | copy-start | bytes 40
  4.8 14.7 %copy-start.2 = (s32[16,32,256]{2,1,0:T(8,128)S(1)}, s32[16,32,256]{2,1,0:T(8,128)}, u32[]{:S(2)}) copy-start(s32[16,32,256]{2,1,0:T(8,128)} %mat.7) | copy-start | bytes 1572868
  4.8 14.7 %copy-start.4 = (f32[3,16,32,256]{3,2,1,0:T(8,128)S(1)}, f32[3,16,32,256]{3,2,1,0:T(8,128)}, u32[]{:S(2)}) copy-start(f32[3,16,32,256]{3,2,1,0:T(8,128)} %v.1) | copy-start | bytes 4718596
  6.5 16.6 %copy-start.16 = (f32[272,128]{1,0:T(8,128)}, f32[272,128]{1,0:T(8,128)S(1)}, u32[]{:S(2)}) copy-start(f32[272,128]{1,0:T(8,128)S(1)} %get-tuple-element.34.own) | copy-start | bytes 417796
  6.5 12.9 %collective-permute-start.4 = (f32[1536,128]{1,0:T(8,128)S(1)}, f32[1536,128]{1,0:T(8,128)S(1)}, u32[]{:S(2)}, u32[]{:S(2)}) collective-permute-start(f32[1536,128]{1,0:T(8,128)S(1)} %get-tuple-element.38), channel_id=1, source_target_pairs={{0,1},{1,0},{2,3},{3,2},{4,5},{5,4},{6,7},{7,6},{8,9},{9,8},{10,11... | collective-permute-start | bytes 2359304 | tf_op jit(solution)/shard_map/ppermute | solution.py:429
  6.5 12.9 %collective-permute-start = (f32[272,128]{1,0:T(8,128)S(1)}, f32[272,128]{1,0:T(8,128)S(1)}, u32[]{:S(2)}, u32[]{:S(2)}) collective-permute-start(f32[272,128]{1,0:T(8,128)S(1)} %get-tuple-element.34.own), channel_id=1, source_target_pairs={{0,16},{16,32},{32,48},{48,64},{64,80},{80,96},{96,112},{112,0},{1... | collective-permute-start | bytes 417800 | tf_op jit(solution)/shard_map/ppermute | solution.py:429
  8.5 10.9 %collective-permute-start.1 = (f32[272,128]{1,0:T(8,128)S(1)}, f32[272,128]{1,0:T(8,128)S(1)}, u32[]{:S(2)}, u32[]{:S(2)}) collective-permute-start(f32[272,128]{1,0:T(8,128)S(1)} %get-tuple-element.35), channel_id=1, source_target_pairs={{0,112},{16,0},{32,16},{48,32},{64,48},{80,64},{96,80},{112,96},{1... | collective-permute-start | bytes 417800 | tf_op jit(solution)/shard_map/ppermute | solution.py:429
  11.7 7.7 %collective-permute-start.2 = (f32[96,128]{1,0:T(8,128)S(1)}, f32[96,128]{1,0:T(8,128)S(1)}, u32[]{:S(2)}, u32[]{:S(2)}) collective-permute-start(f32[96,128]{1,0:T(8,128)S(1)} %get-tuple-element.36), channel_id=1, source_target_pairs={{0,2},{2,4},{4,6},{6,8},{8,10},{10,12},{12,14},{14,0},{1,3},{3,5},... | collective-permute-start | bytes 147464 | tf_op jit(solution)/shard_map/ppermute | solution.py:429
  13.2 6.2 %collective-permute-start.3 = (f32[96,128]{1,0:T(8,128)S(1)}, f32[96,128]{1,0:T(8,128)S(1)}, u32[]{:S(2)}, u32[]{:S(2)}) collective-permute-start(f32[96,128]{1,0:T(8,128)S(1)} %get-tuple-element.37), channel_id=1, source_target_pairs={{0,14},{2,0},{4,2},{6,4},{8,6},{10,8},{12,10},{14,12},{1,15},{3,1}... | collective-permute-start | bytes 147464 | tf_op jit(solution)/shard_map/ppermute | solution.py:429
  17.4 33.4 %copy-start.14 = (f32[24,128]{1,0:T(8,128)}, f32[24,128]{1,0:T(8,128)S(1)}, u32[]{:S(2)}) copy-start(f32[24,128]{1,0:T(8,128)S(1)} %broadcast_bitcast_fusion.tab) | copy-start | bytes 36868
  23.1 12.0 %collective-permute-start.9 = (f32[1536,128]{1,0:T(8,128)S(1)}, f32[1536,128]{1,0:T(8,128)S(1)}, u32[]{:S(2)}, u32[]{:S(2)}) collective-permute-start(f32[1536,128]{1,0:T(8,128)S(1)} %get-tuple-element.44), channel_id=1, source_target_pairs={{0,1},{1,0},{2,3},{3,2},{4,5},{5,4},{6,7},{7,6},{8,9},{9,8},{10,11... | collective-permute-start | bytes 2359304 | tf_op jit(solution)/shard_map/ppermute | solution.py:429
  23.2 11.9 %collective-permute-start.5 = (f32[272,128]{1,0:T(8,128)S(1)}, f32[272,128]{1,0:T(8,128)S(1)}, u32[]{:S(2)}, u32[]{:S(2)}) collective-permute-start(f32[272,128]{1,0:T(8,128)S(1)} %get-tuple-element.40), channel_id=1, source_target_pairs={{0,16},{16,32},{32,48},{48,64},{64,80},{80,96},{96,112},{112,0},{1... | collective-permute-start | bytes 417800 | tf_op jit(solution)/shard_map/ppermute | solution.py:429
  23.3 11.8 %collective-permute-start.6 = (f32[272,128]{1,0:T(8,128)S(1)}, f32[272,128]{1,0:T(8,128)S(1)}, u32[]{:S(2)}, u32[]{:S(2)}) collective-permute-start(f32[272,128]{1,0:T(8,128)S(1)} %get-tuple-element.41), channel_id=1, source_target_pairs={{0,112},{16,0},{32,16},{48,32},{64,48},{80,64},{96,80},{112,96},{1... | collective-permute-start | bytes 417800 | tf_op jit(solution)/shard_map/ppermute | solution.py:429
  27.4 7.7 %collective-permute-start.7 = (f32[96,128]{1,0:T(8,128)S(1)}, f32[96,128]{1,0:T(8,128)S(1)}, u32[]{:S(2)}, u32[]{:S(2)}) collective-permute-start(f32[96,128]{1,0:T(8,128)S(1)} %get-tuple-element.42), channel_id=1, source_target_pairs={{0,2},{2,4},{4,6},{6,8},{8,10},{10,12},{12,14},{14,0},{1,3},{3,5},... | collective-permute-start | bytes 147464 | tf_op jit(solution)/shard_map/ppermute | solution.py:429
  27.4 7.7 %collective-permute-start.8 = (f32[96,128]{1,0:T(8,128)S(1)}, f32[96,128]{1,0:T(8,128)S(1)}, u32[]{:S(2)}, u32[]{:S(2)}) collective-permute-start(f32[96,128]{1,0:T(8,128)S(1)} %get-tuple-element.43), channel_id=1, source_target_pairs={{0,14},{2,0},{4,2},{6,4},{8,6},{10,8},{12,10},{14,12},{1,15},{3,1}... | collective-permute-start | bytes 147464 | tf_op jit(solution)/shard_map/ppermute | solution.py:429
  35.1 3.6 %copy-start.6 = (f32[272,128]{1,0:T(8,128)}, f32[272,128]{1,0:T(8,128)S(1)}, u32[]{:S(2)}) copy-start(f32[272,128]{1,0:T(8,128)S(1)} %collective-permute-done.5.xdn.d2) | copy-start | bytes 417796
  35.1 3.6 %copy-start.8 = (f32[272,128]{1,0:T(8,128)}, f32[272,128]{1,0:T(8,128)S(1)}, u32[]{:S(2)}) copy-start(f32[272,128]{1,0:T(8,128)S(1)} %collective-permute-done.6.xup.u2) | copy-start | bytes 417796
  38.7 12.0 %collective-permute-start.14 = (f32[1536,128]{1,0:T(8,128)S(1)}, f32[1536,128]{1,0:T(8,128)S(1)}, u32[]{:S(2)}, u32[]{:S(2)}) collective-permute-start(f32[1536,128]{1,0:T(8,128)S(1)} %get-tuple-element.50), channel_id=1, source_target_pairs={{0,1},{1,0},{2,3},{3,2},{4,5},{5,4},{6,7},{7,6},{8,9},{9,8},{10,11... | collective-permute-start | bytes 2359304 | tf_op jit(solution)/shard_map/ppermute | solution.py:429
  38.8 11.9 %collective-permute-start.10 = (f32[272,128]{1,0:T(8,128)S(1)}, f32[272,128]{1,0:T(8,128)S(1)}, u32[]{:S(2)}, u32[]{:S(2)}) collective-permute-start(f32[272,128]{1,0:T(8,128)S(1)} %get-tuple-element.46), channel_id=1, source_target_pairs={{0,16},{16,32},{32,48},{48,64},{64,80},{80,96},{96,112},{112,0},{1... | collective-permute-start | bytes 417800 | tf_op jit(solution)/shard_map/ppermute | solution.py:429
  38.9 11.8 %collective-permute-start.11 = (f32[272,128]{1,0:T(8,128)S(1)}, f32[272,128]{1,0:T(8,128)S(1)}, u32[]{:S(2)}, u32[]{:S(2)}) collective-permute-start(f32[272,128]{1,0:T(8,128)S(1)} %get-tuple-element.47), channel_id=1, source_target_pairs={{0,112},{16,0},{32,16},{48,32},{64,48},{80,64},{96,80},{112,96},{1... | collective-permute-start | bytes 417800 | tf_op jit(solution)/shard_map/ppermute | solution.py:429
  43.0 7.7 %collective-permute-start.12 = (f32[96,128]{1,0:T(8,128)S(1)}, f32[96,128]{1,0:T(8,128)S(1)}, u32[]{:S(2)}, u32[]{:S(2)}) collective-permute-start(f32[96,128]{1,0:T(8,128)S(1)} %get-tuple-element.48), channel_id=1, source_target_pairs={{0,2},{2,4},{4,6},{6,8},{8,10},{10,12},{12,14},{14,0},{1,3},{3,5},... | collective-permute-start | bytes 147464 | tf_op jit(solution)/shard_map/ppermute | solution.py:429
  44.4 6.4 %collective-permute-start.13 = (f32[96,128]{1,0:T(8,128)S(1)}, f32[96,128]{1,0:T(8,128)S(1)}, u32[]{:S(2)}, u32[]{:S(2)}) collective-permute-start(f32[96,128]{1,0:T(8,128)S(1)} %get-tuple-element.49), channel_id=1, source_target_pairs={{0,14},{2,0},{4,2},{6,4},{8,6},{10,8},{12,10},{14,12},{1,15},{3,1}... | collective-permute-start | bytes 147464 | tf_op jit(solution)/shard_map/ppermute | solution.py:429
  50.8 5.0 %copy-start.10 = (f32[272,128]{1,0:T(8,128)}, f32[272,128]{1,0:T(8,128)S(1)}, u32[]{:S(2)}) copy-start(f32[272,128]{1,0:T(8,128)S(1)} %collective-permute-done.10.xdn.d3) | copy-start | bytes 417796
  50.8 4.9 %copy-start.12 = (f32[272,128]{1,0:T(8,128)}, f32[272,128]{1,0:T(8,128)S(1)}, u32[]{:S(2)}) copy-start(f32[272,128]{1,0:T(8,128)S(1)} %collective-permute-done.11.xup.u3) | copy-start | bytes 417796
  58.2 13.1 %collective-permute-start.19 = (f32[1568,128]{1,0:T(8,128)}, f32[1568,128]{1,0:T(8,128)}, u32[]{:S(2)}, u32[]{:S(2)}) collective-permute-start(f32[1568,128]{1,0:T(8,128)} %get-tuple-element.57.pz), channel_id=1, source_target_pairs={{0,1},{1,0},{2,3},{3,2},{4,5},{5,4},{6,7},{7,6},{8,9},{9,8},{10,11... | collective-permute-start | bytes 2408456 | tf_op jit(solution)/shard_map/ppermute | solution.py:429
  58.3 21.5 %collective-permute-start.15 = (f32[272,128]{1,0:T(8,128)}, f32[272,128]{1,0:T(8,128)}, u32[]{:S(2)}, u32[]{:S(2)}) collective-permute-start(f32[272,128]{1,0:T(8,128)} %copy-done.33), channel_id=1, source_target_pairs={{0,16},{16,32},{32,48},{48,64},{64,80},{80,96},{96,112},{112,0},{1... | collective-permute-start | bytes 417800 | tf_op jit(solution)/shard_map/ppermute | solution.py:429
  58.3 21.4 %collective-permute-start.16 = (f32[272,128]{1,0:T(8,128)}, f32[272,128]{1,0:T(8,128)}, u32[]{:S(2)}, u32[]{:S(2)}) collective-permute-start(f32[272,128]{1,0:T(8,128)} %copy-done.32), channel_id=1, source_target_pairs={{0,112},{16,0},{32,16},{48,32},{64,48},{80,64},{96,80},{112,96},{1... | collective-permute-start | bytes 417800 | tf_op jit(solution)/shard_map/ppermute | solution.py:429
  62.5 17.3 %collective-permute-start.17 = (f32[96,128]{1,0:T(8,128)}, f32[96,128]{1,0:T(8,128)}, u32[]{:S(2)}, u32[]{:S(2)}) collective-permute-start(f32[96,128]{1,0:T(8,128)} %copy-done.35), channel_id=1, source_target_pairs={{0,2},{2,4},{4,6},{6,8},{8,10},{10,12},{12,14},{14,0},{1,3},{3,5},... | collective-permute-start | bytes 147464 | tf_op jit(solution)/shard_map/ppermute | solution.py:429
  63.8 16.0 %collective-permute-start.18 = (f32[96,128]{1,0:T(8,128)}, f32[96,128]{1,0:T(8,128)}, u32[]{:S(2)}, u32[]{:S(2)}) collective-permute-start(f32[96,128]{1,0:T(8,128)} %copy-done.34), channel_id=1, source_target_pairs={{0,14},{2,0},{4,2},{6,4},{8,6},{10,8},{12,10},{14,12},{1,15},{3,1}... | collective-permute-start | bytes 147464 | tf_op jit(solution)/shard_map/ppermute | solution.py:429
  74.3 15.3 %all-to-all-start = ((f32[64,1,128]{2,1,0:T(1,128)}), f32[64,1,128]{2,1,0:T(1,128)}, u32[]{:S(2)}, u32[]{:S(2)}) async-start(f32[64,1,128]{2,1,0:T(1,128)} %bitcast.13), calls=%async_computation | async-start | bytes 65536 | tf_op jit(solution)/shard_map/all_to_all | solution.py:481
  (26 other events, 21.0 us)
where the time goes:
time: 103 us; the launch traced here: 101 us
  starting transfers between devices  46 us (45%)
  Pallas kernels  26.4 us (26%)
  local copies, waits for them, and re-layouts  21.7 us (21%)
  waiting for transfers between devices  6.19 us (6%)
    ppermute x20, starting transfers between devices, ring(): return lax.ppermute(value, axis, [(i, (i + step) % n) for i in range(n)])  40.5 us
    pallas_call x8, Pallas kernels, call(): pl.pallas_call(body, out_shape=outs, in_specs=[SM] + [VM] * (len(args) -...  26.4 us
    unnamed x74, local copies, waits for them, and re-layouts  21 us
    ppermute x20, waiting for transfers between devices, ring(): return lax.ppermute(value, axis, [(i, (i + step) % n) for i in range(n)])  6.18 us
    all_to_all x1, starting transfers between devices, local(): lax.all_to_all(out, ('gx', 'gy'), split_axis=0, concat_axis=0, tiled=True)  5.45 us
  transfers between devices with their start and end apart: 21, of which 3 were waited for; matrix products, arithmetic and copies ran while one was open for 1% of the time, Pallas kernels for 10%

commit v1 on v0

v1 whole, which is shorter than its diff:
```python
import functools

import jax
import jax.numpy as jnp
from jax import lax
from jax.experimental import pallas as pl
from jax.experimental.pallas import tpu as pltpu
from jax.sharding import PartitionSpec as P

F32 = jnp.float32
CX, CY, CZ = 16, 32, 256
LAT = 128
LON = 32
NB = 8
SX, SY, SZ = (0, 5, 4), (5, 1, 3), (4, 3, 2)
VA = (0, 1, 2)
XF = 3 * 2 * CY
OCR = 80
XR = XF + OCR
YR = 3 * 2 * CX
FAC = NB * OCR
BAG = FAC + 128
HIGH = lax.Precision.HIGHEST
VM = pl.BlockSpec(memory_space=pltpu.VMEM)
HB = pl.BlockSpec(memory_space=pltpu.HBM)


def iotas():
    return (
        lax.broadcasted_iota(jnp.int32, (8, 128), 0),
        lax.broadcasted_iota(jnp.int32, (8, 128), 1),
    )


def tile(ref, c, x, t, h):
    return ref[c, x, t * 8 : t * 8 + 8, h * 128 : h * 128 + 128]


def call(body, outs, *args, scratch=(), ins=None, outs_at=None, aliases=None, limit=20):
    return pl.pallas_call(
        body,
        out_shape=outs,
        in_specs=[VM] * len(args) if ins is None else ins,
        out_specs=[VM] * len(outs) if outs_at is None else outs_at,
        scratch_shapes=list(scratch),
        input_output_aliases=aliases or {},
        compiler_params=pltpu.CompilerParams(vmem_limit_bytes=limit * 1024 * 1024),
    )(*args)


def place():
    return lax.axis_index("gx"), lax.axis_index("gy"), lax.axis_index("gz")


def shape(*dims):
    return jax.ShapeDtypeStruct(dims, F32)


PARTS = 3
def resident(*dims):
    return pltpu.VMEM(dims, F32)


def outside(*arrays):
    return [pltpu.with_memory_space_constraint(a, pltpu.HBM) for a in arrays]


PAYLOAD = [shape(XR, 128), shape(XR, 128), shape(YR, 128), shape(YR, 128)]


def put_x_faces(ref, comps, pxu, pxd):
    for i, c in enumerate(comps):
        for h in range(2):
            rows = slice(i * 64 + h * 32, i * 64 + h * 32 + 32)
            lanes = slice(h * 128, h * 128 + 128)
            pxu[rows, :] = ref[c, CX - 1, :, lanes]
            pxd[rows, :] = ref[c, 0, :, lanes]


def put_y(x, i, tiles, pyu, pyd):
    for h in range(2):
        row = i * 32 + h * 16 + x
        pyu[row : row + 1, :] = tiles[3][h][7:8, :]
        pyd[row : row + 1, :] = tiles[0][h][0:1, :]


def put_z(gz, x, i, tiles, pz):
    for t in range(4):
        pz[i * CX + x, t * 8 : t * 8 + 8, :] = jnp.where(gz == 0, tiles[t][1], tiles[t][0])


def prepare(s, depth, height, wet, pxu, pxd, pyu, pyd, pz, bag, rows, high, deep, damp, edge, sems):
    gx, _, gz = place()
    copies = []

    def start(src, dst):
        copy = pltpu.make_async_copy(src, dst, sems.at[len(copies)])
        copy.start()
        copies.append(copy)

    start(depth, deep)
    start(height, high)
    start(wet, damp)
    for i, c in enumerate(SX):
        for h in range(2):
            lanes = pl.ds(h * 128, 128)
            start(s.at[c, CX - 1, :, lanes], pxu.at[pl.ds(i * 64 + h * 32, 32), :])
            start(s.at[c, 0, :, lanes], pxd.at[pl.ds(i * 64 + h * 32, 32), :])
    for i, c in enumerate(SY):
        start(s.at[c, :, pl.ds(24, 8), :], edge.at[0, i])
        start(s.at[c, :, pl.ds(0, 8), :], edge.at[1, i])
    lanes = pl.ds(pl.multiple_of(128 * (1 - gz), 128), 128)
    for i, c in enumerate(SZ):
        start(s.at[c, :, :, lanes], pz.at[pl.ds(i * CX, CX)])
    for copy in copies[:3]:
        copy.wait()
    factor(deep, high, damp, pxu, bag, rows)
    pxd[XF:, :] = pxu[XF:, :]
    bag[pl.ds(pl.multiple_of(gx * OCR, 8), OCR), :] = pxu[XF:, :]
    for copy in copies[3:]:
        copy.wait()
    for i in range(3):
        for x in range(CX):
            for h in range(2):
                row = i * 32 + h * 16 + x
                lanes = slice(h * 128, h * 128 + 128)
                pyu[row : row + 1, :] = edge[0, i, x, 7:8, lanes]
                pyd[row : row + 1, :] = edge[1, i, x, 0:1, lanes]


def factor(depth, height, wet, pxu, bag, rows):
    spread = depth[...] * depth[...] / 3.0
    rows[0:32, :] = spread
    w = [None] * LON
    inv = [None] * LON
    right = [None] * LON
    after = jnp.zeros((1, LAT), F32)
    link = jnp.ones((1, LAT), F32)
    for j in reversed(range(LON)):
        sp = rows[j : j + 1, :]
        inv[j] = 1.0 / (1.0 + 2.0 * sp - sp * after)
        w[j] = after = sp * inv[j]
        right[j] = link = w[j] * link
    left_run = jnp.ones((1, LAT), F32)
    right_run = jnp.zeros((1, LAT), F32)
    past = jnp.zeros((1, LAT), F32)
    weight = [None] * LON
    weight[LON - 1] = jnp.ones((1, LAT), F32)
    for j in reversed(range(LON - 1)):
        weight[j] = w[j + 1] * weight[j + 1]
    total = jnp.zeros((1, LAT), F32)
    p_before = q_before = jnp.zeros((1, LAT), F32)
    for j in range(LON):
        p_now = left_run * inv[j]
        total = weight[j] + (w[j - 1] * total if j else 0.0)
        q_now = inv[j] * total
        left_run = w[j] * left_run
        right_run = right[j] + w[j] * right_run
        bag[FAC + j : FAC + j + 1, :] = left_run
        bag[FAC + 32 + j : FAC + 33 + j, :] = right_run
        bag[FAC + 64 + j : FAC + 65 + j, :] = w[j]
        bag[FAC + 96 + j : FAC + 97 + j, :] = inv[j]
        if j == 0:
            first_left, first_right = left_run, right_run
        rows[j : j + 1, :] = p_now - p_before
        rows[32 + j : 33 + j, :] = q_now - q_before
        p_before, q_before = p_now, q_now
    wet_float = wet[...].astype(F32)
    high = height[...]
    a1 = 400.0 * rows[0:32, :] * wet_float
    a2 = 400.0 * rows[32:64, :] * wet_float
    pxu[XF : XF + 32, :] = a1
    pxu[XF + 32 : XF + 64, :] = a2
    base = XF + 64
    pxu[base : base + 1, :] = jnp.sum(a1 * high, axis=0, keepdims=True)
    pxu[base + 1 : base + 2, :] = jnp.sum(a2 * high, axis=0, keepdims=True)
    pxu[base + 2 : base + 3, :] = first_left
    pxu[base + 3 : base + 4, :] = left_run
    pxu[base + 4 : base + 5, :] = first_right
    pxu[base + 5 : base + 6, :] = right_run
    pxu[base + 6 : base + 7, :] = -400.0 * p_before
    pxu[base + 7 : base + 8, :] = -400.0 * q_before
    pxu[base + 8 : base + 9, :] = wet_float[0:1, :]
    pxu[base + 9 : base + 10, :] = wet_float[0:1, :] * high[0:1, :]
    pxu[base + 10 : base + 16, :] = jnp.zeros((6, LAT), F32)


def slopes_z(src, comps, out):
    k = lax.broadcasted_iota(jnp.int32, (CZ, CZ), 0)
    n = lax.broadcasted_iota(jnp.int32, (CZ, CZ), 1)
    step = jnp.where(k == n + 1, 1.0, 0.0) - jnp.where(k == n - 1, 1.0, 0.0)
    step = step.astype(jnp.bfloat16)
    for i, c in enumerate(comps):
        full = src[c].reshape(CX * CY, CZ)
        total = None
        for _ in range(PARTS):
            part = full.astype(jnp.bfloat16)
            full = full - part.astype(F32)
            product = jnp.dot(part, step, preferred_element_type=F32)
            total = product if total is None else total + product
        out[i] = total.reshape(CX, CY, CZ)


def differences(src, comps, dzs, xdn, xup, ydn, yup, zs):
    gx, gy, gz = place()
    sub, lane = iotas()
    cx, cy, cz = comps

    def flag(cond):
        return jnp.where(cond, 1.0, 0.0).astype(F32)

    m_xd, m_xu = flag(gx > 0), flag(gx < NB - 1)
    m_yd, m_yu = flag(gy > 0), flag(gy < NB - 1)
    top, bottom = sub == 7, sub == 0
    far, near = (lane == 127) & (gz == 0), (lane == 0) & (gz == 1)
    shift = jnp.where(gz == 0, 127, 1)

    def halo_x(ref, mask, i, t, h):
        row = i * 64 + h * 32 + t * 8
        return ref[row : row + 8, :] * mask

    def dx(x, i, t, h):
        c = cx[i]
        low = halo_x(xdn, m_xd, i, t, h) if x == 0 else tile(src, c, x - 1, t, h)
        high = halo_x(xup, m_xu, i, t, h) if x == CX - 1 else tile(src, c, x + 1, t, h)
        return high - low

    def dy(x, i, tiles):
        out = [[None, None] for _ in range(4)]
        for h in range(2):
            up = [pltpu.roll(tiles[t][h], 7, 0) for t in range(4)]
            dn = [pltpu.roll(tiles[t][h], 1, 0) for t in range(4)]
            row = i * 32 + h * 16 + x
            up.append(jnp.broadcast_to(yup[row : row + 1, :] * m_yu, (8, 128)))
            dn.insert(0, jnp.broadcast_to(ydn[row : row + 1, :] * m_yd, (8, 128)))
            for t in range(4):
                out[t][h] = jnp.where(top, up[t + 1], up[t]) - jnp.where(bottom, dn[t], dn[t + 1])
        return out

    def dz(x, i):
        out = [[None, None] for _ in range(4)]
        for t in range(4):
            slab = pltpu.roll(zs[i * CX + x, t * 8 : t * 8 + 8, :], shift, 1)
            out[t][0] = tile(dzs, i, x, t, 0) - jnp.where(near, slab, 0.0)
            out[t][1] = tile(dzs, i, x, t, 1) + jnp.where(far, slab, 0.0)
        return out

    return dx, dy, dz


def grab(ref, c, x):
    return [[tile(ref, c, x, t, h) for h in range(2)] for t in range(4)]


def lookup(tab, mat, coef, rows):
    table = [tab[i * 8 : i * 8 + 8, :] for i in rows]

    def plane(x, carry):
        for t in range(4):
            for h in range(2):
                index = mat[x, t * 8 : t * 8 + 8, h * 128 : h * 128 + 128]
                for i in range(len(rows)):
                    coef[i, x, t * 8 : t * 8 + 8, h * 128 : h * 128 + 128] = jnp.take_along_axis(
                        table[i], index, axis=1, mode="promise_in_bounds"
                    )
        return carry

    lax.fori_loop(0, CX, plane, 0)


def fetch(v_hbm, s_hbm, mat_hbm, tab, v, s, mat, coef, sems):
    copies = [
        pltpu.make_async_copy(a, b, sems.at[i])
        for i, (a, b) in enumerate(((mat_hbm, mat), (s_hbm, s), (v_hbm, v)))
    ]
    for copy in copies:
        copy.start()
    copies[0].wait()
    lookup(tab, mat, coef, (0,))
    copies[1].wait()
    copies[2].wait()


def lame(tab, mat, coef):
    lookup(tab, mat, coef, (1, 2))


def collect(distance, xdn, xup, bag):
    gx = lax.axis_index("gx")
    for ref, steps in ((xdn, NB - distance), (xup, distance)):
        row = pl.multiple_of(lax.rem(gx + steps, NB) * OCR, 8)
        bag[pl.ds(row, OCR), :] = ref[XF:, :]


def move(distance, has_lift, v, s, coef, xdn, xup, ydn, yup, zs, bag_in, *refs):
    if has_lift:
        lift_in, vo, pxu, pxd, pyu, pyd, pz, lift_out, bag, dzs = refs
    else:
        vo, pxu, pxd, pyu, pyd, pz, lift_out, bag, dzs = refs
    gz = lax.axis_index("gz")
    sub, lane = iotas()
    collect(distance, xdn, xup, bag)
    slopes_z(s, SZ, dzs)
    dx, dy, dz = differences(s, (SX, SY, SZ), dzs, xdn, xup, ydn, yup, zs)
    lift = [lift_in[t * 8 : t * 8 + 8, :] if has_lift else jnp.zeros((8, 128), F32) for t in range(4)]
    for x in range(CX):
        for i in range(3):
            ey = dy(x, i, grab(s, SY[i], x))
            ez = dz(x, i)
            new = [[None, None] for _ in range(4)]
            for t in range(4):
                for h in range(2):
                    force = dx(x, i, t, h) + ey[t][h] + ez[t][h]
                    new[t][h] = tile(v, i, x, t, h) + tile(coef, 0, x, t, h) * force
                    vo[i, x, t * 8 : t * 8 + 8, h * 128 : h * 128 + 128] = new[t][h]
            put_y(x, i, new, pyu, pyd)
            put_z(gz, x, i, new, pz)
        for t in range(4):
            lift[t] = jnp.where(lane == x, lift[t] - 0.25 * pltpu.roll(new[t][0], x, 1), lift[t])
    for t in range(4):
        lift_out[t * 8 : t * 8 + 8, :] = lift[t]
        if has_lift:
            pz[3 * CX, t * 8 : t * 8 + 8, :] = lift[t]
    put_x_faces(vo, VA, pxu, pxd)
    pxu[XF:, :] = xdn[XF:, :]
    pxd[XF:, :] = xup[XF:, :]


def strain(distance, last, s, v, coef, xdn, xup, ydn, yup, zs, *refs):
    if last:
        bag, lift, group, slot, code, v_hbm, s_hbm, out_hbm, bag_hbm, far_hbm, so, dzs, out, wide, sems = refs
        copies = [
            pltpu.make_async_copy(v, v_hbm, sems.at[CX]),
            pltpu.make_async_copy(bag, bag_hbm, sems.at[CX + 1]),
            pltpu.make_async_copy(xdn.at[pl.ds(XF, OCR), :], far_hbm, sems.at[CX + 2]),
            pltpu.make_async_copy(out, out_hbm, sems.at[CX + 3]),
        ]
        pack_lift(jnp.where(lax.axis_index("gz") == 0, lift[...], zs[3 * CX]), group, slot, code, out, wide)
        for copy in copies:
            copy.start()
    else:
        bag_in, so, pxu, pxd, pyu, pyd, pz, bag, dzs = refs
        collect(distance, xdn, xup, bag)
    gz = lax.axis_index("gz")
    slopes_z(v, VA, dzs)
    dx, dy, dz = differences(v, (VA, VA, VA), dzs, xdn, xup, ydn, yup, zs)
    for x in range(CX):
        ey = [dy(x, c, grab(v, c, x)) for c in range(3)]
        ez = [dz(x, c) for c in range(3)]
        new = [[[None, None] for _ in range(4)] for _ in range(6)]
        for t in range(4):
            for h in range(2):
                ex = [dx(x, c, t, h) for c in range(3)]
                mu = tile(coef, 1, x, t, h)
                bulk = tile(coef, 0, x, t, h) * (ex[0] + ey[1][t][h] + ez[2][t][h])
                mu2 = mu + mu
                change = (
                    bulk + mu2 * ex[0],
                    bulk + mu2 * ey[1][t][h],
                    bulk + mu2 * ez[2][t][h],
                    mu * (ez[1][t][h] + ey[2][t][h]),
                    mu * (ez[0][t][h] + ex[2]),
                    mu * (ey[0][t][h] + ex[1]),
                )
                for c in range(6):
                    new[c][t][h] = tile(s, c, x, t, h) + change[c]
                    so[c, x, t * 8 : t * 8 + 8, h * 128 : h * 128 + 128] = new[c][t][h]
        if last:
            copies.append(pltpu.make_async_copy(so.at[:, x], s_hbm.at[:, x], sems.at[x]))
            copies[-1].start()
        else:
            for i in range(3):
                put_y(x, i, new[SY[i]], pyu, pyd)
                put_z(gz, x, i, new[SZ[i]], pz)
    if last:
        for copy in copies:
            copy.wait()
    else:
        put_x_faces(so, SX, pxu, pxd)
        pxu[XF:, :] = xdn[XF:, :]
        pxd[XF:, :] = xup[XF:, :]


def as_column(row, sub, lane):
    parts = []
    for i in range(4):
        part = jnp.broadcast_to(row[:, i * 128 : i * 128 + 128], (128, 128))
        parts.append(jnp.sum(jnp.where(sub == lane, part, 0.0), axis=1, keepdims=True))
    return jnp.concatenate(parts, axis=0)


def address(owners, cell_rows, group, slot, code, owner, cell, sems):
    gx, gy, gz = place()
    copies = [
        pltpu.make_async_copy(owners.at[gx * NB + gy], owner, sems.at[0]),
        pltpu.make_async_copy(cell_rows.at[pl.ds(pl.multiple_of(gx * NB, 8), 8), :], cell, sems.at[1]),
    ]
    for copy in copies:
        copy.start()
    for copy in copies:
        copy.wait()
    sub = lax.broadcasted_iota(jnp.int32, (128, 128), 0)
    lane = lax.broadcasted_iota(jnp.int32, (128, 128), 1)
    own = owner[...]
    column = as_column(own.astype(F32), sub, lane).astype(jnp.int32)
    cells = as_column(cell[pl.ds(gy, 1), :].astype(F32) + 1.0, sub, lane)
    wide = lax.broadcasted_iota(jnp.int32, (512, 128), 1)
    same = (jnp.broadcast_to(column, (512, 128)) == wide).astype(F32)
    earlier = (
        lax.broadcasted_iota(jnp.int32, (512, 512), 1) < lax.broadcasted_iota(jnp.int32, (512, 512), 0)
    ).astype(F32)
    before = jnp.dot(earlier, same, preferred_element_type=F32)
    position = jnp.sum(same * before, axis=1, keepdims=True).astype(jnp.int32)
    spot = (column >> 4) * 8 + position
    taken = (jnp.broadcast_to(spot, (512, 128)) == wide).astype(F32)
    slot[...] = taken
    rows = lax.broadcasted_iota(jnp.int32, (8, 512), 0)
    mine = jnp.broadcast_to(own, (8, 512))
    chosen = ((((mine >> 1) & 7) == rows) & ((mine & 1) == gz)).astype(F32)
    group[...] = chosen
    found = jnp.dot(chosen, taken * cells, precision=HIGH, preferred_element_type=F32)
    code[...] = pltpu.roll(found, 64, 1)


def pack_lift(lift, group, slot, code, out, wide):
    for x in range(CX):
        rows = slice(x * 32, x * 32 + 32)
        wide[rows, :] = slot[rows, :] * jnp.broadcast_to(lift[:, x : x + 1], (32, 128))
    row = jnp.dot(group[...], wide[...], precision=HIGH, preferred_element_type=F32) + code[...]
    for i in range(8):
        out[i * 8 : i * 8 + 8, :] = row


def ocean(arrived_in, far_in, bag_in, height_in, current_in, wet_in, ho, co, arrived, far, bag, height, current, wet, hot, val, pair, src, ends, sweep, sems):
    gx = lax.axis_index("gx")
    copies = [
        pltpu.make_async_copy(a, b, sems.at[i])
        for i, (a, b) in enumerate(
            (
                (arrived_in, arrived),
                (far_in, far),
                (bag_in, bag),
                (height_in, height),
                (current_in, current),
                (wet_in, wet),
            )
        )
    ]
    for copy in copies:
        copy.start()
    copies[0].wait()
    b16 = jnp.bfloat16
    lane = lax.broadcasted_iota(jnp.int32, (32, 128), 1)
    half = lane < 64
    one, two = arrived[0:32, :], arrived[32:64, :]
    value = jnp.where(half, one, pltpu.roll(two, 64, 1))
    cell = jnp.where(half, pltpu.roll(one, 64, 1), two).astype(jnp.int32) - 1
    band = (lane & 63) >> 3
    pair[0:32, :] = jnp.where(cell >= 0, band * 32 + (cell >> 7), -1)
    pair[32:64, :] = cell & 127
    coarse = value.astype(b16).astype(F32)
    val[0:32, :] = coarse
    val[32:64, :] = value - coarse
    lon_rows = lax.broadcasted_iota(jnp.int32, (256, 128), 0)
    lat_rows = lax.broadcasted_iota(jnp.int32, (128, 128), 0)
    for r in range(32):
        cols = slice(r * 128, r * 128 + 128)
        hot[0:256, cols] = (lon_rows == pair[r : r + 1, :]).astype(F32).astype(b16)
        here = lat_rows == pair[32 + r : 33 + r, :]
        hot[256:384, cols] = jnp.where(here, val[r : r + 1, :], 0.0).astype(b16)
        hot[384:512, cols] = jnp.where(here, val[32 + r : 33 + r, :], 0.0).astype(b16)
    both = lax.dot_general(
        hot[0:256, :], hot[256:512, :], (((1,), (1,)), ((), ())), preferred_element_type=F32
    )
    src[...] = both[:, 0:128] + both[:, 128:256]
    for copy in copies[1:]:
        copy.wait()
    opposite = lax.rem(gx + 4, NB) * OCR
    bag_rows = lambda b, k, n: jnp.where(opposite == b * OCR, far[k : k + n, :], bag[b * OCR + k : b * OCR + k + n, :])
    zero = jnp.zeros((1, LAT), F32)

    def extra(b, k):
        return bag_rows(b, 64 + k, 1)

    head = [extra(b, 8) * src[b * 32 : b * 32 + 1, :] + extra(b, 9) for b in range(NB)] + [zero]
    y0, yl = [], []
    for b in range(NB):
        s_b = src[b * 32 : b * 32 + 32, :]
        y0.append(jnp.sum(bag_rows(b, 0, 32) * s_b, axis=0, keepdims=True) + extra(b, 0) + extra(b, 6) * head[b + 1])
        yl.append(jnp.sum(bag_rows(b, 32, 32) * s_b, axis=0, keepdims=True) + extra(b, 1) + extra(b, 7) * head[b + 1])
    a = [zero] * (NB + 1)
    m = [zero] * (NB + 1)
    zc = [zero] * NB
    zl = [zero] * NB
    for b in reversed(range(NB)):
        scale = 1.0 / (1.0 - extra(b, 5) * m[b + 1])
        zc[b] = scale * (yl[b] + extra(b, 5) * a[b + 1])
        zl[b] = scale * extra(b, 3)
        a[b] = y0[b] + extra(b, 4) * (a[b + 1] + m[b + 1] * zc[b])
        m[b] = extra(b, 2) + extra(b, 4) * m[b + 1] * zl[b]
    z = zero
    ends[0:1, :] = zero
    ends[16 + NB : 17 + NB, :] = zero
    for b in range(NB):
        ends[16 + b : 17 + b, :] = a[b] + m[b] * z
        z = zc[b] + zl[b] * z
        ends[b + 1 : b + 2, :] = z
    left = ends[pl.ds(gx, 1), :]
    right = ends[pl.ds(gx + 17, 1), :]
    wet_float = wet[...].astype(F32)
    new_height = wet_float * (height[...] + src[pl.ds(pl.multiple_of(gx * 32, 32), 32), :])
    ho[...] = new_height
    sweep[0:32, :] = new_height
    nxt = lax.rem(gx + 1, NB)
    next_head = bag[pl.ds(nxt * OCR + 72, 1), :] * src[pl.ds(nxt * 32, 1), :] + bag[pl.ds(nxt * OCR + 73, 1), :]
    sweep[32:33, :] = jnp.where(gx == NB - 1, 0.0, next_head)
    forced = bag[FAC + 96 : FAC + 128, :] * (-400.0 * (sweep[1:33, :] - new_height))
    sweep[40:72, :] = forced
    run = zero
    offs = [None] * LON
    for j in reversed(range(LON)):
        offs[j] = run = sweep[40 + j : 41 + j, :] + bag[FAC + 64 + j : FAC + 65 + j, :] * run
    run = zero
    for j in range(LON):
        run = offs[j] + bag[FAC + 64 + j : FAC + 65 + j, :] * run
        sweep[40 + j : 41 + j, :] = run
    increment = sweep[40:72, :] + bag[FAC : FAC + 32, :] * left + bag[FAC + 32 : FAC + 64, :] * right
    co[...] = wet_float * (current[...] + increment)


def ring(value, axis, step):
    n = lax.axis_size(axis)
    return lax.ppermute(value, axis, [(i, (i + step) % n) for i in range(n)])


def exchange(payload):
    pxu, pxd, pyu, pyd, pz = payload
    zs = ring(pz, "gz", 1)
    xdn, xup = ring(pxu, "gx", 1), ring(pxd, "gx", -1)
    ydn, yup = ring(pyu, "gy", 1), ring(pyd, "gy", -1)
    return xdn, xup, ydn, yup, zs


def local(velocity, stress, material, properties, owner_map, cell_map, height, current, sea_depth, wet_mask):
    scaled = 0.125 * properties.T
    tab = jnp.pad(jnp.concatenate([scaled[2:3], scaled[0:1], scaled[1:2]]), ((0, 0), (0, 112)))
    tab = jnp.repeat(tab, 8, axis=0)
    pz_shape, pz_lift = shape(3 * CX, CY, 128), shape(3 * CX + 1, CY, 128)
    v_shape, s_shape = resident(3, CX, CY, CZ), resident(6, CX, CY, CZ)
    bag_shape = shape(BAG, 128)
    plane_z = pltpu.VMEM((3, CX, CY, CZ), F32)
    *sent, bag = call(
        prepare,
        PAYLOAD + [pz_shape, bag_shape],
        *outside(stress, sea_depth, height, wet_mask),
        ins=[HB] * 4,
        scratch=[
            pltpu.VMEM((64, LAT), F32),
            pltpu.VMEM((LON, LAT), F32),
            pltpu.VMEM((LON, LAT), F32),
            pltpu.VMEM((LON, LAT), jnp.int32),
            pltpu.VMEM((2, 3, CX, 8, CZ), F32),
            pltpu.SemaphoreType.DMA((24,)),
        ],
    )
    r1 = exchange(sent)
    velocity, stress, mat, coef = call(
        fetch,
        [v_shape, s_shape, pltpu.VMEM((CX, CY, CZ), jnp.int32), resident(1, CX, CY, CZ)],
        *outside(velocity, stress, material), tab,
        ins=[HB] * 3 + [VM],
        scratch=[pltpu.SemaphoreType.DMA((3,))],
    )
    v1, *sent, lift, bag = call(
        functools.partial(move, 1, False),
        [v_shape] + PAYLOAD + [pz_shape, shape(32, 128), bag_shape],
        velocity, stress, coef, *r1, bag,
        scratch=[plane_z], aliases={0: 0, 8: 7},
    )
    r2 = exchange(sent)
    mat, v1 = lax.optimization_barrier((mat, v1))
    (coef2,) = call(lame, [resident(2, CX, CY, CZ)], tab, mat)
    s1, *sent, bag = call(
        functools.partial(strain, 2, False),
        [s_shape] + PAYLOAD + [pz_shape, bag_shape],
        stress, v1, coef2, *r2, bag,
        scratch=[plane_z], aliases={0: 0, 8: 6},
    )
    r3 = exchange(sent)
    owners, cells, s1 = lax.optimization_barrier((owner_map.reshape(64, 1, 512), cell_map, s1))
    group, slot, code = call(
        address,
        [shape(8, 512), shape(512, 128), shape(8, 128)],
        *outside(owners, cells),
        ins=[HB] * 2,
        scratch=[
            pltpu.VMEM((1, 512), jnp.int32),
            pltpu.VMEM((8, 512), jnp.int32),
            pltpu.SemaphoreType.DMA((2,)),
        ],
    )
    r3, group, slot, code = lax.optimization_barrier((r3, group, slot, code))
    v2, *sent, lift, bag = call(
        functools.partial(move, 3, True),
        [v_shape] + PAYLOAD + [pz_lift, shape(32, 128), bag_shape],
        v1, s1, coef, *r3, bag, lift,
        scratch=[plane_z], aliases={0: 0, 8: 7},
    )
    r4 = exchange(sent)
    v_out, s2, out, bag, far = call(
        functools.partial(strain, 4, True),
        [pltpu.HBM(dims, F32) for dims in ((3, CX, CY, CZ), (6, CX, CY, CZ), (64, 128), (BAG, 128), (OCR, 128))],
        s1, v2, coef2, *r4, bag, lift, group, slot, code,
        outs_at=[HB] * 5,
        scratch=[
            pltpu.VMEM((6, CX, CY, CZ), F32),
            plane_z,
            pltpu.VMEM((64, 128), F32),
            pltpu.VMEM((512, 128), F32),
            pltpu.SemaphoreType.DMA((CX + 4,)),
        ],
    )
    arrived = lax.all_to_all(out, ("gx", "gy"), split_axis=0, concat_axis=0, tiled=True)
    block = pltpu.VMEM((LON, LAT), F32)
    height_out, current_out = call(
        ocean, [shape(LON, LAT)] * 2,
        *outside(arrived, far, bag, height, current, wet_mask),
        ins=[HB] * 6,
        scratch=[
            pltpu.VMEM((64, 128), F32), pltpu.VMEM((OCR, 128), F32), pltpu.VMEM((BAG, 128), F32),
            block, block, pltpu.VMEM((LON, LAT), jnp.int32),
            pltpu.VMEM((512, 4096), jnp.bfloat16),
            pltpu.VMEM((64, 128), F32),
            pltpu.VMEM((64, 128), jnp.int32),
            pltpu.VMEM((256, 128), F32),
            pltpu.VMEM((32, 128), F32),
            pltpu.VMEM((72, 128), F32),
            pltpu.SemaphoreType.DMA((6,)),
        ],
    )
    return v_out, s2, height_out, current_out


def solution(mesh):
    return jax.shard_map(
        local,
        mesh=mesh,
        in_specs=(
            P(None, "gx", "gy", "gz"),
            P(None, "gx", "gy", "gz"),
            P("gx", "gy", "gz"),
            P(),
            P(),
            P(),
            P("gx", ("gy", "gz")),
            P("gx", ("gy", "gz")),
            P("gx", ("gy", "gz")),
            P("gx", ("gy", "gz")),
        ),
        out_specs=(
            P(None, "gx", "gy", "gz"),
            P(None, "gx", "gy", "gz"),
            P("gx", ("gy", "gz")),
            P("gx", ("gy", "gz")),
        ),
        check_vma=False,
    )
```

time: 103 us -> 84.5 us (0.82); the launches traced: 101 us -> 84.2 us
  local copies, waits for them, and re-layouts: 21.7 us -> 0.02 us
  blocking collectives: 0 us -> 18.2 us
  Pallas kernels: 26.4 us -> 20.7 us
  starting transfers between devices: 46 us -> 40.7 us
  waiting for transfers between devices: 6.19 us -> 3.7 us
    unnamed x74 -> x2, local copies, waits for them, and re-layouts: 21 us -> 0.01 us
    all_to_all x0 -> x1, blocking collectives: none -> 18.2 us  [local(): lax.all_to_all(out, ('gx', 'gy'), split_axis=0, concat_axis=0, tiled=True)]
    pallas_call x8 -> x9, Pallas kernels: 26.4 us -> 20.7 us  [call(): pl.pallas_call(body, out_shape=outs, in_specs=[VM] * len(args) if ins is...]
    all_to_all x1 -> x0, starting transfers between devices: 5.45 us -> none  [local(): lax.all_to_all(out, ('gx', 'gy'), split_axis=0, concat_axis=0, tiled=True)]
    ppermute x20, waiting for transfers between devices: 6.18 us -> 3.7 us  [ring(): return lax.ppermute(value, axis, [(i, (i + step) % n) for i in range(n)])]
  transfers between devices with their start and end apart: 21 -> 20, of which waited for: 3 -> 3; matrix products, arithmetic and copies ran while one was open for 1% -> 0% of each run, Pallas kernels for 10% -> 8%
where the time goes in v1:
time: 84.5 us; the launch traced here: 84.2 us
  starting transfers between devices  40.7 us (48%)
  Pallas kernels  20.7 us (24%)
  blocking collectives  18.2 us (22%)
  waiting for transfers between devices  3.7 us (4%)
  between operations  1.01 us (1%)
    ppermute x20, starting transfers between devices, ring(): return lax.ppermute(value, axis, [(i, (i + step) % n) for i in range(n)])  40.7 us
    pallas_call x9, Pallas kernels, call(): pl.pallas_call(body, out_shape=outs, in_specs=[VM] * len(args) if ins is...  20.7 us
    all_to_all x1, blocking collectives, local(): lax.all_to_all(out, ('gx', 'gy'), split_axis=0, concat_axis=0, tiled=True)  18.2 us
    ppermute x20, waiting for transfers between devices, ring(): return lax.ppermute(value, axis, [(i, (i + step) % n) for i in range(n)])  3.7 us
  transfers between devices with their start and end apart: 20, of which 3 were waited for; matrix products, arithmetic and copies ran while one was open for 0% of the time, Pallas kernels for 8%

profile of v1, /device:TPU:0, one launch (start us, length us, event | category | flops | bytes accessed | tf_op | source)
XLA Modules:
  0.0 84.2 jit_solution(1986767686034494554)
XLA Ops:
  0.6 1.9 %shard_map.130 = (f32[272,128]{1,0:T(8,128)S(1)}, f32[272,128]{1,0:T(8,128)S(1)}, f32[96,128]{1,0:T(8,128)S(1)}, f32[96,128]{1,0:T(8,128)S(1)}, f32[48,32,128]{2,1,0:T(8,128)S(1)}, /*index=5*/f32[768,128]{1,0:T(8,128)S(1)}) custom-call(f32[6,16,32,256]{3,2,1,0:T(8,128)} %s.1, f32[32,128]{1,0:T(8,128)} %depth.1, f32[32,128]{1,0:T(8,128)} %height_in.1, ...), custom_call_target="tpu_custom_call" | custom-call | tf_op jit(solution)/shard_map/pallas_call | solution.py:40
  2.5 0.1 collective-permute-start.4
  2.6 1.6 %collective-permute-start.2 = (f32[96,128]{1,0:T(8,128)S(1)}, f32[96,128]{1,0:T(8,128)S(1)}, u32[]{:S(2)}, u32[]{:S(2)}) collective-permute-start(f32[96,128]{1,0:T(8,128)S(1)} %get-tuple-element.66), channel_id=1, source_target_pairs={{0,2},{2,4},{4,6},{6,8},{8,10},{10,12},{12,14},{14,0},{1,3},{3,5},... | collective-permute-start | bytes 147464 | tf_op jit(solution)/shard_map/ppermute | solution.py:533
  4.3 4.1 %collective-permute-start.3 = (f32[96,128]{1,0:T(8,128)S(1)}, f32[96,128]{1,0:T(8,128)S(1)}, u32[]{:S(2)}, u32[]{:S(2)}) collective-permute-start(f32[96,128]{1,0:T(8,128)S(1)} %get-tuple-element.67), channel_id=1, source_target_pairs={{0,14},{2,0},{4,2},{6,4},{8,6},{10,8},{12,10},{14,12},{1,15},{3,1}... | collective-permute-start | bytes 147464 | tf_op jit(solution)/shard_map/ppermute | solution.py:533
  8.3 2.0 %collective-permute-start = (f32[272,128]{1,0:T(8,128)S(1)}, f32[272,128]{1,0:T(8,128)S(1)}, u32[]{:S(2)}, u32[]{:S(2)}) collective-permute-start(f32[272,128]{1,0:T(8,128)S(1)} %get-tuple-element.64), channel_id=1, source_target_pairs={{0,16},{16,32},{32,48},{48,64},{64,80},{80,96},{96,112},{112,0},{1... | collective-permute-start | bytes 417800 | tf_op jit(solution)/shard_map/ppermute | solution.py:533
  10.3 3.1 %collective-permute-start.1 = (f32[272,128]{1,0:T(8,128)S(1)}, f32[272,128]{1,0:T(8,128)S(1)}, u32[]{:S(2)}, u32[]{:S(2)}) collective-permute-start(f32[272,128]{1,0:T(8,128)S(1)} %get-tuple-element.65), channel_id=1, source_target_pairs={{0,112},{16,0},{32,16},{48,32},{64,48},{80,64},{96,80},{112,96},{1... | collective-permute-start | bytes 417800 | tf_op jit(solution)/shard_map/ppermute | solution.py:533
  13.5 2.6 %shard_map.129 = (f32[3,16,32,256]{3,2,1,0:T(8,128)S(1)}, f32[6,16,32,256]{3,2,1,0:T(8,128)S(1)}, s32[16,32,256]{2,1,0:T(8,128)S(1)}, f32[1,16,32,256]{3,2,1,0:T(8,128)S(1)}) custom-call(f32[3,16,32,256]{3,2,1,0:T(8,128)} %v_hbm.1, f32[6,16,32,256]{3,2,1,0:T(8,128)} %s.1, s32[16,32,256]{2,1,0:T(8,128)} %mat_hbm.1, f32[24,128]{1,0:T(8,128)S(1)} %broadcast_bitcast_fusion.tab), custom_call_target="tpu_custom_call" | custom-call | tf_op jit(solution)/shard_map/pallas_call | solution.py:40
  16.1 0.0 collective-permute-done.3.yup
  16.1 1.2 %collective-permute-done.xdn = f32[272,128]{1,0:T(8,128)S(1)} collective-permute-done((f32[272,128]{1,0:T(8,128)S(1)}, f32[272,128]{1,0:T(8,128)S(1)}, u32[]{:S(2)}, u32[]{:S(2)}) %collective-permute-start) | collective-permute-done | bytes 139296 | tf_op jit(solution)/shard_map/ppermute | solution.py:533
  17.3 1.9 %shard_map.131 = (f32[3,16,32,256]{3,2,1,0:T(8,128)S(1)}, f32[272,128]{1,0:T(8,128)S(1)}, f32[272,128]{1,0:T(8,128)S(1)}, f32[96,128]{1,0:T(8,128)S(1)}, f32[96,...) custom-call(f32[3,16,32,256]{3,2,1,0:T(8,128)S(1)} %get-tuple-elemen, ...), custom_call_target="tpu_custom_call", output_to_operand_aliasing={{0}: (0, {}), {7}: (8, {})} | custom-call | tf_op jit(solution)/shard_map/pallas_call | solution.py:40
  19.2 0.1 collective-permute-start.9
  19.2 0.2 collective-permute-start.5
  19.5 4.0 %collective-permute-start.6 = (f32[272,128]{1,0:T(8,128)S(1)}, f32[272,128]{1,0:T(8,128)S(1)}, u32[]{:S(2)}, u32[]{:S(2)}) collective-permute-start(f32[272,128]{1,0:T(8,128)S(1)} %get-tuple-element.74), channel_id=1, source_target_pairs={{0,112},{16,0},{32,16},{48,32},{64,48},{80,64},{96,80},{112,96},{1... | collective-permute-start | bytes 417800 | tf_op jit(solution)/shard_map/ppermute | solution.py:533
  23.5 5.6 %collective-permute-start.8 = (f32[96,128]{1,0:T(8,128)S(1)}, f32[96,128]{1,0:T(8,128)S(1)}, u32[]{:S(2)}, u32[]{:S(2)}) collective-permute-start(f32[96,128]{1,0:T(8,128)S(1)} %get-tuple-element.76), channel_id=1, source_target_pairs={{0,14},{2,0},{4,2},{6,4},{8,6},{10,8},{12,10},{14,12},{1,15},{3,1}... | collective-permute-start | bytes 147464 | tf_op jit(solution)/shard_map/ppermute | solution.py:533
  29.1 1.6 %shard_map.132.coef = f32[2,16,32,256]{3,2,1,0:T(8,128)S(1)} custom-call(f32[24,128]{1,0:T(8,128)S(1)} %broadcast_bitcast_fusion.tab, s32[16,32,256]{2,1,0:T(8,128)S(1)} %get-tuple-element.72.mat), custom_call_target="tpu_custom_call" | custom-call | tf_op jit(solution)/shard_map/pallas_call | solution.py:40
  30.7 0.4 collective-permute-done.7.ydn
  31.2 2.1 %shard_map.133 = (f32[6,16,32,256]{3,2,1,0:T(8,128)S(1)}, f32[272,128]{1,0:T(8,128)S(1)}, f32[272,128]{1,0:T(8,128)S(1)}, f32[96,128]{1,0:T(8,128)S(1)}, f32[96,...) custom-call(f32[6,16,32,256]{3,2,1,0:T(8,128)S(1)} %get-tuple-elemen, ...), custom_call_target="tpu_custom_call", output_to_operand_aliasing={{0}: (0, {}), {6}: (8, {})} | custom-call | tf_op jit(solution)/shard_map/pallas_call | solution.py:40
  33.3 0.1 collective-permute-start.14
  33.4 0.1 collective-permute-start.10
  33.5 4.1 %collective-permute-start.11 = (f32[272,128]{1,0:T(8,128)S(1)}, f32[272,128]{1,0:T(8,128)S(1)}, u32[]{:S(2)}, u32[]{:S(2)}) collective-permute-start(f32[272,128]{1,0:T(8,128)S(1)} %get-tuple-element.82), channel_id=1, source_target_pairs={{0,112},{16,0},{32,16},{48,32},{64,48},{80,64},{96,80},{112,96},{1... | collective-permute-start | bytes 417800 | tf_op jit(solution)/shard_map/ppermute | solution.py:533
  37.6 5.6 %collective-permute-start.13 = (f32[96,128]{1,0:T(8,128)S(1)}, f32[96,128]{1,0:T(8,128)S(1)}, u32[]{:S(2)}, u32[]{:S(2)}) collective-permute-start(f32[96,128]{1,0:T(8,128)S(1)} %get-tuple-element.84), channel_id=1, source_target_pairs={{0,14},{2,0},{4,2},{6,4},{8,6},{10,8},{12,10},{14,12},{1,15},{3,1}... | collective-permute-start | bytes 147464 | tf_op jit(solution)/shard_map/ppermute | solution.py:533
  43.2 2.1 %shard_map.134 = (f32[8,512]{1,0:T(8,128)S(1)}, f32[512,128]{1,0:T(8,128)S(1)}, f32[8,128]{1,0:T(8,128)S(1)}) custom-call(s32[64,1,512]{2,1,0:T(1,128)} %bitcast.10, s32[64,512]{1,0:T(8,128)} %cell_rows), custom_call_target="tpu_custom_call" | custom-call | tf_op jit(solution)/shard_map/pallas_call | solution.py:40
  45.4 1.9 %shard_map.135 = (f32[3,16,32,256]{3,2,1,0:T(8,128)S(1)}, f32[272,128]{1,0:T(8,128)S(1)}, f32[272,128]{1,0:T(8,128)S(1)}, f32[96,128]{1,0:T(8,128)S(1)}, f32[96,...) custom-call(f32[3,16,32,256]{3,2,1,0:T(8,128)S(1)} %get-tuple-elemen, ...), custom_call_target="tpu_custom_call", output_to_operand_aliasing={{0}: (0, {}), {7}: (8, {})} | custom-call | tf_op jit(solution)/shard_map/pallas_call | solution.py:40
  47.3 0.1 collective-permute-start.19
  47.4 0.1 collective-permute-start.15
  47.5 4.1 %collective-permute-start.16 = (f32[272,128]{1,0:T(8,128)S(1)}, f32[272,128]{1,0:T(8,128)S(1)}, u32[]{:S(2)}, u32[]{:S(2)}) collective-permute-start(f32[272,128]{1,0:T(8,128)S(1)} %get-tuple-element.100), channel_id=1, source_target_pairs={{0,112},{16,0},{32,16},{48,32},{64,48},{80,64},{96,80},{112,96},{1... | collective-permute-start | bytes 417800 | tf_op jit(solution)/shard_map/ppermute | solution.py:533
  51.6 1.1 %collective-permute-start.17 = (f32[96,128]{1,0:T(8,128)S(1)}, f32[96,128]{1,0:T(8,128)S(1)}, u32[]{:S(2)}, u32[]{:S(2)}) collective-permute-start(f32[96,128]{1,0:T(8,128)S(1)} %get-tuple-element.101), channel_id=1, source_target_pairs={{0,2},{2,4},{4,6},{6,8},{8,10},{10,12},{12,14},{14,0},{1,3},{3,5},... | collective-permute-start | bytes 147464 | tf_op jit(solution)/shard_map/ppermute | solution.py:533
  52.7 4.5 %collective-permute-start.18 = (f32[96,128]{1,0:T(8,128)S(1)}, f32[96,128]{1,0:T(8,128)S(1)}, u32[]{:S(2)}, u32[]{:S(2)}) collective-permute-start(f32[96,128]{1,0:T(8,128)S(1)} %get-tuple-element.102), channel_id=1, source_target_pairs={{0,14},{2,0},{4,2},{6,4},{8,6},{10,8},{12,10},{14,12},{1,15},{3,1}... | collective-permute-start | bytes 147464 | tf_op jit(solution)/shard_map/ppermute | solution.py:533
  57.2 2.1 %collective-permute-done.17.ydn = f32[96,128]{1,0:T(8,128)S(1)} collective-permute-done((f32[96,128]{1,0:T(8,128)S(1)}, f32[96,128]{1,0:T(8,128)S(1)}, u32[]{:S(2)}, u32[]{:S(2)}) %collective-permute-start.17) | collective-permute-done | bytes 49184 | tf_op jit(solution)/shard_map/ppermute | solution.py:533
  59.3 3.1 %shard_map.136 = (f32[3,16,32,256]{3,2,1,0:T(8,128)}, f32[6,16,32,256]{3,2,1,0:T(8,128)}, f32[64,128]{1,0:T(8,128)}, f32[768,128]{1,0:T(8,128)}, f32[80,128]{1,0:T(8,128)}) custom-call(f32[6,16,32,256]{3,2,1,0:T(8,128)S(1)} %get-tuple-element.80.s, f32[3,16,32,256]{3,2,1,0:T(8,128)S(1)} %get-tuple-element.98.v, f32[2,16,32,256]{3,2,1,0:T(8,128)S(1)} %shard_map.132.coef, ...), custom_call_target="tpu_custom_call" | custom-call | tf_op jit(solution)/shard_map/pallas_call | solution.py:40
  62.5 18.2 %all_to_all.11 = f32[64,1,128]{2,1,0:T(1,128)} all-to-all(f32[64,1,128]{2,1,0:T(1,128)} %bitcast.11), channel_id=1, replica_groups=mesh['gx'=8,'gy'=8,'gz'=2] {'gx','gy'}, dimensions={0} | all-to-all | bytes 65536 | tf_op jit(solution)/shard_map/all_to_all | solution.py:623
  80.6 3.5 %shard_map.137 = (f32[32,128]{1,0:T(8,128)}, f32[32,128]{1,0:T(8,128)}) custom-call(f32[64,128]{1,0:T(8,128)} %bitcast.9, f32[80,128]{1,0:T(8,128)} %get-tuple-element.112.far_in, f32[768,128]{1,0:T(8,128)} %get-tuple-element.113.bag_in, f32[32,128]{1,0:T(8,128)} %height_in.1, f32[32,128]{1,0:T(8,128)} %current_in.1, s32[32,128]{1,0:T(8,128)} %wet_in.1), custom_call_target="tpu_custom_call" | custom-call | tf_op jit(solution)/shard_map/pallas_call | solution.py:40
  (25 shorter events, 0.1 us)
Async XLA Ops:
  0.6 12.8 %copy-start = (f32[16,3]{0,1:T(4,128)S(1)}, f32[16,3]{0,1:T(4,128)}, u32[]{:S(2)}) copy-start(f32[16,3]{0,1:T(4,128)} %param.13) | copy-start | bytes 580
  2.5 14.8 %collective-permute-start.4 = (f32[48,32,128]{2,1,0:T(8,128)S(1)}, f32[48,32,128]{2,1,0:T(8,128)S(1)}, u32[]{:S(2)}, u32[]{:S(2)}) collective-permute-start(f32[48,32,128]{2,1,0:T(8,128)S(1)} %get-tuple-element.68), channel_id=1, source_target_pairs={{0,1},{1,0},{2,3},{3,2},{4,5},{5,4},{6,7},{7,6},{8,9},{9,8},{10,11... | collective-permute-start | bytes 2359304 | tf_op jit(solution)/shard_map/ppermute | solution.py:533
  2.6 13.5 %collective-permute-start.2 = (f32[96,128]{1,0:T(8,128)S(1)}, f32[96,128]{1,0:T(8,128)S(1)}, u32[]{:S(2)}, u32[]{:S(2)}) collective-permute-start(f32[96,128]{1,0:T(8,128)S(1)} %get-tuple-element.66), channel_id=1, source_target_pairs={{0,2},{2,4},{4,6},{6,8},{8,10},{10,12},{12,14},{14,0},{1,3},{3,5},... | collective-permute-start | bytes 147464 | tf_op jit(solution)/shard_map/ppermute | solution.py:533
  4.3 11.8 %collective-permute-start.3 = (f32[96,128]{1,0:T(8,128)S(1)}, f32[96,128]{1,0:T(8,128)S(1)}, u32[]{:S(2)}, u32[]{:S(2)}) collective-permute-start(f32[96,128]{1,0:T(8,128)S(1)} %get-tuple-element.67), channel_id=1, source_target_pairs={{0,14},{2,0},{4,2},{6,4},{8,6},{10,8},{12,10},{14,12},{1,15},{3,1}... | collective-permute-start | bytes 147464 | tf_op jit(solution)/shard_map/ppermute | solution.py:533
  8.3 8.9 %collective-permute-start = (f32[272,128]{1,0:T(8,128)S(1)}, f32[272,128]{1,0:T(8,128)S(1)}, u32[]{:S(2)}, u32[]{:S(2)}) collective-permute-start(f32[272,128]{1,0:T(8,128)S(1)} %get-tuple-element.64), channel_id=1, source_target_pairs={{0,16},{16,32},{32,48},{48,64},{64,80},{80,96},{96,112},{112,0},{1... | collective-permute-start | bytes 417800 | tf_op jit(solution)/shard_map/ppermute | solution.py:533
  10.3 6.9 %collective-permute-start.1 = (f32[272,128]{1,0:T(8,128)S(1)}, f32[272,128]{1,0:T(8,128)S(1)}, u32[]{:S(2)}, u32[]{:S(2)}) collective-permute-start(f32[272,128]{1,0:T(8,128)S(1)} %get-tuple-element.65), channel_id=1, source_target_pairs={{0,112},{16,0},{32,16},{48,32},{64,48},{80,64},{96,80},{112,96},{1... | collective-permute-start | bytes 417800 | tf_op jit(solution)/shard_map/ppermute | solution.py:533
  19.2 12.0 %collective-permute-start.9 = (f32[48,32,128]{2,1,0:T(8,128)S(1)}, f32[48,32,128]{2,1,0:T(8,128)S(1)}, u32[]{:S(2)}, u32[]{:S(2)}) collective-permute-start(f32[48,32,128]{2,1,0:T(8,128)S(1)} %get-tuple-element.77), channel_id=1, source_target_pairs={{0,1},{1,0},{2,3},{3,2},{4,5},{5,4},{6,7},{7,6},{8,9},{9,8},{10,11... | collective-permute-start | bytes 2359304 | tf_op jit(solution)/shard_map/ppermute | solution.py:533
  19.2 11.9 %collective-permute-start.5 = (f32[272,128]{1,0:T(8,128)S(1)}, f32[272,128]{1,0:T(8,128)S(1)}, u32[]{:S(2)}, u32[]{:S(2)}) collective-permute-start(f32[272,128]{1,0:T(8,128)S(1)} %get-tuple-element.73), channel_id=1, source_target_pairs={{0,16},{16,32},{32,48},{48,64},{64,80},{80,96},{96,112},{112,0},{1... | collective-permute-start | bytes 417800 | tf_op jit(solution)/shard_map/ppermute | solution.py:533
  19.5 11.7 %collective-permute-start.6 = (f32[272,128]{1,0:T(8,128)S(1)}, f32[272,128]{1,0:T(8,128)S(1)}, u32[]{:S(2)}, u32[]{:S(2)}) collective-permute-start(f32[272,128]{1,0:T(8,128)S(1)} %get-tuple-element.74), channel_id=1, source_target_pairs={{0,112},{16,0},{32,16},{48,32},{64,48},{80,64},{96,80},{112,96},{1... | collective-permute-start | bytes 417800 | tf_op jit(solution)/shard_map/ppermute | solution.py:533
  23.4 7.7 %collective-permute-start.7 = (f32[96,128]{1,0:T(8,128)S(1)}, f32[96,128]{1,0:T(8,128)S(1)}, u32[]{:S(2)}, u32[]{:S(2)}) collective-permute-start(f32[96,128]{1,0:T(8,128)S(1)} %get-tuple-element.75), channel_id=1, source_target_pairs={{0,2},{2,4},{4,6},{6,8},{8,10},{10,12},{12,14},{14,0},{1,3},{3,5},... | collective-permute-start | bytes 147464 | tf_op jit(solution)/shard_map/ppermute | solution.py:533
  23.5 7.7 %collective-permute-start.8 = (f32[96,128]{1,0:T(8,128)S(1)}, f32[96,128]{1,0:T(8,128)S(1)}, u32[]{:S(2)}, u32[]{:S(2)}) collective-permute-start(f32[96,128]{1,0:T(8,128)S(1)} %get-tuple-element.76), channel_id=1, source_target_pairs={{0,14},{2,0},{4,2},{6,4},{8,6},{10,8},{12,10},{14,12},{1,15},{3,1}... | collective-permute-start | bytes 147464 | tf_op jit(solution)/shard_map/ppermute | solution.py:533
  33.3 12.1 %collective-permute-start.14 = (f32[48,32,128]{2,1,0:T(8,128)S(1)}, f32[48,32,128]{2,1,0:T(8,128)S(1)}, u32[]{:S(2)}, u32[]{:S(2)}) collective-permute-start(f32[48,32,128]{2,1,0:T(8,128)S(1)} %get-tuple-element.85), channel_id=1, source_target_pairs={{0,1},{1,0},{2,3},{3,2},{4,5},{5,4},{6,7},{7,6},{8,9},{9,8},{10,11... | collective-permute-start | bytes 2359304 | tf_op jit(solution)/shard_map/ppermute | solution.py:533
  33.4 12.0 %collective-permute-start.10 = (f32[272,128]{1,0:T(8,128)S(1)}, f32[272,128]{1,0:T(8,128)S(1)}, u32[]{:S(2)}, u32[]{:S(2)}) collective-permute-start(f32[272,128]{1,0:T(8,128)S(1)} %get-tuple-element.81), channel_id=1, source_target_pairs={{0,16},{16,32},{32,48},{48,64},{64,80},{80,96},{96,112},{112,0},{1... | collective-permute-start | bytes 417800 | tf_op jit(solution)/shard_map/ppermute | solution.py:533
  33.5 11.9 %collective-permute-start.11 = (f32[272,128]{1,0:T(8,128)S(1)}, f32[272,128]{1,0:T(8,128)S(1)}, u32[]{:S(2)}, u32[]{:S(2)}) collective-permute-start(f32[272,128]{1,0:T(8,128)S(1)} %get-tuple-element.82), channel_id=1, source_target_pairs={{0,112},{16,0},{32,16},{48,32},{64,48},{80,64},{96,80},{112,96},{1... | collective-permute-start | bytes 417800 | tf_op jit(solution)/shard_map/ppermute | solution.py:533
  37.6 7.8 %collective-permute-start.12 = (f32[96,128]{1,0:T(8,128)S(1)}, f32[96,128]{1,0:T(8,128)S(1)}, u32[]{:S(2)}, u32[]{:S(2)}) collective-permute-start(f32[96,128]{1,0:T(8,128)S(1)} %get-tuple-element.83), channel_id=1, source_target_pairs={{0,2},{2,4},{4,6},{6,8},{8,10},{10,12},{12,14},{14,0},{1,3},{3,5},... | collective-permute-start | bytes 147464 | tf_op jit(solution)/shard_map/ppermute | solution.py:533
  37.6 7.8 %collective-permute-start.13 = (f32[96,128]{1,0:T(8,128)S(1)}, f32[96,128]{1,0:T(8,128)S(1)}, u32[]{:S(2)}, u32[]{:S(2)}) collective-permute-start(f32[96,128]{1,0:T(8,128)S(1)} %get-tuple-element.84), channel_id=1, source_target_pairs={{0,14},{2,0},{4,2},{6,4},{8,6},{10,8},{12,10},{14,12},{1,15},{3,1}... | collective-permute-start | bytes 147464 | tf_op jit(solution)/shard_map/ppermute | solution.py:533
  47.3 12.0 %collective-permute-start.19 = (f32[49,32,128]{2,1,0:T(8,128)S(1)}, f32[49,32,128]{2,1,0:T(8,128)S(1)}, u32[]{:S(2)}, u32[]{:S(2)}) collective-permute-start(f32[49,32,128]{2,1,0:T(8,128)S(1)} %get-tuple-element.103), channel_id=1, source_target_pairs={{0,1},{1,0},{2,3},{3,2},{4,5},{5,4},{6,7},{7,6},{8,9},{9,8},{10,11... | collective-permute-start | bytes 2408456 | tf_op jit(solution)/shard_map/ppermute | solution.py:533
  47.4 11.9 %collective-permute-start.15 = (f32[272,128]{1,0:T(8,128)S(1)}, f32[272,128]{1,0:T(8,128)S(1)}, u32[]{:S(2)}, u32[]{:S(2)}) collective-permute-start(f32[272,128]{1,0:T(8,128)S(1)} %get-tuple-element.99), channel_id=1, source_target_pairs={{0,16},{16,32},{32,48},{48,64},{64,80},{80,96},{96,112},{112,0},{1... | collective-permute-start | bytes 417800 | tf_op jit(solution)/shard_map/ppermute | solution.py:533
  47.5 11.8 %collective-permute-start.16 = (f32[272,128]{1,0:T(8,128)S(1)}, f32[272,128]{1,0:T(8,128)S(1)}, u32[]{:S(2)}, u32[]{:S(2)}) collective-permute-start(f32[272,128]{1,0:T(8,128)S(1)} %get-tuple-element.100), channel_id=1, source_target_pairs={{0,112},{16,0},{32,16},{48,32},{64,48},{80,64},{96,80},{112,96},{1... | collective-permute-start | bytes 417800 | tf_op jit(solution)/shard_map/ppermute | solution.py:533
  51.6 7.7 %collective-permute-start.17 = (f32[96,128]{1,0:T(8,128)S(1)}, f32[96,128]{1,0:T(8,128)S(1)}, u32[]{:S(2)}, u32[]{:S(2)}) collective-permute-start(f32[96,128]{1,0:T(8,128)S(1)} %get-tuple-element.101), channel_id=1, source_target_pairs={{0,2},{2,4},{4,6},{6,8},{8,10},{10,12},{12,14},{14,0},{1,3},{3,5},... | collective-permute-start | bytes 147464 | tf_op jit(solution)/shard_map/ppermute | solution.py:533
  52.7 6.6 %collective-permute-start.18 = (f32[96,128]{1,0:T(8,128)S(1)}, f32[96,128]{1,0:T(8,128)S(1)}, u32[]{:S(2)}, u32[]{:S(2)}) collective-permute-start(f32[96,128]{1,0:T(8,128)S(1)} %get-tuple-element.102), channel_id=1, source_target_pairs={{0,14},{2,0},{4,2},{6,4},{8,6},{10,8},{12,10},{14,12},{1,15},{3,1}... | collective-permute-start | bytes 147464 | tf_op jit(solution)/shard_map/ppermute | solution.py:533

commit v2 on v1

--- a/solution.py
+++ b/solution.py
@@ -68,20 +68,27 @@
 PAYLOAD = [shape(XR, 128), shape(XR, 128), shape(YR, 128), shape(YR, 128)]
 
 
-def put_x_faces(ref, comps, pxu, pxd):
+def odd(axis):
+    return lax.rem(lax.axis_index(axis), 2) == 1
+
+
+def put_x_faces(ref, comps, pxe, pxo):
+    flip = odd("gx")
     for i, c in enumerate(comps):
         for h in range(2):
             rows = slice(i * 64 + h * 32, i * 64 + h * 32 + 32)
             lanes = slice(h * 128, h * 128 + 128)
-            pxu[rows, :] = ref[c, CX - 1, :, lanes]
-            pxd[rows, :] = ref[c, 0, :, lanes]
-
-
-def put_y(x, i, tiles, pyu, pyd):
+            above, below = ref[c, CX - 1, :, lanes], ref[c, 0, :, lanes]
+            pxe[rows, :] = jnp.where(flip, below, above)
+            pxo[rows, :] = jnp.where(flip, above, below)
+
+
+def put_y(flip, x, i, tiles, pye, pyo):
     for h in range(2):
         row = i * 32 + h * 16 + x
-        pyu[row : row + 1, :] = tiles[3][h][7:8, :]
-        pyd[row : row + 1, :] = tiles[0][h][0:1, :]
+        above, below = tiles[3][h][7:8, :], tiles[0][h][0:1, :]
+        pye[row : row + 1, :] = jnp.where(flip, below, above)
+        pyo[row : row + 1, :] = jnp.where(flip, above, below)
 
 
 def put_z(gz, x, i, tiles, pz):
@@ -89,7 +96,7 @@
         pz[i * CX + x, t * 8 : t * 8 + 8, :] = jnp.where(gz == 0, tiles[t][1], tiles[t][0])
 
 
-def prepare(s, depth, height, wet, pxu, pxd, pyu, pyd, pz, bag, rows, high, deep, damp, edge, sems):
+def prepare(s, depth, height, wet, pxe, pxo, pye, pyo, pz, bag, rows, high, deep, damp, edge, sems):
     gx, _, gz = place()
     copies = []
 
@@ -101,11 +108,13 @@
     start(depth, deep)
     start(height, high)
     start(wet, damp)
+    first_face = jnp.where(odd("gx"), 0, CX - 1)
+    flip = odd("gy")
     for i, c in enumerate(SX):
         for h in range(2):
             lanes = pl.ds(h * 128, 128)
-            start(s.at[c, CX - 1, :, lanes], pxu.at[pl.ds(i * 64 + h * 32, 32), :])
-            start(s.at[c, 0, :, lanes], pxd.at[pl.ds(i * 64 + h * 32, 32), :])
+            start(s.at[c, first_face, :, lanes], pxe.at[pl.ds(i * 64 + h * 32, 32), :])
+            start(s.at[c, CX - 1 - first_face, :, lanes], pxo.at[pl.ds(i * 64 + h * 32, 32), :])
     for i, c in enumerate(SY):
         start(s.at[c, :, pl.ds(24, 8), :], edge.at[0, i])
         start(s.at[c, :, pl.ds(0, 8), :], edge.at[1, i])
@@ -114,9 +123,9 @@
         start(s.at[c, :, :, lanes], pz.at[pl.ds(i * CX, CX)])
     for copy in copies[:3]:
         copy.wait()
-    factor(deep, high, damp, pxu, bag, rows)
-    pxd[XF:, :] = pxu[XF:, :]
-    bag[pl.ds(pl.multiple_of(gx * OCR, 8), OCR), :] = pxu[XF:, :]
+    factor(deep, high, damp, pxe, bag, rows)
+    pxo[XF:, :] = pxe[XF:, :]
+    bag[pl.ds(pl.multiple_of(gx * OCR, 8), OCR), :] = pxe[XF:, :]
     for copy in copies[3:]:
         copy.wait()
     for i in range(3):
@@ -124,11 +133,12 @@
             for h in range(2):
                 row = i * 32 + h * 16 + x
                 lanes = slice(h * 128, h * 128 + 128)
-                pyu[row : row + 1, :] = edge[0, i, x, 7:8, lanes]
-                pyd[row : row + 1, :] = edge[1, i, x, 0:1, lanes]
-
-
-def factor(depth, height, wet, pxu, bag, rows):
+                above, below = edge[0, i, x, 7:8, lanes], edge[1, i, x, 0:1, lanes]
+                pye[row : row + 1, :] = jnp.where(flip, below, above)
+                pyo[row : row + 1, :] = jnp.where(flip, above, below)
+
+
+def factor(depth, height, wet, pxe, bag, rows):
     spread = depth[...] * depth[...] / 3.0
     rows[0:32, :] = spread
     w = [None] * LON
@@ -169,20 +179,20 @@
     high = height[...]
     a1 = 400.0 * rows[0:32, :] * wet_float
     a2 = 400.0 * rows[32:64, :] * wet_float
-    pxu[XF : XF + 32, :] = a1
-    pxu[XF + 32 : XF + 64, :] = a2
+    pxe[XF : XF + 32, :] = a1
+    pxe[XF + 32 : XF + 64, :] = a2
     base = XF + 64
-    pxu[base : base + 1, :] = jnp.sum(a1 * high, axis=0, keepdims=True)
-    pxu[base + 1 : base + 2, :] = jnp.sum(a2 * high, axis=0, keepdims=True)
-    pxu[base + 2 : base + 3, :] = first_left
-    pxu[base + 3 : base + 4, :] = left_run
-    pxu[base + 4 : base + 5, :] = first_right
-    pxu[base + 5 : base + 6, :] = right_run
-    pxu[base + 6 : base + 7, :] = -400.0 * p_before
-    pxu[base + 7 : base + 8, :] = -400.0 * q_before
-    pxu[base + 8 : base + 9, :] = wet_float[0:1, :]
-    pxu[base + 9 : base + 10, :] = wet_float[0:1, :] * high[0:1, :]
-    pxu[base + 10 : base + 16, :] = jnp.zeros((6, LAT), F32)
+    pxe[base : base + 1, :] = jnp.sum(a1 * high, axis=0, keepdims=True)
+    pxe[base + 1 : base + 2, :] = jnp.sum(a2 * high, axis=0, keepdims=True)
+    pxe[base + 2 : base + 3, :] = first_left
+    pxe[base + 3 : base + 4, :] = left_run
+    pxe[base + 4 : base + 5, :] = first_right
+    pxe[base + 5 : base + 6, :] = right_run
+    pxe[base + 6 : base + 7, :] = -400.0 * p_before
+    pxe[base + 7 : base + 8, :] = -400.0 * q_before
+    pxe[base + 8 : base + 9, :] = wet_float[0:1, :]
+    pxe[base + 9 : base + 10, :] = wet_float[0:1, :] * high[0:1, :]
+    pxe[base + 10 : base + 16, :] = jnp.zeros((6, LAT), F32)
 
 
 def slopes_z(src, comps, out):
@@ -201,7 +211,7 @@
         out[i] = total.reshape(CX, CY, CZ)
 
 
-def differences(src, comps, dzs, xdn, xup, ydn, yup, zs):
+def differences(src, comps, dzs, xe, xo, ye, yo, zs):
     gx, gy, gz = place()
     sub, lane = iotas()
     cx, cy, cz = comps
@@ -215,14 +225,20 @@
     far, near = (lane == 127) & (gz == 0), (lane == 0) & (gz == 1)
     shift = jnp.where(gz == 0, 127, 1)
 
-    def halo_x(ref, mask, i, t, h):
+    flip_x, flip_y = odd("gx"), odd("gy")
+
+    def halo_x(one, two, mask, i, t, h):
         row = i * 64 + h * 32 + t * 8
-        return ref[row : row + 8, :] * mask
+        return jnp.where(flip_x, one[row : row + 8, :], two[row : row + 8, :]) * mask
+
+    def halo_y(one, two, mask, row):
+        line = jnp.where(flip_y, one[row : row + 1, :], two[row : row + 1, :]) * mask
+        return jnp.broadcast_to(line, (8, 128))
 
     def dx(x, i, t, h):
         c = cx[i]
-        low = halo_x(xdn, m_xd, i, t, h) if x == 0 else tile(src, c, x - 1, t, h)
-        high = halo_x(xup, m_xu, i, t, h) if x == CX - 1 else tile(src, c, x + 1, t, h)
+        low = halo_x(xe, xo, m_xd, i, t, h) if x == 0 else tile(src, c, x - 1, t, h)
+        high = halo_x(xo, xe, m_xu, i, t, h) if x == CX - 1 else tile(src, c, x + 1, t, h)
         return high - low
 
     def dy(x, i, tiles):
@@ -231,8 +247,8 @@
             up = [pltpu.roll(tiles[t][h], 7, 0) for t in range(4)]
             dn = [pltpu.roll(tiles[t][h], 1, 0) for t in range(4)]
             row = i * 32 + h * 16 + x
-            up.append(jnp.broadcast_to(yup[row : row + 1, :] * m_yu, (8, 128)))
-            dn.insert(0, jnp.broadcast_to(ydn[row : row + 1, :] * m_yd, (8, 128)))
+            up.append(halo_y(yo, ye, m_yu, row))
+            dn.insert(0, halo_y(ye, yo, m_yd, row))
             for t in range(4):
                 out[t][h] = jnp.where(top, up[t + 1], up[t]) - jnp.where(bottom, dn[t], dn[t + 1])
         return out
@@ -285,23 +301,34 @@
     lookup(tab, mat, coef, (1, 2))
 
 
-def collect(distance, xdn, xup, bag):
+def collect(distance, xe, xo, bag):
     gx = lax.axis_index("gx")
-    for ref, steps in ((xdn, NB - distance), (xup, distance)):
+    first = jnp.where(odd("gx"), NB - distance, distance)
+    for ref, steps in ((xe, first), (xo, NB - first)):
         row = pl.multiple_of(lax.rem(gx + steps, NB) * OCR, 8)
         bag[pl.ds(row, OCR), :] = ref[XF:, :]
 
 
-def move(distance, has_lift, v, s, coef, xdn, xup, ydn, yup, zs, bag_in, *refs):
+def move(distance, has_lift, v, s, coef, xe, xo, ye, yo, zs, bag_in, *refs):
     if has_lift:
-        lift_in, vo, pxu, pxd, pyu, pyd, pz, lift_out, bag, dzs = refs
+        lift_in, coef2, pxe, pxo, pye, pyo, pz, lift_out, v_hbm, s_hbm, coef_hbm, bag_hbm, vo, bag, dzs, sems = refs
+        copies = [
+            pltpu.make_async_copy(s, s_hbm, sems.at[CX]),
+            pltpu.make_async_copy(coef2, coef_hbm, sems.at[CX + 1]),
+            pltpu.make_async_copy(bag, bag_hbm, sems.at[CX + 2]),
+        ]
+        bag[...] = bag_in[...]
     else:
-        vo, pxu, pxd, pyu, pyd, pz, lift_out, bag, dzs = refs
+        vo, pxe, pxo, pye, pyo, pz, lift_out, bag, dzs = refs
     gz = lax.axis_index("gz")
+    flip = odd("gy")
     sub, lane = iotas()
-    collect(distance, xdn, xup, bag)
+    collect(distance, xe, xo, bag)
+    if has_lift:
+        for copy in copies:
+            copy.start()
     slopes_z(s, SZ, dzs)
-    dx, dy, dz = differences(s, (SX, SY, SZ), dzs, xdn, xup, ydn, yup, zs)
+    dx, dy, dz = differences(s, (SX, SY, SZ), dzs, xe, xo, ye, yo, zs)
     lift = [lift_in[t * 8 : t * 8 + 8, :] if has_lift else jnp.zeros((8, 128), F32) for t in range(4)]
     for x in range(CX):
         for i in range(3):
@@ -313,37 +340,71 @@
                     force = dx(x, i, t, h) + ey[t][h] + ez[t][h]
                     new[t][h] = tile(v, i, x, t, h) + tile(coef, 0, x, t, h) * force
                     vo[i, x, t * 8 : t * 8 + 8, h * 128 : h * 128 + 128] = new[t][h]
-            put_y(x, i, new, pyu, pyd)
+            put_y(flip, x, i, new, pye, pyo)
             put_z(gz, x, i, new, pz)
+        if has_lift:
+            copies.append(pltpu.make_async_copy(vo.at[:, x], v_hbm.at[:, x], sems.at[x]))
+            copies[-1].start()
         for t in range(4):
             lift[t] = jnp.where(lane == x, lift[t] - 0.25 * pltpu.roll(new[t][0], x, 1), lift[t])
     for t in range(4):
         lift_out[t * 8 : t * 8 + 8, :] = lift[t]
         if has_lift:
             pz[3 * CX, t * 8 : t * 8 + 8, :] = lift[t]
-    put_x_faces(vo, VA, pxu, pxd)
-    pxu[XF:, :] = xdn[XF:, :]
-    pxd[XF:, :] = xup[XF:, :]
-
-
-def strain(distance, last, s, v, coef, xdn, xup, ydn, yup, zs, *refs):
-    if last:
-        bag, lift, group, slot, code, v_hbm, s_hbm, out_hbm, bag_hbm, far_hbm, so, dzs, out, wide, sems = refs
-        copies = [
-            pltpu.make_async_copy(v, v_hbm, sems.at[CX]),
-            pltpu.make_async_copy(bag, bag_hbm, sems.at[CX + 1]),
-            pltpu.make_async_copy(xdn.at[pl.ds(XF, OCR), :], far_hbm, sems.at[CX + 2]),
-            pltpu.make_async_copy(out, out_hbm, sems.at[CX + 3]),
-        ]
-        pack_lift(jnp.where(lax.axis_index("gz") == 0, lift[...], zs[3 * CX]), group, slot, code, out, wide)
+    put_x_faces(vo, VA, pxe, pxo)
+    pxe[XF:, :] = xo[XF:, :]
+    pxo[XF:, :] = xe[XF:, :]
+    if has_lift:
         for copy in copies:
-            copy.start()
-    else:
-        bag_in, so, pxu, pxd, pyu, pyd, pz, bag, dzs = refs
-        collect(distance, xdn, xup, bag)
-    gz = lax.axis_index("gz")
+            copy.wait()
+
+
+def strain(distance, s, v, coef, xe, xo, ye, yo, zs, bag_in, so, pxe, pxo, pye, pyo, pz, bag, dzs):
+    collect(distance, xe, xo, bag)
     slopes_z(v, VA, dzs)
-    dx, dy, dz = differences(v, (VA, VA, VA), dzs, xdn, xup, ydn, yup, zs)
+    gz, flip = lax.axis_index("gz"), odd("gy")
+
+    def done(x, new):
+        for i in range(3):
+            put_y(flip, x, i, new[SY[i]], pye, pyo)
+            put_z(gz, x, i, new[SZ[i]], pz)
+
+    stretch(s, v, coef, dzs, xe, xo, ye, yo, zs, so, done)
+    put_x_faces(so, SX, pxe, pxo)
+    pxe[XF:, :] = xo[XF:, :]
+    pxo[XF:, :] = xe[XF:, :]
+
+
+def finish(s_in, v_in, coef_in, zs_in, xe, xo, ye, yo, s_hbm, far_hbm, s, v, coef, zs, dzs, sems):
+    early = [
+        pltpu.make_async_copy(v_in, v, sems.at[0]),
+        pltpu.make_async_copy(zs_in, zs, sems.at[1]),
+        pltpu.make_async_copy(coef_in, coef, sems.at[2]),
+        pltpu.make_async_copy(xe.at[pl.ds(XF, OCR), :], far_hbm, sems.at[3]),
+    ]
+    parts = [
+        pltpu.make_async_copy(s_in.at[:, pl.ds(i * 4, 4)], s.at[:, pl.ds(i * 4, 4)], sems.at[4 + i])
+        for i in range(4)
+    ]
+    for copy in early + parts:
+        copy.start()
+    early[0].wait()
+    slopes_z(v, VA, dzs)
+    for copy in early[1:] + parts:
+        copy.wait()
+    late = []
+
+    def done(x, new):
+        late.append(pltpu.make_async_copy(s.at[:, x], s_hbm.at[:, x], sems.at[8 + x]))
+        late[-1].start()
+
+    stretch(s, v, coef, dzs, xe, xo, ye, yo, zs, s, done)
+    for copy in late:
+        copy.wait()
+
+
+def stretch(s, v, coef, dzs, xe, xo, ye, yo, zs, so, done):
+    dx, dy, dz = differences(v, (VA, VA, VA), dzs, xe, xo, ye, yo, zs)
     for x in range(CX):
         ey = [dy(x, c, grab(v, c, x)) for c in range(3)]
         ez = [dz(x, c) for c in range(3)]
@@ -365,20 +426,7 @@
                 for c in range(6):
                     new[c][t][h] = tile(s, c, x, t, h) + change[c]
                     so[c, x, t * 8 : t * 8 + 8, h * 128 : h * 128 + 128] = new[c][t][h]
-        if last:
-            copies.append(pltpu.make_async_copy(so.at[:, x], s_hbm.at[:, x], sems.at[x]))
-            copies[-1].start()
-        else:
-            for i in range(3):
-                put_y(x, i, new[SY[i]], pyu, pyd)
-                put_z(gz, x, i, new[SZ[i]], pz)
-    if last:
-        for copy in copies:
-            copy.wait()
-    else:
-        put_x_faces(so, SX, pxu, pxd)
-        pxu[XF:, :] = xdn[XF:, :]
-        pxd[XF:, :] = xup[XF:, :]
+        done(x, new)
 
 
 def as_column(row, sub, lane):
@@ -422,7 +470,8 @@
     code[...] = pltpu.roll(found, 64, 1)
 
 
-def pack_lift(lift, group, slot, code, out, wide):
+def pack_lift(lift_here, zs, group, slot, code, out, wide):
+    lift = jnp.where(lax.axis_index("gz") == 0, lift_here[...], zs[3 * CX])
     for x in range(CX):
         rows = slice(x * 32, x * 32 + 32)
         wide[rows, :] = slot[rows, :] * jnp.broadcast_to(lift[:, x : x + 1], (32, 128))
@@ -431,13 +480,12 @@
         out[i * 8 : i * 8 + 8, :] = row
 
 
-def ocean(arrived_in, far_in, bag_in, height_in, current_in, wet_in, ho, co, arrived, far, bag, height, current, wet, hot, val, pair, src, ends, sweep, sems):
+def ocean(arrived, far_in, bag_in, height_in, current_in, wet_in, ho, co, far, bag, height, current, wet, hot, val, pair, src, ends, sweep, sems):
     gx = lax.axis_index("gx")
     copies = [
         pltpu.make_async_copy(a, b, sems.at[i])
         for i, (a, b) in enumerate(
             (
-                (arrived_in, arrived),
                 (far_in, far),
                 (bag_in, bag),
                 (height_in, height),
@@ -448,7 +496,6 @@
     ]
     for copy in copies:
         copy.start()
-    copies[0].wait()
     b16 = jnp.bfloat16
     lane = lax.broadcasted_iota(jnp.int32, (32, 128), 1)
     half = lane < 64
@@ -473,7 +520,7 @@
         hot[0:256, :], hot[256:512, :], (((1,), (1,)), ((), ())), preferred_element_type=F32
     )
     src[...] = both[:, 0:128] + both[:, 128:256]
-    for copy in copies[1:]:
+    for copy in copies:
         copy.wait()
     opposite = lax.rem(gx + 4, NB) * OCR
     bag_rows = lambda b, k, n: jnp.where(opposite == b * OCR, far[k : k + n, :], bag[b * OCR + k : b * OCR + k + n, :])
@@ -528,17 +575,18 @@
     co[...] = wet_float * (current[...] + increment)
 
 
-def ring(value, axis, step):
+def swap(value, axis, first):
     n = lax.axis_size(axis)
-    return lax.ppermute(value, axis, [(i, (i + step) % n) for i in range(n)])
+    pairs = [(i, (i + 1) % n) for i in range(0 if first else 1, n, 2)]
+    return lax.ppermute(value, axis, pairs + [(j, i) for i, j in pairs])
 
 
 def exchange(payload):
-    pxu, pxd, pyu, pyd, pz = payload
-    zs = ring(pz, "gz", 1)
-    xdn, xup = ring(pxu, "gx", 1), ring(pxd, "gx", -1)
-    ydn, yup = ring(pyu, "gy", 1), ring(pyd, "gy", -1)
-    return xdn, xup, ydn, yup, zs
+    pxe, pxo, pye, pyo, pz = payload
+    zs = swap(pz, "gz", True)
+    xe, xo = swap(pxe, "gx", True), swap(pxo, "gx", False)
+    ye, yo = swap(pye, "gy", True), swap(pyo, "gy", False)
+    return xe, xo, ye, yo, zs
 
 
 def local(velocity, stress, material, properties, owner_map, cell_map, height, current, sea_depth, wet_mask):
@@ -581,7 +629,7 @@
     mat, v1 = lax.optimization_barrier((mat, v1))
     (coef2,) = call(lame, [resident(2, CX, CY, CZ)], tab, mat)
     s1, *sent, bag = call(
-        functools.partial(strain, 2, False),
+        functools.partial(strain, 2),
         [s_shape] + PAYLOAD + [pz_shape, bag_shape],
         stress, v1, coef2, *r2, bag,
         scratch=[plane_z], aliases={0: 0, 8: 6},
@@ -600,34 +648,45 @@
         ],
     )
     r3, group, slot, code = lax.optimization_barrier((r3, group, slot, code))
-    v2, *sent, lift, bag = call(
+    *sent, lift, v_out, s1, coef2, bag = call(
         functools.partial(move, 3, True),
-        [v_shape] + PAYLOAD + [pz_lift, shape(32, 128), bag_shape],
-        v1, s1, coef, *r3, bag, lift,
-        scratch=[plane_z], aliases={0: 0, 8: 7},
-    )
-    r4 = exchange(sent)
-    v_out, s2, out, bag, far = call(
-        functools.partial(strain, 4, True),
-        [pltpu.HBM(dims, F32) for dims in ((3, CX, CY, CZ), (6, CX, CY, CZ), (64, 128), (BAG, 128), (OCR, 128))],
-        s1, v2, coef2, *r4, bag, lift, group, slot, code,
-        outs_at=[HB] * 5,
+        PAYLOAD
+        + [pz_lift, shape(32, 128)]
+        + [pltpu.HBM(dims, F32) for dims in ((3, CX, CY, CZ), (6, CX, CY, CZ), (2, CX, CY, CZ), (BAG, 128))],
+        v1, s1, coef, *r3, bag, lift, coef2,
+        outs_at=[VM] * 6 + [HB] * 4,
+        scratch=[plane_z, pltpu.VMEM((BAG, 128), F32), plane_z, pltpu.SemaphoreType.DMA((CX + 3,))],
+    )
+    *r4, zs = exchange(sent)
+    (out,) = call(
+        pack_lift,
+        [shape(64, 128)],
+        lift, zs, group, slot, code,
+        scratch=[pltpu.VMEM((512, 128), F32)],
+    )
+    s2, far = call(
+        finish,
+        [pltpu.HBM(dims, F32) for dims in ((6, CX, CY, CZ), (OCR, 128))],
+        *outside(s1, v_out, coef2, zs), *r4,
+        ins=[HB] * 4 + [VM] * 4,
+        outs_at=[HB] * 2,
         scratch=[
             pltpu.VMEM((6, CX, CY, CZ), F32),
             plane_z,
-            pltpu.VMEM((64, 128), F32),
-            pltpu.VMEM((512, 128), F32),
-            pltpu.SemaphoreType.DMA((CX + 4,)),
+            pltpu.VMEM((2, CX, CY, CZ), F32),
+            pltpu.VMEM((3 * CX + 1, CY, 128), F32),
+            plane_z,
+            pltpu.SemaphoreType.DMA((8 + CX,)),
         ],
     )
     arrived = lax.all_to_all(out, ("gx", "gy"), split_axis=0, concat_axis=0, tiled=True)
     block = pltpu.VMEM((LON, LAT), F32)
     height_out, current_out = call(
         ocean, [shape(LON, LAT)] * 2,
-        *outside(arrived, far, bag, height, current, wet_mask),
-        ins=[HB] * 6,
+        arrived, *outside(far, bag, height, current, wet_mask),
+        ins=[VM] + [HB] * 5,
         scratch=[
-            pltpu.VMEM((64, 128), F32), pltpu.VMEM((OCR, 128), F32), pltpu.VMEM((BAG, 128), F32),
+            pltpu.VMEM((OCR, 128), F32), pltpu.VMEM((BAG, 128), F32),
             block, block, pltpu.VMEM((LON, LAT), jnp.int32),
             pltpu.VMEM((512, 4096), jnp.bfloat16),
             pltpu.VMEM((64, 128), F32),
@@ -635,7 +694,7 @@
             pltpu.VMEM((256, 128), F32),
             pltpu.VMEM((32, 128), F32),
             pltpu.VMEM((72, 128), F32),
-            pltpu.SemaphoreType.DMA((6,)),
+            pltpu.SemaphoreType.DMA((5,)),
         ],
     )
     return v_out, s2, height_out, current_out

time: 84.5 us -> 72.4 us (0.86)
  blocking collectives: 18.2 us -> 0 us
  waiting for transfers between devices: 3.7 us -> 14.4 us
  starting transfers between devices: 40.7 us -> 32.6 us
  Pallas kernels: 20.7 us -> 24.2 us
    all_to_all x1 -> x0, blocking collectives: 18.2 us -> none  [local(): lax.all_to_all(out, ('gx', 'gy'), split_axis=0, concat_axis=0, tiled=True)]
    ppermute x20, starting transfers between devices: 40.7 us -> 25.1 us  [swap(): return lax.ppermute(value, axis, pairs + [(j, i) for i, j in pairs])]
    all_to_all x0 -> x1, starting transfers between devices: none -> 7.5 us  [local(): lax.all_to_all(out, ('gx', 'gy'), split_axis=0, concat_axis=0, tiled=True)]
    ppermute x20, waiting for transfers between devices: 3.7 us -> 9.77 us  [swap(): return lax.ppermute(value, axis, pairs + [(j, i) for i, j in pairs])]
    all_to_all x0 -> x1, waiting for transfers between devices: none -> 4.58 us  [local(): lax.all_to_all(out, ('gx', 'gy'), split_axis=0, concat_axis=0, tiled=True)]
    pallas_call x9 -> x10, Pallas kernels: 20.7 us -> 24.2 us  [call(): pl.pallas_call(body, out_shape=outs, in_specs=[VM] * len(args) if ins is...]
  transfers between devices with their start and end apart: 20 -> 21, of which waited for: 3 -> 4; matrix products, arithmetic and copies ran while one was open for 0% -> 0% of each run, Pallas kernels for 8% -> 17%
where the time goes in v2:
time: 72.4 us; the launch traced here: 72.2 us
  starting transfers between devices  32.6 us (45%)
  Pallas kernels  24.2 us (33%)
  waiting for transfers between devices  14.4 us (20%)
  between operations  1.02 us (1%)
    ppermute x20, starting transfers between devices, swap(): return lax.ppermute(value, axis, pairs + [(j, i) for i, j in pairs])  25.1 us
    pallas_call x10, Pallas kernels, call(): pl.pallas_call(body, out_shape=outs, in_specs=[VM] * len(args) if ins is...  24.2 us
    ppermute x20, waiting for transfers between devices, swap(): return lax.ppermute(value, axis, pairs + [(j, i) for i, j in pairs])  9.77 us
    all_to_all x1, starting transfers between devices, local(): lax.all_to_all(out, ('gx', 'gy'), split_axis=0, concat_axis=0, tiled=True)  7.5 us
    all_to_all x1, waiting for transfers between devices, local(): lax.all_to_all(out, ('gx', 'gy'), split_axis=0, concat_axis=0, tiled=True)  4.58 us
  transfers between devices with their start and end apart: 21, of which 4 were waited for; matrix products, arithmetic and copies ran while one was open for 0% of the time, Pallas kernels for 17%

profile of v2, /device:TPU:0, one launch (start us, length us, event | category | flops | bytes accessed | tf_op | source)
XLA Modules:
  0.0 72.2 jit_solution(13356470804454338649)
XLA Ops:
  0.6 1.9 %shard_map.130 = (f32[272,128]{1,0:T(8,128)S(1)}, f32[272,128]{1,0:T(8,128)S(1)}, f32[96,128]{1,0:T(8,128)S(1)}, f32[96,128]{1,0:T(8,128)S(1)}, f32[48,32,128]{2,1,0:T(8,128)S(1)}, /*index=5*/f32[768,128]{1,0:T(8,128)S(1)}) custom-call(f32[6,16,32,256]{3,2,1,0:T(8,128)} %s.1, f32[32,128]{1,0:T(8,128)} %depth.1, f32[32,128]{1,0:T(8,128)} %height_in.1, ...), custom_call_target="tpu_custom_call" | custom-call | tf_op jit(solution)/shard_map/pallas_call | solution.py:40
  2.5 0.1 collective-permute-start.4
  2.6 1.7 %collective-permute-start.2 = (f32[96,128]{1,0:T(8,128)S(1)}, f32[96,128]{1,0:T(8,128)S(1)}, u32[]{:S(2)}, u32[]{:S(2)}) collective-permute-start(f32[96,128]{1,0:T(8,128)S(1)} %get-tuple-element.65), channel_id=1, source_target_pairs={{0,2},{4,6},{8,10},{12,14},{2,0},{6,4},{10,8},{14,12},{1,3},{5,7},... | collective-permute-start | bytes 147464 | tf_op jit(solution)/shard_map/ppermute | solution.py:581
  4.3 4.7 %collective-permute-start.3 = (f32[96,128]{1,0:T(8,128)S(1)}, f32[96,128]{1,0:T(8,128)S(1)}, u32[]{:S(2)}, u32[]{:S(2)}) collective-permute-start(f32[96,128]{1,0:T(8,128)S(1)} %get-tuple-element.66), channel_id=1, source_target_pairs={{2,4},{6,8},{10,12},{14,0},{4,2},{8,6},{12,10},{0,14},{3,5},{7,9},... | collective-permute-start | bytes 147464 | tf_op jit(solution)/shard_map/ppermute | solution.py:581
  9.0 1.9 %collective-permute-start = (f32[272,128]{1,0:T(8,128)S(1)}, f32[272,128]{1,0:T(8,128)S(1)}, u32[]{:S(2)}, u32[]{:S(2)}) collective-permute-start(f32[272,128]{1,0:T(8,128)S(1)} %get-tuple-element.63), channel_id=1, source_target_pairs={{0,16},{32,48},{64,80},{96,112},{16,0},{48,32},{80,64},{112,96},{1... | collective-permute-start | bytes 417800 | tf_op jit(solution)/shard_map/ppermute | solution.py:581
  10.9 2.6 %collective-permute-start.1 = (f32[272,128]{1,0:T(8,128)S(1)}, f32[272,128]{1,0:T(8,128)S(1)}, u32[]{:S(2)}, u32[]{:S(2)}) collective-permute-start(f32[272,128]{1,0:T(8,128)S(1)} %get-tuple-element.64), channel_id=1, source_target_pairs={{16,32},{48,64},{80,96},{112,0},{32,16},{64,48},{96,80},{0,112},{1... | collective-permute-start | bytes 417800 | tf_op jit(solution)/shard_map/ppermute | solution.py:581
  13.6 2.6 %shard_map.129 = (f32[3,16,32,256]{3,2,1,0:T(8,128)S(1)}, f32[6,16,32,256]{3,2,1,0:T(8,128)S(1)}, s32[16,32,256]{2,1,0:T(8,128)S(1)}, f32[1,16,32,256]{3,2,1,0:T(8,128)S(1)}) custom-call(f32[3,16,32,256]{3,2,1,0:T(8,128)} %v_hbm.1, f32[6,16,32,256]{3,2,1,0:T(8,128)} %s.1, s32[16,32,256]{2,1,0:T(8,128)} %mat_hbm.1, f32[24,128]{1,0:T(8,128)S(1)} %broadcast_bitcast_fusion.tab), custom_call_target="tpu_custom_call" | custom-call | tf_op jit(solution)/shard_map/pallas_call | solution.py:40
  16.2 2.5 %collective-permute-done.1.xo = f32[272,128]{1,0:T(8,128)S(1)} collective-permute-done((f32[272,128]{1,0:T(8,128)S(1)}, f32[272,128]{1,0:T(8,128)S(1)}, u32[]{:S(2)}, u32[]{:S(2)}) %collective-permute-start.1) | collective-permute-done | bytes 139296 | tf_op jit(solution)/shard_map/ppermute | solution.py:581
  18.7 1.9 %shard_map.131 = (f32[3,16,32,256]{3,2,1,0:T(8,128)S(1)}, f32[272,128]{1,0:T(8,128)S(1)}, f32[272,128]{1,0:T(8,128)S(1)}, f32[96,128]{1,0:T(8,128)S(1)}, f32[96,...) custom-call(f32[3,16,32,256]{3,2,1,0:T(8,128)S(1)} %get-tuple-elemen, ...), custom_call_target="tpu_custom_call", output_to_operand_aliasing={{0}: (0, {}), {7}: (8, {})} | custom-call | tf_op jit(solution)/shard_map/pallas_call | solution.py:40
  20.7 0.1 collective-permute-start.9
  20.7 0.1 collective-permute-start.5
  20.8 2.2 %collective-permute-start.6 = (f32[272,128]{1,0:T(8,128)S(1)}, f32[272,128]{1,0:T(8,128)S(1)}, u32[]{:S(2)}, u32[]{:S(2)}) collective-permute-start(f32[272,128]{1,0:T(8,128)S(1)} %get-tuple-element.73), channel_id=1, source_target_pairs={{16,32},{48,64},{80,96},{112,0},{32,16},{64,48},{96,80},{0,112},{1... | collective-permute-start | bytes 417800 | tf_op jit(solution)/shard_map/ppermute | solution.py:581
  23.0 2.4 %collective-permute-start.8 = (f32[96,128]{1,0:T(8,128)S(1)}, f32[96,128]{1,0:T(8,128)S(1)}, u32[]{:S(2)}, u32[]{:S(2)}) collective-permute-start(f32[96,128]{1,0:T(8,128)S(1)} %get-tuple-element.75), channel_id=1, source_target_pairs={{2,4},{6,8},{10,12},{14,0},{4,2},{8,6},{12,10},{0,14},{3,5},{7,9},... | collective-permute-start | bytes 147464 | tf_op jit(solution)/shard_map/ppermute | solution.py:581
  25.4 1.6 %shard_map.132.coef.refs_1_ = f32[2,16,32,256]{3,2,1,0:T(8,128)S(1)} custom-call(f32[24,128]{1,0:T(8,128)S(1)} %broadcast_bitcast_fusion.tab, s32[16,32,256]{2,1,0:T(8,128)S(1)} %get-tuple-element.71.mat), custom_call_target="tpu_custom_call" | custom-call | tf_op jit(solution)/shard_map/pallas_call | solution.py:40
  27.1 3.6 %collective-permute-done.8.yo = f32[96,128]{1,0:T(8,128)S(1)} collective-permute-done((f32[96,128]{1,0:T(8,128)S(1)}, f32[96,128]{1,0:T(8,128)S(1)}, u32[]{:S(2)}, u32[]{:S(2)}) %collective-permute-start.8) | collective-permute-done | bytes 49184 | tf_op jit(solution)/shard_map/ppermute | solution.py:581
  30.7 2.2 %shard_map.133 = (f32[6,16,32,256]{3,2,1,0:T(8,128)S(1)}, f32[272,128]{1,0:T(8,128)S(1)}, f32[272,128]{1,0:T(8,128)S(1)}, f32[96,128]{1,0:T(8,128)S(1)}, f32[96,...) custom-call(f32[6,16,32,256]{3,2,1,0:T(8,128)S(1)} %get-tuple-elemen, ...), custom_call_target="tpu_custom_call", output_to_operand_aliasing={{0}: (0, {}), {6}: (8, {})} | custom-call | tf_op jit(solution)/shard_map/pallas_call | solution.py:40
  32.9 0.1 collective-permute-start.14
  33.0 1.3 %collective-permute-start.10 = (f32[272,128]{1,0:T(8,128)S(1)}, f32[272,128]{1,0:T(8,128)S(1)}, u32[]{:S(2)}, u32[]{:S(2)}) collective-permute-start(f32[272,128]{1,0:T(8,128)S(1)} %get-tuple-element.80), channel_id=1, source_target_pairs={{0,16},{32,48},{64,80},{96,112},{16,0},{48,32},{80,64},{112,96},{1... | collective-permute-start | bytes 417800 | tf_op jit(solution)/shard_map/ppermute | solution.py:581
  34.3 1.8 %collective-permute-start.11 = (f32[272,128]{1,0:T(8,128)S(1)}, f32[272,128]{1,0:T(8,128)S(1)}, u32[]{:S(2)}, u32[]{:S(2)}) collective-permute-start(f32[272,128]{1,0:T(8,128)S(1)} %get-tuple-element.81), channel_id=1, source_target_pairs={{16,32},{48,64},{80,96},{112,0},{32,16},{64,48},{96,80},{0,112},{1... | collective-permute-start | bytes 417800 | tf_op jit(solution)/shard_map/ppermute | solution.py:581
  36.1 2.0 %collective-permute-start.13 = (f32[96,128]{1,0:T(8,128)S(1)}, f32[96,128]{1,0:T(8,128)S(1)}, u32[]{:S(2)}, u32[]{:S(2)}) collective-permute-start(f32[96,128]{1,0:T(8,128)S(1)} %get-tuple-element.83), channel_id=1, source_target_pairs={{2,4},{6,8},{10,12},{14,0},{4,2},{8,6},{12,10},{0,14},{3,5},{7,9},... | collective-permute-start | bytes 147464 | tf_op jit(solution)/shard_map/ppermute | solution.py:581
  38.1 2.1 %shard_map.134 = (f32[8,512]{1,0:T(8,128)S(1)}, f32[512,128]{1,0:T(8,128)S(1)}, f32[8,128]{1,0:T(8,128)S(1)}) custom-call(s32[64,1,512]{2,1,0:T(1,128)} %bitcast.10, s32[64,512]{1,0:T(8,128)} %cell_rows), custom_call_target="tpu_custom_call" | custom-call | tf_op jit(solution)/shard_map/pallas_call | solution.py:40
  40.2 3.6 %collective-permute-done.13.yo = f32[96,128]{1,0:T(8,128)S(1)} collective-permute-done((f32[96,128]{1,0:T(8,128)S(1)}, f32[96,128]{1,0:T(8,128)S(1)}, u32[]{:S(2)}, u32[]{:S(2)}) %collective-permute-start.13) | collective-permute-done | bytes 49184 | tf_op jit(solution)/shard_map/ppermute | solution.py:581
  43.8 3.4 %shard_map.135 = (f32[272,128]{1,0:T(8,128)S(1)}, f32[272,128]{1,0:T(8,128)S(1)}, f32[96,128]{1,0:T(8,128)S(1)}, f32[96,128]{1,0:T(8,128)S(1)}, f32[49,32,128]{2...) custom-call(f32[3,16,32,256]{3,2,1,0:T(8,128)S(1)} %get-tuple-elemen, ...), custom_call_target="tpu_custom_call" | custom-call | tf_op jit(solution)/shard_map/pallas_call | solution.py:40
  47.2 0.1 collective-permute-start.15
  47.3 0.2 collective-permute-start.16
  47.5 2.4 %collective-permute-start.17 = (f32[272,128]{1,0:T(8,128)S(1)}, f32[272,128]{1,0:T(8,128)S(1)}, u32[]{:S(2)}, u32[]{:S(2)}) collective-permute-start(f32[272,128]{1,0:T(8,128)S(1)} %get-tuple-element.102), channel_id=1, source_target_pairs={{16,32},{48,64},{80,96},{112,0},{32,16},{64,48},{96,80},{0,112},{1... | collective-permute-start | bytes 417800 | tf_op jit(solution)/shard_map/ppermute | solution.py:581
  49.8 1.6 %collective-permute-start.19 = (f32[96,128]{1,0:T(8,128)S(1)}, f32[96,128]{1,0:T(8,128)S(1)}, u32[]{:S(2)}, u32[]{:S(2)}) collective-permute-start(f32[96,128]{1,0:T(8,128)S(1)} %get-tuple-element.104), channel_id=1, source_target_pairs={{2,4},{6,8},{10,12},{14,0},{4,2},{8,6},{12,10},{0,14},{3,5},{7,9},... | collective-permute-start | bytes 147464 | tf_op jit(solution)/shard_map/ppermute | solution.py:581
  51.4 0.9 %shard_map.137 = f32[64,128]{1,0:T(8,128)} custom-call(f32[32,128]{1,0:T(8,128)S(1)} %get-tuple-element.106.lift_here, f32[49,32,128]{2,1,0:T(8,128)S(1)} %collective-permute-done.15.zs_in.zs, f32[8,512]{1,0:T(8,128)S(1)} %get-tuple-element.107.group, f32[512,128]{1,0:T(8,128)S(1)} %get-tuple-element.108.slot, f32[8,128]{1,0:T(8,128)S(1)} %get-tuple-element.109.code), custom_call_target="tpu_custom_call" | custom-call | tf_op jit(solution)/shard_map/pallas_call | solution.py:40
  52.3 7.5 %all-to-all-start = ((f32[64,1,128]{2,1,0:T(1,128)}), f32[64,1,128]{2,1,0:T(1,128)S(1)}, u32[]{:S(2)}, u32[]{:S(2)}) async-start(f32[64,1,128]{2,1,0:T(1,128)} %bitcast.4), calls=%async_computation | async-start | bytes 65536 | tf_op jit(solution)/shard_map/all_to_all | solution.py:682
  59.9 4.8 %shard_map.136 = (f32[6,16,32,256]{3,2,1,0:T(8,128)}, f32[80,128]{1,0:T(8,128)}) custom-call(f32[6,16,32,256]{3,2,1,0:T(8,128)} %get-tuple-element.98.s_in, f32[3,16,32,256]{3,2,1,0:T(8,128)} %get-tuple-element.55.v_in, f32[2,16,32,256]{3,2,1,0:T(8,128)} %get-tuple-element.99.coef_in, f32[49,32,128]{2,1,0:T(8,128)} %copy-done, ...), custom_call_target="tpu_custom_call" | custom-call | tf_op jit(solution)/shard_map/pallas_call | solution.py:40
  64.8 4.6 %all-to-all-done = f32[64,1,128]{2,1,0:T(1,128)S(1)} async-done(((f32[64,1,128]{2,1,0:T(1,128)}), f32[64,1,128]{2,1,0:T(1,128)S(1)}, u32[]{:S(2)}, u32[]{:S(2)}) %all-to-all-start) | async-done | bytes 32800 | tf_op jit(solution)/shard_map/all_to_all | solution.py:682
  69.3 2.7 %shard_map.138 = (f32[32,128]{1,0:T(8,128)}, f32[32,128]{1,0:T(8,128)}) custom-call(f32[64,128]{1,0:T(8,128)S(1)} %bitcast.9, f32[80,128]{1,0:T(8,128)} %get-tuple-element.110.far_in, f32[768,128]{1,0:T(8,128)} %get-tuple-element.111.bag_in, f32[32,128]{1,0:T(8,128)} %height_in.1, f32[32,128]{1,0:T(8,128)} %current_in.1, s32[32,128]{1,0:T(8,128)} %wet_in.1), custom_call_target="tpu_custom_call" | custom-call | tf_op jit(solution)/shard_map/pallas_call | solution.py:40
  (29 shorter events, 0.1 us)
Async XLA Ops:
  0.6 12.9 %copy-start.1 = (f32[16,3]{0,1:T(4,128)S(1)}, f32[16,3]{0,1:T(4,128)}, u32[]{:S(2)}) copy-start(f32[16,3]{0,1:T(4,128)} %param.13) | copy-start | bytes 580
  2.5 16.2 %collective-permute-start.4 = (f32[48,32,128]{2,1,0:T(8,128)S(1)}, f32[48,32,128]{2,1,0:T(8,128)S(1)}, u32[]{:S(2)}, u32[]{:S(2)}) collective-permute-start(f32[48,32,128]{2,1,0:T(8,128)S(1)} %get-tuple-element.67), channel_id=1, source_target_pairs={{0,1},{1,0},{2,3},{3,2},{4,5},{5,4},{6,7},{7,6},{8,9},{9,8},{10,11... | collective-permute-start | bytes 2359304 | tf_op jit(solution)/shard_map/ppermute | solution.py:581
  2.6 13.6 %collective-permute-start.2 = (f32[96,128]{1,0:T(8,128)S(1)}, f32[96,128]{1,0:T(8,128)S(1)}, u32[]{:S(2)}, u32[]{:S(2)}) collective-permute-start(f32[96,128]{1,0:T(8,128)S(1)} %get-tuple-element.65), channel_id=1, source_target_pairs={{0,2},{4,6},{8,10},{12,14},{2,0},{6,4},{10,8},{14,12},{1,3},{5,7},... | collective-permute-start | bytes 147464 | tf_op jit(solution)/shard_map/ppermute | solution.py:581
  4.3 11.9 %collective-permute-start.3 = (f32[96,128]{1,0:T(8,128)S(1)}, f32[96,128]{1,0:T(8,128)S(1)}, u32[]{:S(2)}, u32[]{:S(2)}) collective-permute-start(f32[96,128]{1,0:T(8,128)S(1)} %get-tuple-element.66), channel_id=1, source_target_pairs={{2,4},{6,8},{10,12},{14,0},{4,2},{8,6},{12,10},{0,14},{3,5},{7,9},... | collective-permute-start | bytes 147464 | tf_op jit(solution)/shard_map/ppermute | solution.py:581
  9.0 7.2 %collective-permute-start = (f32[272,128]{1,0:T(8,128)S(1)}, f32[272,128]{1,0:T(8,128)S(1)}, u32[]{:S(2)}, u32[]{:S(2)}) collective-permute-start(f32[272,128]{1,0:T(8,128)S(1)} %get-tuple-element.63), channel_id=1, source_target_pairs={{0,16},{32,48},{64,80},{96,112},{16,0},{48,32},{80,64},{112,96},{1... | collective-permute-start | bytes 417800 | tf_op jit(solution)/shard_map/ppermute | solution.py:581
  10.9 7.8 %collective-permute-start.1 = (f32[272,128]{1,0:T(8,128)S(1)}, f32[272,128]{1,0:T(8,128)S(1)}, u32[]{:S(2)}, u32[]{:S(2)}) collective-permute-start(f32[272,128]{1,0:T(8,128)S(1)} %get-tuple-element.64), channel_id=1, source_target_pairs={{16,32},{48,64},{80,96},{112,0},{32,16},{64,48},{96,80},{0,112},{1... | collective-permute-start | bytes 417800 | tf_op jit(solution)/shard_map/ppermute | solution.py:581
  20.7 10.1 %collective-permute-start.9 = (f32[48,32,128]{2,1,0:T(8,128)S(1)}, f32[48,32,128]{2,1,0:T(8,128)S(1)}, u32[]{:S(2)}, u32[]{:S(2)}) collective-permute-start(f32[48,32,128]{2,1,0:T(8,128)S(1)} %get-tuple-element.76), channel_id=1, source_target_pairs={{0,1},{1,0},{2,3},{3,2},{4,5},{5,4},{6,7},{7,6},{8,9},{9,8},{10,11... | collective-permute-start | bytes 2359304 | tf_op jit(solution)/shard_map/ppermute | solution.py:581
  20.7 10.0 %collective-permute-start.5 = (f32[272,128]{1,0:T(8,128)S(1)}, f32[272,128]{1,0:T(8,128)S(1)}, u32[]{:S(2)}, u32[]{:S(2)}) collective-permute-start(f32[272,128]{1,0:T(8,128)S(1)} %get-tuple-element.72), channel_id=1, source_target_pairs={{0,16},{32,48},{64,80},{96,112},{16,0},{48,32},{80,64},{112,96},{1... | collective-permute-start | bytes 417800 | tf_op jit(solution)/shard_map/ppermute | solution.py:581
  20.8 9.9 %collective-permute-start.6 = (f32[272,128]{1,0:T(8,128)S(1)}, f32[272,128]{1,0:T(8,128)S(1)}, u32[]{:S(2)}, u32[]{:S(2)}) collective-permute-start(f32[272,128]{1,0:T(8,128)S(1)} %get-tuple-element.73), channel_id=1, source_target_pairs={{16,32},{48,64},{80,96},{112,0},{32,16},{64,48},{96,80},{0,112},{1... | collective-permute-start | bytes 417800 | tf_op jit(solution)/shard_map/ppermute | solution.py:581
  23.0 4.1 %collective-permute-start.7 = (f32[96,128]{1,0:T(8,128)S(1)}, f32[96,128]{1,0:T(8,128)S(1)}, u32[]{:S(2)}, u32[]{:S(2)}) collective-permute-start(f32[96,128]{1,0:T(8,128)S(1)} %get-tuple-element.74), channel_id=1, source_target_pairs={{0,2},{4,6},{8,10},{12,14},{2,0},{6,4},{10,8},{14,12},{1,3},{5,7},... | collective-permute-start | bytes 147464 | tf_op jit(solution)/shard_map/ppermute | solution.py:581
  23.0 7.7 %collective-permute-start.8 = (f32[96,128]{1,0:T(8,128)S(1)}, f32[96,128]{1,0:T(8,128)S(1)}, u32[]{:S(2)}, u32[]{:S(2)}) collective-permute-start(f32[96,128]{1,0:T(8,128)S(1)} %get-tuple-element.75), channel_id=1, source_target_pairs={{2,4},{6,8},{10,12},{14,0},{4,2},{8,6},{12,10},{0,14},{3,5},{7,9},... | collective-permute-start | bytes 147464 | tf_op jit(solution)/shard_map/ppermute | solution.py:581
  32.9 10.9 %collective-permute-start.14 = (f32[48,32,128]{2,1,0:T(8,128)S(1)}, f32[48,32,128]{2,1,0:T(8,128)S(1)}, u32[]{:S(2)}, u32[]{:S(2)}) collective-permute-start(f32[48,32,128]{2,1,0:T(8,128)S(1)} %get-tuple-element.84), channel_id=1, source_target_pairs={{0,1},{1,0},{2,3},{3,2},{4,5},{5,4},{6,7},{7,6},{8,9},{9,8},{10,11... | collective-permute-start | bytes 2359304 | tf_op jit(solution)/shard_map/ppermute | solution.py:581
  33.0 10.8 %collective-permute-start.10 = (f32[272,128]{1,0:T(8,128)S(1)}, f32[272,128]{1,0:T(8,128)S(1)}, u32[]{:S(2)}, u32[]{:S(2)}) collective-permute-start(f32[272,128]{1,0:T(8,128)S(1)} %get-tuple-element.80), channel_id=1, source_target_pairs={{0,16},{32,48},{64,80},{96,112},{16,0},{48,32},{80,64},{112,96},{1... | collective-permute-start | bytes 417800 | tf_op jit(solution)/shard_map/ppermute | solution.py:581
  34.3 9.5 %collective-permute-start.11 = (f32[272,128]{1,0:T(8,128)S(1)}, f32[272,128]{1,0:T(8,128)S(1)}, u32[]{:S(2)}, u32[]{:S(2)}) collective-permute-start(f32[272,128]{1,0:T(8,128)S(1)} %get-tuple-element.81), channel_id=1, source_target_pairs={{16,32},{48,64},{80,96},{112,0},{32,16},{64,48},{96,80},{0,112},{1... | collective-permute-start | bytes 417800 | tf_op jit(solution)/shard_map/ppermute | solution.py:581
  36.1 4.1 %collective-permute-start.12 = (f32[96,128]{1,0:T(8,128)S(1)}, f32[96,128]{1,0:T(8,128)S(1)}, u32[]{:S(2)}, u32[]{:S(2)}) collective-permute-start(f32[96,128]{1,0:T(8,128)S(1)} %get-tuple-element.82), channel_id=1, source_target_pairs={{0,2},{4,6},{8,10},{12,14},{2,0},{6,4},{10,8},{14,12},{1,3},{5,7},... | collective-permute-start | bytes 147464 | tf_op jit(solution)/shard_map/ppermute | solution.py:581
  36.1 7.7 %collective-permute-start.13 = (f32[96,128]{1,0:T(8,128)S(1)}, f32[96,128]{1,0:T(8,128)S(1)}, u32[]{:S(2)}, u32[]{:S(2)}) collective-permute-start(f32[96,128]{1,0:T(8,128)S(1)} %get-tuple-element.83), channel_id=1, source_target_pairs={{2,4},{6,8},{10,12},{14,0},{4,2},{8,6},{12,10},{0,14},{3,5},{7,9},... | collective-permute-start | bytes 147464 | tf_op jit(solution)/shard_map/ppermute | solution.py:581
  47.2 4.2 %collective-permute-start.15 = (f32[49,32,128]{2,1,0:T(8,128)S(1)}, f32[49,32,128]{2,1,0:T(8,128)S(1)}, u32[]{:S(2)}, u32[]{:S(2)}) collective-permute-start(f32[49,32,128]{2,1,0:T(8,128)S(1)} %get-tuple-element.100), channel_id=1, source_target_pairs={{0,1},{1,0},{2,3},{3,2},{4,5},{5,4},{6,7},{7,6},{8,9},{9,8},{10,11... | collective-permute-start | bytes 2408456 | tf_op jit(solution)/shard_map/ppermute | solution.py:581
  47.3 12.6 %collective-permute-start.16 = (f32[272,128]{1,0:T(8,128)S(1)}, f32[272,128]{1,0:T(8,128)S(1)}, u32[]{:S(2)}, u32[]{:S(2)}) collective-permute-start(f32[272,128]{1,0:T(8,128)S(1)} %get-tuple-element.101), channel_id=1, source_target_pairs={{0,16},{32,48},{64,80},{96,112},{16,0},{48,32},{80,64},{112,96},{1... | collective-permute-start | bytes 417800 | tf_op jit(solution)/shard_map/ppermute | solution.py:581
  47.5 12.4 %collective-permute-start.17 = (f32[272,128]{1,0:T(8,128)S(1)}, f32[272,128]{1,0:T(8,128)S(1)}, u32[]{:S(2)}, u32[]{:S(2)}) collective-permute-start(f32[272,128]{1,0:T(8,128)S(1)} %get-tuple-element.102), channel_id=1, source_target_pairs={{16,32},{48,64},{80,96},{112,0},{32,16},{64,48},{96,80},{0,112},{1... | collective-permute-start | bytes 417800 | tf_op jit(solution)/shard_map/ppermute | solution.py:581
  49.8 10.0 %collective-permute-start.18 = (f32[96,128]{1,0:T(8,128)S(1)}, f32[96,128]{1,0:T(8,128)S(1)}, u32[]{:S(2)}, u32[]{:S(2)}) collective-permute-start(f32[96,128]{1,0:T(8,128)S(1)} %get-tuple-element.103), channel_id=1, source_target_pairs={{0,2},{4,6},{8,10},{12,14},{2,0},{6,4},{10,8},{14,12},{1,3},{5,7},... | collective-permute-start | bytes 147464 | tf_op jit(solution)/shard_map/ppermute | solution.py:581
  49.8 10.0 %collective-permute-start.19 = (f32[96,128]{1,0:T(8,128)S(1)}, f32[96,128]{1,0:T(8,128)S(1)}, u32[]{:S(2)}, u32[]{:S(2)}) collective-permute-start(f32[96,128]{1,0:T(8,128)S(1)} %get-tuple-element.104), channel_id=1, source_target_pairs={{2,4},{6,8},{10,12},{14,0},{4,2},{8,6},{12,10},{0,14},{3,5},{7,9},... | collective-permute-start | bytes 147464 | tf_op jit(solution)/shard_map/ppermute | solution.py:581
  51.4 8.5 %copy-start = (f32[49,32,128]{2,1,0:T(8,128)}, f32[49,32,128]{2,1,0:T(8,128)S(1)}, u32[]{:S(2)}) copy-start(f32[49,32,128]{2,1,0:T(8,128)S(1)} %collective-permute-done.15.zs_in.zs) | copy-start | bytes 2408452
  52.3 17.0 %all-to-all-start = ((f32[64,1,128]{2,1,0:T(1,128)}), f32[64,1,128]{2,1,0:T(1,128)S(1)}, u32[]{:S(2)}, u32[]{:S(2)}) async-start(f32[64,1,128]{2,1,0:T(1,128)} %bitcast.4), calls=%async_computation | async-start | bytes 65536 | tf_op jit(solution)/shard_map/all_to_all | solution.py:682

commit v3 on v2

--- a/solution.py
+++ b/solution.py
@@ -195,7 +195,7 @@
     pxe[base + 10 : base + 16, :] = jnp.zeros((6, LAT), F32)
 
 
-def slopes_z(src, comps, out):
+def slopes_z(src, out, comps):
     k = lax.broadcasted_iota(jnp.int32, (CZ, CZ), 0)
     n = lax.broadcasted_iota(jnp.int32, (CZ, CZ), 1)
     step = jnp.where(k == n + 1, 1.0, 0.0) - jnp.where(k == n - 1, 1.0, 0.0)
@@ -284,7 +284,7 @@
     lax.fori_loop(0, CX, plane, 0)
 
 
-def fetch(v_hbm, s_hbm, mat_hbm, tab, v, s, mat, coef, sems):
+def fetch(v_hbm, s_hbm, mat_hbm, tab, v, s, mat, coef, dzs, sems):
     copies = [
         pltpu.make_async_copy(a, b, sems.at[i])
         for i, (a, b) in enumerate(((mat_hbm, mat), (s_hbm, s), (v_hbm, v)))
@@ -294,10 +294,12 @@
     copies[0].wait()
     lookup(tab, mat, coef, (0,))
     copies[1].wait()
+    slopes_z(s, dzs, SZ)
     copies[2].wait()
 
 
-def lame(tab, mat, coef):
+def lame(tab, mat, v, coef, dzs):
+    slopes_z(v, dzs, VA)
     lookup(tab, mat, coef, (1, 2))
 
 
@@ -309,17 +311,13 @@
         bag[pl.ds(row, OCR), :] = ref[XF:, :]
 
 
-def move(distance, has_lift, v, s, coef, xe, xo, ye, yo, zs, bag_in, *refs):
+def move(distance, has_lift, v, s, coef, dzs, xe, xo, ye, yo, zs, bag_in, *refs):
     if has_lift:
-        lift_in, coef2, pxe, pxo, pye, pyo, pz, lift_out, v_hbm, s_hbm, coef_hbm, bag_hbm, vo, bag, dzs, sems = refs
-        copies = [
-            pltpu.make_async_copy(s, s_hbm, sems.at[CX]),
-            pltpu.make_async_copy(coef2, coef_hbm, sems.at[CX + 1]),
-            pltpu.make_async_copy(bag, bag_hbm, sems.at[CX + 2]),
-        ]
+        lift_in, pxe, pxo, pye, pyo, pz, lift_out, v_hbm, bag_hbm, vo, bag, sems = refs
+        copies = [pltpu.make_async_copy(bag, bag_hbm, sems.at[CX])]
         bag[...] = bag_in[...]
     else:
-        vo, pxe, pxo, pye, pyo, pz, lift_out, bag, dzs = refs
+        vo, pxe, pxo, pye, pyo, pz, lift_out, bag = refs
     gz = lax.axis_index("gz")
     flip = odd("gy")
     sub, lane = iotas()
@@ -327,7 +325,6 @@
     if has_lift:
         for copy in copies:
             copy.start()
-    slopes_z(s, SZ, dzs)
     dx, dy, dz = differences(s, (SX, SY, SZ), dzs, xe, xo, ye, yo, zs)
     lift = [lift_in[t * 8 : t * 8 + 8, :] if has_lift else jnp.zeros((8, 128), F32) for t in range(4)]
     for x in range(CX):
@@ -359,20 +356,25 @@
             copy.wait()
 
 
-def strain(distance, s, v, coef, xe, xo, ye, yo, zs, bag_in, so, pxe, pxo, pye, pyo, pz, bag, dzs):
+def strain(distance, s, v, coef, dzs, xe, xo, ye, yo, zs, bag_in, so, pxe, pxo, pye, pyo, pz, bag, s_hbm, coef_hbm, sems):
+    copies = [pltpu.make_async_copy(coef, coef_hbm, sems.at[CX])]
+    copies[0].start()
     collect(distance, xe, xo, bag)
-    slopes_z(v, VA, dzs)
     gz, flip = lax.axis_index("gz"), odd("gy")
 
     def done(x, new):
         for i in range(3):
             put_y(flip, x, i, new[SY[i]], pye, pyo)
             put_z(gz, x, i, new[SZ[i]], pz)
+        copies.append(pltpu.make_async_copy(so.at[:, x], s_hbm.at[:, x], sems.at[x]))
+        copies[-1].start()
 
     stretch(s, v, coef, dzs, xe, xo, ye, yo, zs, so, done)
     put_x_faces(so, SX, pxe, pxo)
     pxe[XF:, :] = xo[XF:, :]
     pxo[XF:, :] = xe[XF:, :]
+    for copy in copies:
+        copy.wait()
 
 
 def finish(s_in, v_in, coef_in, zs_in, xe, xo, ye, yo, s_hbm, far_hbm, s, v, coef, zs, dzs, sems):
@@ -389,8 +391,8 @@
     for copy in early + parts:
         copy.start()
     early[0].wait()
-    slopes_z(v, VA, dzs)
-    for copy in early[1:] + parts:
+    slopes_z(v, dzs, VA)
+    for copy in early[1:]:
         copy.wait()
     late = []
 
@@ -398,14 +400,19 @@
         late.append(pltpu.make_async_copy(s.at[:, x], s_hbm.at[:, x], sems.at[8 + x]))
         late[-1].start()
 
-    stretch(s, v, coef, dzs, xe, xo, ye, yo, zs, s, done)
+    def ready(x):
+        if x % 4 == 0:
+            parts[x // 4].wait()
+
+    stretch(s, v, coef, dzs, xe, xo, ye, yo, zs, s, done, ready)
     for copy in late:
         copy.wait()
 
 
-def stretch(s, v, coef, dzs, xe, xo, ye, yo, zs, so, done):
+def stretch(s, v, coef, dzs, xe, xo, ye, yo, zs, so, done, ready=lambda x: None):
     dx, dy, dz = differences(v, (VA, VA, VA), dzs, xe, xo, ye, yo, zs)
     for x in range(CX):
+        ready(x)
         ey = [dy(x, c, grab(v, c, x)) for c in range(3)]
         ez = [dz(x, c) for c in range(3)]
         new = [[[None, None] for _ in range(4)] for _ in range(6)]
@@ -612,9 +619,9 @@
         ],
     )
     r1 = exchange(sent)
-    velocity, stress, mat, coef = call(
+    velocity, stress, mat, coef, dzs = call(
         fetch,
-        [v_shape, s_shape, pltpu.VMEM((CX, CY, CZ), jnp.int32), resident(1, CX, CY, CZ)],
+        [v_shape, s_shape, pltpu.VMEM((CX, CY, CZ), jnp.int32), resident(1, CX, CY, CZ), v_shape],
         *outside(velocity, stress, material), tab,
         ins=[HB] * 3 + [VM],
         scratch=[pltpu.SemaphoreType.DMA((3,))],
@@ -622,17 +629,18 @@
     v1, *sent, lift, bag = call(
         functools.partial(move, 1, False),
         [v_shape] + PAYLOAD + [pz_shape, shape(32, 128), bag_shape],
-        velocity, stress, coef, *r1, bag,
-        scratch=[plane_z], aliases={0: 0, 8: 7},
+        velocity, stress, coef, dzs, *r1, bag,
+        aliases={0: 0, 9: 7},
     )
     r2 = exchange(sent)
     mat, v1 = lax.optimization_barrier((mat, v1))
-    (coef2,) = call(lame, [resident(2, CX, CY, CZ)], tab, mat)
-    s1, *sent, bag = call(
+    coef2, dzs = call(lame, [resident(2, CX, CY, CZ), v_shape], tab, mat, v1)
+    s1, *sent, bag, s_copy, coef_copy = call(
         functools.partial(strain, 2),
-        [s_shape] + PAYLOAD + [pz_shape, bag_shape],
-        stress, v1, coef2, *r2, bag,
-        scratch=[plane_z], aliases={0: 0, 8: 6},
+        [s_shape] + PAYLOAD + [pz_shape, bag_shape] + [pltpu.HBM(dims, F32) for dims in ((6, CX, CY, CZ), (2, CX, CY, CZ))],
+        stress, v1, coef2, dzs, *r2, bag,
+        outs_at=[VM] * 7 + [HB] * 2,
+        scratch=[pltpu.SemaphoreType.DMA((CX + 1,))], aliases={0: 0, 9: 6},
     )
     r3 = exchange(sent)
     owners, cells, s1 = lax.optimization_barrier((owner_map.reshape(64, 1, 512), cell_map, s1))
@@ -647,15 +655,16 @@
             pltpu.SemaphoreType.DMA((2,)),
         ],
     )
+    (dzs,) = call(functools.partial(slopes_z, comps=SZ), [v_shape], s1)
     r3, group, slot, code = lax.optimization_barrier((r3, group, slot, code))
-    *sent, lift, v_out, s1, coef2, bag = call(
+    *sent, lift, v_out, bag = call(
         functools.partial(move, 3, True),
         PAYLOAD
         + [pz_lift, shape(32, 128)]
-        + [pltpu.HBM(dims, F32) for dims in ((3, CX, CY, CZ), (6, CX, CY, CZ), (2, CX, CY, CZ), (BAG, 128))],
-        v1, s1, coef, *r3, bag, lift, coef2,
-        outs_at=[VM] * 6 + [HB] * 4,
-        scratch=[plane_z, pltpu.VMEM((BAG, 128), F32), plane_z, pltpu.SemaphoreType.DMA((CX + 3,))],
+        + [pltpu.HBM(dims, F32) for dims in ((3, CX, CY, CZ), (BAG, 128))],
+        v1, s1, coef, dzs, *r3, bag, lift,
+        outs_at=[VM] * 6 + [HB] * 2,
+        scratch=[plane_z, pltpu.VMEM((BAG, 128), F32), pltpu.SemaphoreType.DMA((CX + 1,))],
     )
     *r4, zs = exchange(sent)
     (out,) = call(
@@ -667,7 +676,7 @@
     s2, far = call(
         finish,
         [pltpu.HBM(dims, F32) for dims in ((6, CX, CY, CZ), (OCR, 128))],
-        *outside(s1, v_out, coef2, zs), *r4,
+        *outside(s_copy, v_out, coef_copy, zs), *r4,
         ins=[HB] * 4 + [VM] * 4,
         outs_at=[HB] * 2,
         scratch=[

time: 72.4 us -> 70.8 us (0.978)
  waiting for transfers between devices: 14.4 us -> 12.6 us
    ppermute x20, waiting for transfers between devices: 9.77 us -> 7.34 us  [swap(): return lax.ppermute(value, axis, pairs + [(j, i) for i, j in pairs])]
    pallas_call x10 -> x11, Pallas kernels: 24.2 us -> 24.1 us  [call(): pl.pallas_call(body, out_shape=outs, in_specs=[VM] * len(args) if ins is...]
  transfers between devices with their start and end apart: 21 -> 21, of which waited for: 4 -> 4; matrix products, arithmetic and copies ran while one was open for 0% -> 0% of each run, Pallas kernels for 17% -> 20%
where the time goes in v3:
time: 70.8 us; the launch traced here: 70.6 us
  starting transfers between devices  32.8 us (46%)
  Pallas kernels  24.1 us (34%)
  waiting for transfers between devices  12.6 us (18%)
  between operations  1.04 us (1%)
    ppermute x20, starting transfers between devices, swap(): return lax.ppermute(value, axis, pairs + [(j, i) for i, j in pairs])  25.3 us
    pallas_call x11, Pallas kernels, call(): pl.pallas_call(body, out_shape=outs, in_specs=[VM] * len(args) if ins is...  24.1 us
    all_to_all x1, starting transfers between devices, local(): lax.all_to_all(out, ('gx', 'gy'), split_axis=0, concat_axis=0, tiled=True)  7.49 us
    ppermute x20, waiting for transfers between devices, swap(): return lax.ppermute(value, axis, pairs + [(j, i) for i, j in pairs])  7.34 us
    all_to_all x1, waiting for transfers between devices, local(): lax.all_to_all(out, ('gx', 'gy'), split_axis=0, concat_axis=0, tiled=True)  5.25 us
  transfers between devices with their start and end apart: 21, of which 4 were waited for; matrix products, arithmetic and copies ran while one was open for 0% of the time, Pallas kernels for 20%

profile of v3, /device:TPU:0, one launch (start us, length us, event | category | flops | bytes accessed | tf_op | source)
XLA Modules:
  0.0 70.6 jit_solution(11442379061236436420)
XLA Ops:
  0.6 1.9 %shard_map.130 = (f32[272,128]{1,0:T(8,128)S(1)}, f32[272,128]{1,0:T(8,128)S(1)}, f32[96,128]{1,0:T(8,128)S(1)}, f32[96,128]{1,0:T(8,128)S(1)}, f32[48,32,128]{2,1,0:T(8,128)S(1)}, /*index=5*/f32[768,128]{1,0:T(8,128)S(1)}) custom-call(f32[6,16,32,256]{3,2,1,0:T(8,128)} %s.1, f32[32,128]{1,0:T(8,128)} %depth.1, f32[32,128]{1,0:T(8,128)} %height_in.1, ...), custom_call_target="tpu_custom_call" | custom-call | tf_op jit(solution)/shard_map/pallas_call | solution.py:40
  2.5 0.1 collective-permute-start.4
  2.6 1.7 %collective-permute-start.2 = (f32[96,128]{1,0:T(8,128)S(1)}, f32[96,128]{1,0:T(8,128)S(1)}, u32[]{:S(2)}, u32[]{:S(2)}) collective-permute-start(f32[96,128]{1,0:T(8,128)S(1)} %get-tuple-element.69), channel_id=1, source_target_pairs={{0,2},{4,6},{8,10},{12,14},{2,0},{6,4},{10,8},{14,12},{1,3},{5,7},... | collective-permute-start | bytes 147464 | tf_op jit(solution)/shard_map/ppermute | solution.py:588
  4.3 4.7 %collective-permute-start.3 = (f32[96,128]{1,0:T(8,128)S(1)}, f32[96,128]{1,0:T(8,128)S(1)}, u32[]{:S(2)}, u32[]{:S(2)}) collective-permute-start(f32[96,128]{1,0:T(8,128)S(1)} %get-tuple-element.70), channel_id=1, source_target_pairs={{2,4},{6,8},{10,12},{14,0},{4,2},{8,6},{12,10},{0,14},{3,5},{7,9},... | collective-permute-start | bytes 147464 | tf_op jit(solution)/shard_map/ppermute | solution.py:588
  9.0 1.9 %collective-permute-start = (f32[272,128]{1,0:T(8,128)S(1)}, f32[272,128]{1,0:T(8,128)S(1)}, u32[]{:S(2)}, u32[]{:S(2)}) collective-permute-start(f32[272,128]{1,0:T(8,128)S(1)} %get-tuple-element.67), channel_id=1, source_target_pairs={{0,16},{32,48},{64,80},{96,112},{16,0},{48,32},{80,64},{112,96},{1... | collective-permute-start | bytes 417800 | tf_op jit(solution)/shard_map/ppermute | solution.py:588
  10.9 2.6 %collective-permute-start.1 = (f32[272,128]{1,0:T(8,128)S(1)}, f32[272,128]{1,0:T(8,128)S(1)}, u32[]{:S(2)}, u32[]{:S(2)}) collective-permute-start(f32[272,128]{1,0:T(8,128)S(1)} %get-tuple-element.68), channel_id=1, source_target_pairs={{16,32},{48,64},{80,96},{112,0},{32,16},{64,48},{96,80},{0,112},{1... | collective-permute-start | bytes 417800 | tf_op jit(solution)/shard_map/ppermute | solution.py:588
  13.6 3.3 %shard_map.129 = (f32[3,16,32,256]{3,2,1,0:T(8,128)S(1)}, f32[6,16,32,256]{3,2,1,0:T(8,128)S(1)}, s32[16,32,256]{2,1,0:T(8,128)S(1)}, f32[1,16,32,256]{3,2,1,0:T(8,128)S(1)}, f32[3,16,32,256]{3,2,1,0:T(8,128)S(1)}) custom-call(f32[3,16,32,256]{3,2,1,0:T(8,128)} %v_hbm.1, f32[6,16,32,256]{3,2,1,0:T(8,128)} %s.1, s32[16,32,256]{2,1,0:T(8,128)} %mat_hbm.1, ...), custom_call_target="tpu_custom_call" | custom-call | tf_op jit(solution)/shard_map/pallas_call | solution.py:40
  17.0 1.8 %collective-permute-done.1.xo = f32[272,128]{1,0:T(8,128)S(1)} collective-permute-done((f32[272,128]{1,0:T(8,128)S(1)}, f32[272,128]{1,0:T(8,128)S(1)}, u32[]{:S(2)}, u32[]{:S(2)}) %collective-permute-start.1) | collective-permute-done | bytes 139296 | tf_op jit(solution)/shard_map/ppermute | solution.py:588
  18.7 1.4 %shard_map.131 = (f32[3,16,32,256]{3,2,1,0:T(8,128)S(1)}, f32[272,128]{1,0:T(8,128)S(1)}, f32[272,128]{1,0:T(8,128)S(1)}, f32[96,128]{1,0:T(8,128)S(1)}, f32[96,...) custom-call(f32[3,16,32,256]{3,2,1,0:T(8,128)S(1)} %get-tuple-elemen, ...), custom_call_target="tpu_custom_call", output_to_operand_aliasing={{0}: (0, {}), {7}: (9, {})} | custom-call | tf_op jit(solution)/shard_map/pallas_call | solution.py:40
  20.2 0.1 collective-permute-start.9
  20.3 0.1 collective-permute-start.5
  20.4 2.2 %collective-permute-start.6 = (f32[272,128]{1,0:T(8,128)S(1)}, f32[272,128]{1,0:T(8,128)S(1)}, u32[]{:S(2)}, u32[]{:S(2)}) collective-permute-start(f32[272,128]{1,0:T(8,128)S(1)} %get-tuple-element.79), channel_id=1, source_target_pairs={{16,32},{48,64},{80,96},{112,0},{32,16},{64,48},{96,80},{0,112},{1... | collective-permute-start | bytes 417800 | tf_op jit(solution)/shard_map/ppermute | solution.py:588
  22.5 2.4 %collective-permute-start.8 = (f32[96,128]{1,0:T(8,128)S(1)}, f32[96,128]{1,0:T(8,128)S(1)}, u32[]{:S(2)}, u32[]{:S(2)}) collective-permute-start(f32[96,128]{1,0:T(8,128)S(1)} %get-tuple-element.81), channel_id=1, source_target_pairs={{2,4},{6,8},{10,12},{14,0},{4,2},{8,6},{12,10},{0,14},{3,5},{7,9},... | collective-permute-start | bytes 147464 | tf_op jit(solution)/shard_map/ppermute | solution.py:588
  25.0 2.5 %shard_map.132 = (f32[2,16,32,256]{3,2,1,0:T(8,128)S(1)}, f32[3,16,32,256]{3,2,1,0:T(8,128)S(1)}) custom-call(f32[24,128]{1,0:T(8,128)S(1)} %broadcast_bitcast_fusion.tab, s32[16,32,256]{2,1,0:T(8,128)S(1)} %get-tuple-element.75.mat, f32[3,16,32,256]{3,2,1,0:T(8,128)S(1)} %get-tuple-element.74.v), custom_call_target="tpu_custom_call" | custom-call | tf_op jit(solution)/shard_map/pallas_call | solution.py:40
  27.4 2.8 %collective-permute-done.8.yo = f32[96,128]{1,0:T(8,128)S(1)} collective-permute-done((f32[96,128]{1,0:T(8,128)S(1)}, f32[96,128]{1,0:T(8,128)S(1)}, u32[]{:S(2)}, u32[]{:S(2)}) %collective-permute-start.8) | collective-permute-done | bytes 49184 | tf_op jit(solution)/shard_map/ppermute | solution.py:588
  30.3 2.2 %shard_map.133 = (f32[6,16,32,256]{3,2,1,0:T(8,128)S(1)}, f32[272,128]{1,0:T(8,128)S(1)}, f32[272,128]{1,0:T(8,128)S(1)}, f32[96,128]{1,0:T(8,128)S(1)}, f32[96,...) custom-call(f32[6,16,32,256]{3,2,1,0:T(8,128)S(1)} %get-tuple-elemen, ...), custom_call_target="tpu_custom_call", output_to_operand_aliasing={{0}: (0, {}), {6}: (9, {})} | custom-call | tf_op jit(solution)/shard_map/pallas_call | solution.py:40
  32.5 0.1 collective-permute-start.14
  32.6 1.3 %collective-permute-start.10 = (f32[272,128]{1,0:T(8,128)S(1)}, f32[272,128]{1,0:T(8,128)S(1)}, u32[]{:S(2)}, u32[]{:S(2)}) collective-permute-start(f32[272,128]{1,0:T(8,128)S(1)} %get-tuple-element.86), channel_id=1, source_target_pairs={{0,16},{32,48},{64,80},{96,112},{16,0},{48,32},{80,64},{112,96},{1... | collective-permute-start | bytes 417800 | tf_op jit(solution)/shard_map/ppermute | solution.py:588
  33.9 1.8 %collective-permute-start.11 = (f32[272,128]{1,0:T(8,128)S(1)}, f32[272,128]{1,0:T(8,128)S(1)}, u32[]{:S(2)}, u32[]{:S(2)}) collective-permute-start(f32[272,128]{1,0:T(8,128)S(1)} %get-tuple-element.87), channel_id=1, source_target_pairs={{16,32},{48,64},{80,96},{112,0},{32,16},{64,48},{96,80},{0,112},{1... | collective-permute-start | bytes 417800 | tf_op jit(solution)/shard_map/ppermute | solution.py:588
  35.7 2.0 %collective-permute-start.13 = (f32[96,128]{1,0:T(8,128)S(1)}, f32[96,128]{1,0:T(8,128)S(1)}, u32[]{:S(2)}, u32[]{:S(2)}) collective-permute-start(f32[96,128]{1,0:T(8,128)S(1)} %get-tuple-element.89), channel_id=1, source_target_pairs={{2,4},{6,8},{10,12},{14,0},{4,2},{8,6},{12,10},{0,14},{3,5},{7,9},... | collective-permute-start | bytes 147464 | tf_op jit(solution)/shard_map/ppermute | solution.py:588
  37.6 0.8 %shard_map.134.dzs = f32[3,16,32,256]{3,2,1,0:T(8,128)S(1)} custom-call(f32[6,16,32,256]{3,2,1,0:T(8,128)S(1)} %get-tuple-element.85.src.s), custom_call_target="tpu_custom_call" | custom-call | tf_op jit(solution)/shard_map/pallas_call | solution.py:40
  38.5 2.1 %shard_map.135 = (f32[8,512]{1,0:T(8,128)S(1)}, f32[512,128]{1,0:T(8,128)S(1)}, f32[8,128]{1,0:T(8,128)S(1)}) custom-call(s32[64,1,512]{2,1,0:T(1,128)} %bitcast.10, s32[64,512]{1,0:T(8,128)} %cell_rows), custom_call_target="tpu_custom_call" | custom-call | tf_op jit(solution)/shard_map/pallas_call | solution.py:40
  40.6 2.7 %collective-permute-done.13.yo = f32[96,128]{1,0:T(8,128)S(1)} collective-permute-done((f32[96,128]{1,0:T(8,128)S(1)}, f32[96,128]{1,0:T(8,128)S(1)}, u32[]{:S(2)}, u32[]{:S(2)}) %collective-permute-start.13) | collective-permute-done | bytes 49184 | tf_op jit(solution)/shard_map/ppermute | solution.py:588
  43.4 2.0 %shard_map.136 = (f32[272,128]{1,0:T(8,128)S(1)}, f32[272,128]{1,0:T(8,128)S(1)}, f32[96,128]{1,0:T(8,128)S(1)}, f32[96,128]{1,0:T(8,128)S(1)}, f32[49,32,128]{2...) custom-call(f32[3,16,32,256]{3,2,1,0:T(8,128)S(1)} %get-tuple-element.74.v, ...), custom_call_target="tpu_custom_call" | custom-call | tf_op jit(solution)/shard_map/pallas_call | solution.py:40
  45.4 0.4 collective-permute-start.16
  45.8 2.3 %collective-permute-start.17 = (f32[272,128]{1,0:T(8,128)S(1)}, f32[272,128]{1,0:T(8,128)S(1)}, u32[]{:S(2)}, u32[]{:S(2)}) collective-permute-start(f32[272,128]{1,0:T(8,128)S(1)} %get-tuple-element.108), channel_id=1, source_target_pairs={{16,32},{48,64},{80,96},{112,0},{32,16},{64,48},{96,80},{0,112},{1... | collective-permute-start | bytes 417800 | tf_op jit(solution)/shard_map/ppermute | solution.py:588
  48.2 1.6 %collective-permute-start.19 = (f32[96,128]{1,0:T(8,128)S(1)}, f32[96,128]{1,0:T(8,128)S(1)}, u32[]{:S(2)}, u32[]{:S(2)}) collective-permute-start(f32[96,128]{1,0:T(8,128)S(1)} %get-tuple-element.110), channel_id=1, source_target_pairs={{2,4},{6,8},{10,12},{14,0},{4,2},{8,6},{12,10},{0,14},{3,5},{7,9},... | collective-permute-start | bytes 147464 | tf_op jit(solution)/shard_map/ppermute | solution.py:588
  49.7 1.0 %shard_map.138 = f32[64,128]{1,0:T(8,128)} custom-call(f32[32,128]{1,0:T(8,128)S(1)} %get-tuple-element.112.lift_here, f32[49,32,128]{2,1,0:T(8,128)S(1)} %collective-permute-done.15.zs_in.zs, f32[8,512]{1,0:T(8,128)S(1)} %get-tuple-element.113.group, f32[512,128]{1,0:T(8,128)S(1)} %get-tuple-element.114.slot, f32[8,128]{1,0:T(8,128)S(1)} %get-tuple-element.115.code), custom_call_target="tpu_custom_call" | custom-call | tf_op jit(solution)/shard_map/pallas_call | solution.py:40
  50.7 7.5 %all-to-all-start = ((f32[64,1,128]{2,1,0:T(1,128)}), f32[64,1,128]{2,1,0:T(1,128)S(1)}, u32[]{:S(2)}, u32[]{:S(2)}) async-start(f32[64,1,128]{2,1,0:T(1,128)} %bitcast.4), calls=%async_computation | async-start | bytes 65536 | tf_op jit(solution)/shard_map/all_to_all | solution.py:691
  58.2 4.2 %shard_map.137 = (f32[6,16,32,256]{3,2,1,0:T(8,128)}, f32[80,128]{1,0:T(8,128)}) custom-call(f32[6,16,32,256]{3,2,1,0:T(8,128)} %get-tuple-element.104.s_in, f32[3,16,32,256]{3,2,1,0:T(8,128)} %get-tuple-element.58.v_in, f32[2,16,32,256]{3,2,1,0:T(8,128)} %get-tuple-element.105.coef_in, f32[49,32,128]{2,1,0:T(8,128)} %copy-done, ...), custom_call_target="tpu_custom_call" | custom-call | tf_op jit(solution)/shard_map/pallas_call | solution.py:40
  62.5 5.3 %all-to-all-done = f32[64,1,128]{2,1,0:T(1,128)S(1)} async-done(((f32[64,1,128]{2,1,0:T(1,128)}), f32[64,1,128]{2,1,0:T(1,128)S(1)}, u32[]{:S(2)}, u32[]{:S(2)}) %all-to-all-start) | async-done | bytes 32800 | tf_op jit(solution)/shard_map/all_to_all | solution.py:691
  67.7 2.7 %shard_map.139 = (f32[32,128]{1,0:T(8,128)}, f32[32,128]{1,0:T(8,128)}) custom-call(f32[64,128]{1,0:T(8,128)S(1)} %bitcast.9, f32[80,128]{1,0:T(8,128)} %get-tuple-element.116.far_in, f32[768,128]{1,0:T(8,128)} %get-tuple-element.117.bag_in, f32[32,128]{1,0:T(8,128)} %height_in.1, f32[32,128]{1,0:T(8,128)} %current_in.1, s32[32,128]{1,0:T(8,128)} %wet_in.1), custom_call_target="tpu_custom_call" | custom-call | tf_op jit(solution)/shard_map/pallas_call | solution.py:40
  (30 shorter events, 0.2 us)
Async XLA Ops:
  0.6 12.9 %copy-start.1 = (f32[16,3]{0,1:T(4,128)S(1)}, f32[16,3]{0,1:T(4,128)}, u32[]{:S(2)}) copy-start(f32[16,3]{0,1:T(4,128)} %param.13) | copy-start | bytes 580
  2.5 16.2 %collective-permute-start.4 = (f32[48,32,128]{2,1,0:T(8,128)S(1)}, f32[48,32,128]{2,1,0:T(8,128)S(1)}, u32[]{:S(2)}, u32[]{:S(2)}) collective-permute-start(f32[48,32,128]{2,1,0:T(8,128)S(1)} %get-tuple-element.71), channel_id=1, source_target_pairs={{0,1},{1,0},{2,3},{3,2},{4,5},{5,4},{6,7},{7,6},{8,9},{9,8},{10,11... | collective-permute-start | bytes 2359304 | tf_op jit(solution)/shard_map/ppermute | solution.py:588
  2.6 14.3 %collective-permute-start.2 = (f32[96,128]{1,0:T(8,128)S(1)}, f32[96,128]{1,0:T(8,128)S(1)}, u32[]{:S(2)}, u32[]{:S(2)}) collective-permute-start(f32[96,128]{1,0:T(8,128)S(1)} %get-tuple-element.69), channel_id=1, source_target_pairs={{0,2},{4,6},{8,10},{12,14},{2,0},{6,4},{10,8},{14,12},{1,3},{5,7},... | collective-permute-start | bytes 147464 | tf_op jit(solution)/shard_map/ppermute | solution.py:588
  4.3 12.7 %collective-permute-start.3 = (f32[96,128]{1,0:T(8,128)S(1)}, f32[96,128]{1,0:T(8,128)S(1)}, u32[]{:S(2)}, u32[]{:S(2)}) collective-permute-start(f32[96,128]{1,0:T(8,128)S(1)} %get-tuple-element.70), channel_id=1, source_target_pairs={{2,4},{6,8},{10,12},{14,0},{4,2},{8,6},{12,10},{0,14},{3,5},{7,9},... | collective-permute-start | bytes 147464 | tf_op jit(solution)/shard_map/ppermute | solution.py:588
  9.0 8.0 %collective-permute-start = (f32[272,128]{1,0:T(8,128)S(1)}, f32[272,128]{1,0:T(8,128)S(1)}, u32[]{:S(2)}, u32[]{:S(2)}) collective-permute-start(f32[272,128]{1,0:T(8,128)S(1)} %get-tuple-element.67), channel_id=1, source_target_pairs={{0,16},{32,48},{64,80},{96,112},{16,0},{48,32},{80,64},{112,96},{1... | collective-permute-start | bytes 417800 | tf_op jit(solution)/shard_map/ppermute | solution.py:588
  10.9 7.8 %collective-permute-start.1 = (f32[272,128]{1,0:T(8,128)S(1)}, f32[272,128]{1,0:T(8,128)S(1)}, u32[]{:S(2)}, u32[]{:S(2)}) collective-permute-start(f32[272,128]{1,0:T(8,128)S(1)} %get-tuple-element.68), channel_id=1, source_target_pairs={{16,32},{48,64},{80,96},{112,0},{32,16},{64,48},{96,80},{0,112},{1... | collective-permute-start | bytes 417800 | tf_op jit(solution)/shard_map/ppermute | solution.py:588
  20.2 10.1 %collective-permute-start.9 = (f32[48,32,128]{2,1,0:T(8,128)S(1)}, f32[48,32,128]{2,1,0:T(8,128)S(1)}, u32[]{:S(2)}, u32[]{:S(2)}) collective-permute-start(f32[48,32,128]{2,1,0:T(8,128)S(1)} %get-tuple-element.82), channel_id=1, source_target_pairs={{0,1},{1,0},{2,3},{3,2},{4,5},{5,4},{6,7},{7,6},{8,9},{9,8},{10,11... | collective-permute-start | bytes 2359304 | tf_op jit(solution)/shard_map/ppermute | solution.py:588
  20.3 10.0 %collective-permute-start.5 = (f32[272,128]{1,0:T(8,128)S(1)}, f32[272,128]{1,0:T(8,128)S(1)}, u32[]{:S(2)}, u32[]{:S(2)}) collective-permute-start(f32[272,128]{1,0:T(8,128)S(1)} %get-tuple-element.78), channel_id=1, source_target_pairs={{0,16},{32,48},{64,80},{96,112},{16,0},{48,32},{80,64},{112,96},{1... | collective-permute-start | bytes 417800 | tf_op jit(solution)/shard_map/ppermute | solution.py:588
  20.4 9.9 %collective-permute-start.6 = (f32[272,128]{1,0:T(8,128)S(1)}, f32[272,128]{1,0:T(8,128)S(1)}, u32[]{:S(2)}, u32[]{:S(2)}) collective-permute-start(f32[272,128]{1,0:T(8,128)S(1)} %get-tuple-element.79), channel_id=1, source_target_pairs={{16,32},{48,64},{80,96},{112,0},{32,16},{64,48},{96,80},{0,112},{1... | collective-permute-start | bytes 417800 | tf_op jit(solution)/shard_map/ppermute | solution.py:588
  22.5 4.9 %collective-permute-start.7 = (f32[96,128]{1,0:T(8,128)S(1)}, f32[96,128]{1,0:T(8,128)S(1)}, u32[]{:S(2)}, u32[]{:S(2)}) collective-permute-start(f32[96,128]{1,0:T(8,128)S(1)} %get-tuple-element.80), channel_id=1, source_target_pairs={{0,2},{4,6},{8,10},{12,14},{2,0},{6,4},{10,8},{14,12},{1,3},{5,7},... | collective-permute-start | bytes 147464 | tf_op jit(solution)/shard_map/ppermute | solution.py:588
  22.5 7.7 %collective-permute-start.8 = (f32[96,128]{1,0:T(8,128)S(1)}, f32[96,128]{1,0:T(8,128)S(1)}, u32[]{:S(2)}, u32[]{:S(2)}) collective-permute-start(f32[96,128]{1,0:T(8,128)S(1)} %get-tuple-element.81), channel_id=1, source_target_pairs={{2,4},{6,8},{10,12},{14,0},{4,2},{8,6},{12,10},{0,14},{3,5},{7,9},... | collective-permute-start | bytes 147464 | tf_op jit(solution)/shard_map/ppermute | solution.py:588
  32.5 10.9 %collective-permute-start.14 = (f32[48,32,128]{2,1,0:T(8,128)S(1)}, f32[48,32,128]{2,1,0:T(8,128)S(1)}, u32[]{:S(2)}, u32[]{:S(2)}) collective-permute-start(f32[48,32,128]{2,1,0:T(8,128)S(1)} %get-tuple-element.90), channel_id=1, source_target_pairs={{0,1},{1,0},{2,3},{3,2},{4,5},{5,4},{6,7},{7,6},{8,9},{9,8},{10,11... | collective-permute-start | bytes 2359304 | tf_op jit(solution)/shard_map/ppermute | solution.py:588
  32.6 10.8 %collective-permute-start.10 = (f32[272,128]{1,0:T(8,128)S(1)}, f32[272,128]{1,0:T(8,128)S(1)}, u32[]{:S(2)}, u32[]{:S(2)}) collective-permute-start(f32[272,128]{1,0:T(8,128)S(1)} %get-tuple-element.86), channel_id=1, source_target_pairs={{0,16},{32,48},{64,80},{96,112},{16,0},{48,32},{80,64},{112,96},{1... | collective-permute-start | bytes 417800 | tf_op jit(solution)/shard_map/ppermute | solution.py:588
  33.9 9.5 %collective-permute-start.11 = (f32[272,128]{1,0:T(8,128)S(1)}, f32[272,128]{1,0:T(8,128)S(1)}, u32[]{:S(2)}, u32[]{:S(2)}) collective-permute-start(f32[272,128]{1,0:T(8,128)S(1)} %get-tuple-element.87), channel_id=1, source_target_pairs={{16,32},{48,64},{80,96},{112,0},{32,16},{64,48},{96,80},{0,112},{1... | collective-permute-start | bytes 417800 | tf_op jit(solution)/shard_map/ppermute | solution.py:588
  35.7 5.0 %collective-permute-start.12 = (f32[96,128]{1,0:T(8,128)S(1)}, f32[96,128]{1,0:T(8,128)S(1)}, u32[]{:S(2)}, u32[]{:S(2)}) collective-permute-start(f32[96,128]{1,0:T(8,128)S(1)} %get-tuple-element.88), channel_id=1, source_target_pairs={{0,2},{4,6},{8,10},{12,14},{2,0},{6,4},{10,8},{14,12},{1,3},{5,7},... | collective-permute-start | bytes 147464 | tf_op jit(solution)/shard_map/ppermute | solution.py:588
  35.7 7.7 %collective-permute-start.13 = (f32[96,128]{1,0:T(8,128)S(1)}, f32[96,128]{1,0:T(8,128)S(1)}, u32[]{:S(2)}, u32[]{:S(2)}) collective-permute-start(f32[96,128]{1,0:T(8,128)S(1)} %get-tuple-element.89), channel_id=1, source_target_pairs={{2,4},{6,8},{10,12},{14,0},{4,2},{8,6},{12,10},{0,14},{3,5},{7,9},... | collective-permute-start | bytes 147464 | tf_op jit(solution)/shard_map/ppermute | solution.py:588
  45.4 4.4 %collective-permute-start.15 = (f32[49,32,128]{2,1,0:T(8,128)S(1)}, f32[49,32,128]{2,1,0:T(8,128)S(1)}, u32[]{:S(2)}, u32[]{:S(2)}) collective-permute-start(f32[49,32,128]{2,1,0:T(8,128)S(1)} %get-tuple-element.106), channel_id=1, source_target_pairs={{0,1},{1,0},{2,3},{3,2},{4,5},{5,4},{6,7},{7,6},{8,9},{9,8},{10,11... | collective-permute-start | bytes 2408456 | tf_op jit(solution)/shard_map/ppermute | solution.py:588
  45.4 12.8 %collective-permute-start.16 = (f32[272,128]{1,0:T(8,128)S(1)}, f32[272,128]{1,0:T(8,128)S(1)}, u32[]{:S(2)}, u32[]{:S(2)}) collective-permute-start(f32[272,128]{1,0:T(8,128)S(1)} %get-tuple-element.107), channel_id=1, source_target_pairs={{0,16},{32,48},{64,80},{96,112},{16,0},{48,32},{80,64},{112,96},{1... | collective-permute-start | bytes 417800 | tf_op jit(solution)/shard_map/ppermute | solution.py:588
  45.8 12.4 %collective-permute-start.17 = (f32[272,128]{1,0:T(8,128)S(1)}, f32[272,128]{1,0:T(8,128)S(1)}, u32[]{:S(2)}, u32[]{:S(2)}) collective-permute-start(f32[272,128]{1,0:T(8,128)S(1)} %get-tuple-element.108), channel_id=1, source_target_pairs={{16,32},{48,64},{80,96},{112,0},{32,16},{64,48},{96,80},{0,112},{1... | collective-permute-start | bytes 417800 | tf_op jit(solution)/shard_map/ppermute | solution.py:588
  48.2 10.0 %collective-permute-start.18 = (f32[96,128]{1,0:T(8,128)S(1)}, f32[96,128]{1,0:T(8,128)S(1)}, u32[]{:S(2)}, u32[]{:S(2)}) collective-permute-start(f32[96,128]{1,0:T(8,128)S(1)} %get-tuple-element.109), channel_id=1, source_target_pairs={{0,2},{4,6},{8,10},{12,14},{2,0},{6,4},{10,8},{14,12},{1,3},{5,7},... | collective-permute-start | bytes 147464 | tf_op jit(solution)/shard_map/ppermute | solution.py:588
  48.2 10.1 %collective-permute-start.19 = (f32[96,128]{1,0:T(8,128)S(1)}, f32[96,128]{1,0:T(8,128)S(1)}, u32[]{:S(2)}, u32[]{:S(2)}) collective-permute-start(f32[96,128]{1,0:T(8,128)S(1)} %get-tuple-element.110), channel_id=1, source_target_pairs={{2,4},{6,8},{10,12},{14,0},{4,2},{8,6},{12,10},{0,14},{3,5},{7,9},... | collective-permute-start | bytes 147464 | tf_op jit(solution)/shard_map/ppermute | solution.py:588
  49.7 8.5 %copy-start = (f32[49,32,128]{2,1,0:T(8,128)}, f32[49,32,128]{2,1,0:T(8,128)S(1)}, u32[]{:S(2)}) copy-start(f32[49,32,128]{2,1,0:T(8,128)S(1)} %collective-permute-done.15.zs_in.zs) | copy-start | bytes 2408452
  50.7 17.0 %all-to-all-start = ((f32[64,1,128]{2,1,0:T(1,128)}), f32[64,1,128]{2,1,0:T(1,128)S(1)}, u32[]{:S(2)}, u32[]{:S(2)}) async-start(f32[64,1,128]{2,1,0:T(1,128)} %bitcast.4), calls=%async_computation | async-start | bytes 65536 | tf_op jit(solution)/shard_map/all_to_all | solution.py:691

commit v4 on v3

--- a/solution.py
+++ b/solution.py
@@ -57,6 +57,7 @@
 
 
 PARTS = 3
+HALF = 8
 def resident(*dims):
     return pltpu.VMEM(dims, F32)
 
@@ -140,45 +141,36 @@
 
 def factor(depth, height, wet, pxe, bag, rows):
     spread = depth[...] * depth[...] / 3.0
-    rows[0:32, :] = spread
-    w = [None] * LON
-    inv = [None] * LON
-    right = [None] * LON
-    after = jnp.zeros((1, LAT), F32)
-    link = jnp.ones((1, LAT), F32)
-    for j in reversed(range(LON)):
-        sp = rows[j : j + 1, :]
-        inv[j] = 1.0 / (1.0 + 2.0 * sp - sp * after)
-        w[j] = after = sp * inv[j]
-        right[j] = link = w[j] * link
-    left_run = jnp.ones((1, LAT), F32)
-    right_run = jnp.zeros((1, LAT), F32)
-    past = jnp.zeros((1, LAT), F32)
-    weight = [None] * LON
-    weight[LON - 1] = jnp.ones((1, LAT), F32)
-    for j in reversed(range(LON - 1)):
-        weight[j] = w[j + 1] * weight[j + 1]
-    total = jnp.zeros((1, LAT), F32)
-    p_before = q_before = jnp.zeros((1, LAT), F32)
-    for j in range(LON):
-        p_now = left_run * inv[j]
-        total = weight[j] + (w[j - 1] * total if j else 0.0)
-        q_now = inv[j] * total
-        left_run = w[j] * left_run
-        right_run = right[j] + w[j] * right_run
-        bag[FAC + j : FAC + j + 1, :] = left_run
-        bag[FAC + 32 + j : FAC + 33 + j, :] = right_run
-        bag[FAC + 64 + j : FAC + 65 + j, :] = w[j]
-        bag[FAC + 96 + j : FAC + 97 + j, :] = inv[j]
-        if j == 0:
-            first_left, first_right = left_run, right_run
-        rows[j : j + 1, :] = p_now - p_before
-        rows[32 + j : 33 + j, :] = q_now - q_before
-        p_before, q_before = p_now, q_now
+    scale = 1.0 / spread
+    rows[0:32, :] = scale
+    for base, order in ((32, reversed(range(LON))), (65, range(LON))):
+        value, slope = jnp.ones((1, LAT), F32), jnp.ones((1, LAT), F32)
+        last = base + (LON if base == 32 else 0)
+        rows[last : last + 1, :] = value
+        for j in order:
+            slope = slope + value * rows[j : j + 1, :]
+            value = value + slope
+            at = base + (j if base == 32 else j + 1)
+            rows[at : at + 1, :] = value
+    down, down_next = rows[32:64, :], rows[33:65, :]
+    up = rows[65:97, :]
+    top, end = 1.0 / rows[32:33, :], 1.0 / rows[97:98, :]
+    w = down_next / down
+    left, right = down_next * top, up * end
+    p_now, q_now = left * scale, right * scale
+    bag[FAC : FAC + 32, :] = left
+    bag[FAC + 32 : FAC + 64, :] = right
+    bag[FAC + 64 : FAC + 96, :] = w
+    bag[FAC + 96 : FAC + 128, :] = w * scale
+    row = lax.broadcasted_iota(jnp.int32, (LON, LAT), 0)
+    p_before = jnp.where(row == 0, 0.0, pltpu.roll(p_now, 1, 0))
+    q_before = jnp.where(row == 0, 0.0, pltpu.roll(q_now, 1, 0))
+    first_left, left_run = left[0:1, :], left[31:32, :]
+    first_right, right_run = right[0:1, :], right[31:32, :]
     wet_float = wet[...].astype(F32)
     high = height[...]
-    a1 = 400.0 * rows[0:32, :] * wet_float
-    a2 = 400.0 * rows[32:64, :] * wet_float
+    a1 = 400.0 * (p_now - p_before) * wet_float
+    a2 = 400.0 * (q_now - q_before) * wet_float
     pxe[XF : XF + 32, :] = a1
     pxe[XF + 32 : XF + 64, :] = a2
     base = XF + 64
@@ -188,8 +180,8 @@
     pxe[base + 3 : base + 4, :] = left_run
     pxe[base + 4 : base + 5, :] = first_right
     pxe[base + 5 : base + 6, :] = right_run
-    pxe[base + 6 : base + 7, :] = -400.0 * p_before
-    pxe[base + 7 : base + 8, :] = -400.0 * q_before
+    pxe[base + 6 : base + 7, :] = -400.0 * p_now[31:32, :]
+    pxe[base + 7 : base + 8, :] = -400.0 * q_now[31:32, :]
     pxe[base + 8 : base + 9, :] = wet_float[0:1, :]
     pxe[base + 9 : base + 10, :] = wet_float[0:1, :] * high[0:1, :]
     pxe[base + 10 : base + 16, :] = jnp.zeros((6, LAT), F32)
@@ -284,18 +276,26 @@
     lax.fori_loop(0, CX, plane, 0)
 
 
-def fetch(v_hbm, s_hbm, mat_hbm, tab, v, s, mat, coef, dzs, sems):
-    copies = [
-        pltpu.make_async_copy(a, b, sems.at[i])
-        for i, (a, b) in enumerate(((mat_hbm, mat), (s_hbm, s), (v_hbm, v)))
+def fetch(v_hbm, s_hbm, mat_hbm, owners, cell_rows, tab, v, s, mat, coef, dzs, owner, cell, sems):
+    gx, gy, _ = place()
+    wanted = [
+        (s_hbm.at[pl.ds(2, 3)], s.at[pl.ds(2, 3)]),
+        (mat_hbm, mat),
+        (s_hbm.at[pl.ds(0, 2)], s.at[pl.ds(0, 2)]),
+        (s_hbm.at[5], s.at[5]),
+        (v_hbm, v),
+        (owners.at[gx * NB + gy], owner),
+        (cell_rows.at[pl.ds(pl.multiple_of(gx * NB, 8), 8), :], cell),
     ]
+    copies = [pltpu.make_async_copy(a, b, sems.at[i]) for i, (a, b) in enumerate(wanted)]
     for copy in copies:
         copy.start()
     copies[0].wait()
+    slopes_z(s, dzs, SZ)
+    copies[1].wait()
     lookup(tab, mat, coef, (0,))
-    copies[1].wait()
-    slopes_z(s, dzs, SZ)
-    copies[2].wait()
+    for copy in copies[2:]:
+        copy.wait()
 
 
 def lame(tab, mat, v, coef, dzs):
@@ -323,8 +323,7 @@
     sub, lane = iotas()
     collect(distance, xe, xo, bag)
     if has_lift:
-        for copy in copies:
-            copy.start()
+        copies[0].start()
     dx, dy, dz = differences(s, (SX, SY, SZ), dzs, xe, xo, ye, yo, zs)
     lift = [lift_in[t * 8 : t * 8 + 8, :] if has_lift else jnp.zeros((8, 128), F32) for t in range(4)]
     for x in range(CX):
@@ -356,9 +355,8 @@
             copy.wait()
 
 
-def strain(distance, s, v, coef, dzs, xe, xo, ye, yo, zs, bag_in, so, pxe, pxo, pye, pyo, pz, bag, s_hbm, coef_hbm, sems):
-    copies = [pltpu.make_async_copy(coef, coef_hbm, sems.at[CX])]
-    copies[0].start()
+def strain(distance, s, v, coef, dzs, xe, xo, ye, yo, zs, bag_in, so, pxe, pxo, pye, pyo, pz, bag, s_hbm, sems):
+    copies = []
     collect(distance, xe, xo, bag)
     gz, flip = lax.axis_index("gz"), odd("gy")
 
@@ -366,8 +364,9 @@
         for i in range(3):
             put_y(flip, x, i, new[SY[i]], pye, pyo)
             put_z(gz, x, i, new[SZ[i]], pz)
-        copies.append(pltpu.make_async_copy(so.at[:, x], s_hbm.at[:, x], sems.at[x]))
-        copies[-1].start()
+        if x < HALF:
+            copies.append(pltpu.make_async_copy(so.at[:, x], s_hbm.at[:, x], sems.at[x]))
+            copies[-1].start()
 
     stretch(s, v, coef, dzs, xe, xo, ye, yo, zs, so, done)
     put_x_faces(so, SX, pxe, pxo)
@@ -377,7 +376,7 @@
         copy.wait()
 
 
-def finish(s_in, v_in, coef_in, zs_in, xe, xo, ye, yo, s_hbm, far_hbm, s, v, coef, zs, dzs, sems):
+def finish(s_low, s_high, v_in, coef_in, zs_in, xe, xo, ye, yo, s_hbm, far_hbm, s, v, coef, zs, dzs, sems):
     early = [
         pltpu.make_async_copy(v_in, v, sems.at[0]),
         pltpu.make_async_copy(zs_in, zs, sems.at[1]),
@@ -385,8 +384,8 @@
         pltpu.make_async_copy(xe.at[pl.ds(XF, OCR), :], far_hbm, sems.at[3]),
     ]
     parts = [
-        pltpu.make_async_copy(s_in.at[:, pl.ds(i * 4, 4)], s.at[:, pl.ds(i * 4, 4)], sems.at[4 + i])
-        for i in range(4)
+        pltpu.make_async_copy(ref.at[:, pl.ds(at, 4)], s.at[:, pl.ds(i * 4, 4)], sems.at[4 + i])
+        for i, (ref, at) in enumerate(((s_low, 0), (s_low, 4), (s_high, 0), (s_high, 4)))
     ]
     for copy in early + parts:
         copy.start()
@@ -444,16 +443,14 @@
     return jnp.concatenate(parts, axis=0)
 
 
-def address(owners, cell_rows, group, slot, code, owner, cell, sems):
+def address(owner, cell, coef, s, group, slot, code, coef_hbm, s_hbm, sems):
     gx, gy, gz = place()
     copies = [
-        pltpu.make_async_copy(owners.at[gx * NB + gy], owner, sems.at[0]),
-        pltpu.make_async_copy(cell_rows.at[pl.ds(pl.multiple_of(gx * NB, 8), 8), :], cell, sems.at[1]),
+        pltpu.make_async_copy(s.at[:, pl.ds(HALF, CX - HALF)], s_hbm, sems.at[0]),
+        pltpu.make_async_copy(coef, coef_hbm, sems.at[1]),
     ]
     for copy in copies:
         copy.start()
-    for copy in copies:
-        copy.wait()
     sub = lax.broadcasted_iota(jnp.int32, (128, 128), 0)
     lane = lax.broadcasted_iota(jnp.int32, (128, 128), 1)
     own = owner[...]
@@ -475,6 +472,8 @@
     group[...] = chosen
     found = jnp.dot(chosen, taken * cells, precision=HIGH, preferred_element_type=F32)
     code[...] = pltpu.roll(found, 64, 1)
+    for copy in copies:
+        copy.wait()
 
 
 def pack_lift(lift_here, zs, group, slot, code, out, wide):
@@ -510,19 +509,24 @@
     value = jnp.where(half, one, pltpu.roll(two, 64, 1))
     cell = jnp.where(half, pltpu.roll(one, 64, 1), two).astype(jnp.int32) - 1
     band = (lane & 63) >> 3
-    pair[0:32, :] = jnp.where(cell >= 0, band * 32 + (cell >> 7), -1)
-    pair[32:64, :] = cell & 127
+    pair[0:32, :] = jnp.where(cell >= 0, band * 32 + (cell >> 7), -1).astype(F32)
+    pair[32:64, :] = (cell & 127).astype(F32)
     coarse = value.astype(b16).astype(F32)
     val[0:32, :] = coarse
     val[32:64, :] = value - coarse
-    lon_rows = lax.broadcasted_iota(jnp.int32, (256, 128), 0)
-    lat_rows = lax.broadcasted_iota(jnp.int32, (128, 128), 0)
+    lon_rows = lax.broadcasted_iota(jnp.int32, (256, 128), 0).astype(F32).astype(b16)
+    lat_rows = lon_rows[0:128, :]
+    one16, zero16 = jnp.ones((), b16), jnp.zeros((), b16)
+
+    def line(ref, r, rows):
+        return jnp.broadcast_to(jnp.broadcast_to(ref[r : r + 1, :], (16, 128)).astype(b16)[0:1, :], (rows, 128))
+
     for r in range(32):
         cols = slice(r * 128, r * 128 + 128)
-        hot[0:256, cols] = (lon_rows == pair[r : r + 1, :]).astype(F32).astype(b16)
-        here = lat_rows == pair[32 + r : 33 + r, :]
-        hot[256:384, cols] = jnp.where(here, val[r : r + 1, :], 0.0).astype(b16)
-        hot[384:512, cols] = jnp.where(here, val[32 + r : 33 + r, :], 0.0).astype(b16)
+        hot[0:256, cols] = jnp.where(lon_rows == line(pair, r, 256), one16, zero16)
+        here = lat_rows == line(pair, 32 + r, 128)
+        hot[256:384, cols] = jnp.where(here, line(val, r, 128), zero16)
+        hot[384:512, cols] = jnp.where(here, line(val, 32 + r, 128), zero16)
     both = lax.dot_general(
         hot[0:256, :], hot[256:512, :], (((1,), (1,)), ((), ())), preferred_element_type=F32
     )
@@ -610,7 +614,7 @@
         *outside(stress, sea_depth, height, wet_mask),
         ins=[HB] * 4,
         scratch=[
-            pltpu.VMEM((64, LAT), F32),
+            pltpu.VMEM((104, LAT), F32),
             pltpu.VMEM((LON, LAT), F32),
             pltpu.VMEM((LON, LAT), F32),
             pltpu.VMEM((LON, LAT), jnp.int32),
@@ -619,12 +623,15 @@
         ],
     )
     r1 = exchange(sent)
-    velocity, stress, mat, coef, dzs = call(
+    velocity, stress, mat, coef, dzs, owner, cell = call(
         fetch,
-        [v_shape, s_shape, pltpu.VMEM((CX, CY, CZ), jnp.int32), resident(1, CX, CY, CZ), v_shape],
-        *outside(velocity, stress, material), tab,
-        ins=[HB] * 3 + [VM],
-        scratch=[pltpu.SemaphoreType.DMA((3,))],
+        [
+            v_shape, s_shape, pltpu.VMEM((CX, CY, CZ), jnp.int32), resident(1, CX, CY, CZ), v_shape,
+            pltpu.VMEM((1, 512), jnp.int32), pltpu.VMEM((8, 512), jnp.int32),
+        ],
+        *outside(velocity, stress, material, owner_map.reshape(64, 1, 512), cell_map), tab,
+        ins=[HB] * 5 + [VM],
+        scratch=[pltpu.SemaphoreType.DMA((7,))],
     )
     v1, *sent, lift, bag = call(
         functools.partial(move, 1, False),
@@ -635,33 +642,28 @@
     r2 = exchange(sent)
     mat, v1 = lax.optimization_barrier((mat, v1))
     coef2, dzs = call(lame, [resident(2, CX, CY, CZ), v_shape], tab, mat, v1)
-    s1, *sent, bag, s_copy, coef_copy = call(
+    s1, *sent, bag, s_low = call(
         functools.partial(strain, 2),
-        [s_shape] + PAYLOAD + [pz_shape, bag_shape] + [pltpu.HBM(dims, F32) for dims in ((6, CX, CY, CZ), (2, CX, CY, CZ))],
+        [s_shape] + PAYLOAD + [pz_shape, bag_shape] + [pltpu.HBM((6, HALF, CY, CZ), F32)],
         stress, v1, coef2, dzs, *r2, bag,
-        outs_at=[VM] * 7 + [HB] * 2,
-        scratch=[pltpu.SemaphoreType.DMA((CX + 1,))], aliases={0: 0, 9: 6},
+        outs_at=[VM] * 7 + [HB],
+        scratch=[pltpu.SemaphoreType.DMA((HALF,))], aliases={0: 0, 9: 6},
     )
     r3 = exchange(sent)
-    owners, cells, s1 = lax.optimization_barrier((owner_map.reshape(64, 1, 512), cell_map, s1))
-    group, slot, code = call(
+    owner, cell, s1 = lax.optimization_barrier((owner, cell, s1))
+    group, slot, code, coef_copy, s_high = call(
         address,
-        [shape(8, 512), shape(512, 128), shape(8, 128)],
-        *outside(owners, cells),
-        ins=[HB] * 2,
-        scratch=[
-            pltpu.VMEM((1, 512), jnp.int32),
-            pltpu.VMEM((8, 512), jnp.int32),
-            pltpu.SemaphoreType.DMA((2,)),
-        ],
+        [shape(8, 512), shape(512, 128), shape(8, 128)]
+        + [pltpu.HBM((2, CX, CY, CZ), F32), pltpu.HBM((6, CX - HALF, CY, CZ), F32)],
+        owner, cell, coef2, s1,
+        outs_at=[VM] * 3 + [HB] * 2,
+        scratch=[pltpu.SemaphoreType.DMA((2,))],
     )
     (dzs,) = call(functools.partial(slopes_z, comps=SZ), [v_shape], s1)
-    r3, group, slot, code = lax.optimization_barrier((r3, group, slot, code))
+    r3, group, slot, code, coef_copy, s_high = lax.optimization_barrier((r3, group, slot, code, coef_copy, s_high))
     *sent, lift, v_out, bag = call(
         functools.partial(move, 3, True),
-        PAYLOAD
-        + [pz_lift, shape(32, 128)]
-        + [pltpu.HBM(dims, F32) for dims in ((3, CX, CY, CZ), (BAG, 128))],
+        PAYLOAD + [pz_lift, shape(32, 128)] + [pltpu.HBM(dims, F32) for dims in ((3, CX, CY, CZ), (BAG, 128))],
         v1, s1, coef, dzs, *r3, bag, lift,
         outs_at=[VM] * 6 + [HB] * 2,
         scratch=[plane_z, pltpu.VMEM((BAG, 128), F32), pltpu.SemaphoreType.DMA((CX + 1,))],
@@ -676,8 +678,8 @@
     s2, far = call(
         finish,
         [pltpu.HBM(dims, F32) for dims in ((6, CX, CY, CZ), (OCR, 128))],
-        *outside(s_copy, v_out, coef_copy, zs), *r4,
-        ins=[HB] * 4 + [VM] * 4,
+        *outside(s_low, s_high, v_out, coef_copy, zs), *r4,
+        ins=[HB] * 5 + [VM] * 4,
         outs_at=[HB] * 2,
         scratch=[
             pltpu.VMEM((6, CX, CY, CZ), F32),
@@ -699,7 +701,7 @@
             block, block, pltpu.VMEM((LON, LAT), jnp.int32),
             pltpu.VMEM((512, 4096), jnp.bfloat16),
             pltpu.VMEM((64, 128), F32),
-            pltpu.VMEM((64, 128), jnp.int32),
+            pltpu.VMEM((64, 128), F32),
             pltpu.VMEM((256, 128), F32),
             pltpu.VMEM((32, 128), F32),
             pltpu.VMEM((72, 128), F32),

time: 70.8 us -> 69.4 us (0.980)
  waiting for transfers between devices: 12.6 us -> 11.8 us
    ppermute x20, waiting for transfers between devices: 7.34 us -> 6.54 us  [swap(): return lax.ppermute(value, axis, pairs + [(j, i) for i, j in pairs])]
  transfers between devices with their start and end apart: 21 -> 21, of which waited for: 4 -> 4; matrix products, arithmetic and copies ran while one was open for 0% -> 0% of each run, Pallas kernels for 20% -> 21%
where the time goes in v4:
time: 69.4 us; the launch traced here: 69.2 us
  starting transfers between devices  32.6 us (47%)
  Pallas kernels  23.7 us (34%)
  waiting for transfers between devices  11.8 us (17%)
  between operations  1.04 us (1%)
    ppermute x20, starting transfers between devices, swap(): return lax.ppermute(value, axis, pairs + [(j, i) for i, j in pairs])  25.7 us
    pallas_call x11, Pallas kernels, call(): pl.pallas_call(body, out_shape=outs, in_specs=[VM] * len(args) if ins is...  23.7 us
    all_to_all x1, starting transfers between devices, local(): lax.all_to_all(out, ('gx', 'gy'), split_axis=0, concat_axis=0, tiled=True)  6.96 us
    ppermute x20, waiting for transfers between devices, swap(): return lax.ppermute(value, axis, pairs + [(j, i) for i, j in pairs])  6.54 us
    all_to_all x1, waiting for transfers between devices, local(): lax.all_to_all(out, ('gx', 'gy'), split_axis=0, concat_axis=0, tiled=True)  5.26 us
  transfers between devices with their start and end apart: 21, of which 4 were waited for; matrix products, arithmetic and copies ran while one was open for 0% of the time, Pallas kernels for 21%

profile of v4, /device:TPU:0, one launch (start us, length us, event | category | flops | bytes accessed | tf_op | source)
XLA Modules:
  0.0 69.2 jit_solution(10632609491404505008)
XLA Ops:
  0.6 1.9 %shard_map.130 = (f32[272,128]{1,0:T(8,128)S(1)}, f32[272,128]{1,0:T(8,128)S(1)}, f32[96,128]{1,0:T(8,128)S(1)}, f32[96,128]{1,0:T(8,128)S(1)}, f32[48,32,128]{2,1,0:T(8,128)S(1)}, /*index=5*/f32[768,128]{1,0:T(8,128)S(1)}) custom-call(f32[6,16,32,256]{3,2,1,0:T(8,128)} %s.1, f32[32,128]{1,0:T(8,128)} %depth.1, f32[32,128]{1,0:T(8,128)} %height_in.1, ...), custom_call_target="tpu_custom_call" | custom-call | tf_op jit(solution)/shard_map/pallas_call | solution.py:40
  2.5 0.1 collective-permute-start.4
  2.6 1.7 %collective-permute-start.2 = (f32[96,128]{1,0:T(8,128)S(1)}, f32[96,128]{1,0:T(8,128)S(1)}, u32[]{:S(2)}, u32[]{:S(2)}) collective-permute-start(f32[96,128]{1,0:T(8,128)S(1)} %get-tuple-element.74), channel_id=1, source_target_pairs={{0,2},{4,6},{8,10},{12,14},{2,0},{6,4},{10,8},{14,12},{1,3},{5,7},... | collective-permute-start | bytes 147464 | tf_op jit(solution)/shard_map/ppermute | solution.py:592
  4.3 4.7 %collective-permute-start.3 = (f32[96,128]{1,0:T(8,128)S(1)}, f32[96,128]{1,0:T(8,128)S(1)}, u32[]{:S(2)}, u32[]{:S(2)}) collective-permute-start(f32[96,128]{1,0:T(8,128)S(1)} %get-tuple-element.75), channel_id=1, source_target_pairs={{2,4},{6,8},{10,12},{14,0},{4,2},{8,6},{12,10},{0,14},{3,5},{7,9},... | collective-permute-start | bytes 147464 | tf_op jit(solution)/shard_map/ppermute | solution.py:592
  9.0 1.9 %collective-permute-start = (f32[272,128]{1,0:T(8,128)S(1)}, f32[272,128]{1,0:T(8,128)S(1)}, u32[]{:S(2)}, u32[]{:S(2)}) collective-permute-start(f32[272,128]{1,0:T(8,128)S(1)} %get-tuple-element.72), channel_id=1, source_target_pairs={{0,16},{32,48},{64,80},{96,112},{16,0},{48,32},{80,64},{112,96},{1... | collective-permute-start | bytes 417800 | tf_op jit(solution)/shard_map/ppermute | solution.py:592
  10.9 2.6 %collective-permute-start.1 = (f32[272,128]{1,0:T(8,128)S(1)}, f32[272,128]{1,0:T(8,128)S(1)}, u32[]{:S(2)}, u32[]{:S(2)}) collective-permute-start(f32[272,128]{1,0:T(8,128)S(1)} %get-tuple-element.73), channel_id=1, source_target_pairs={{16,32},{48,64},{80,96},{112,0},{32,16},{64,48},{96,80},{0,112},{1... | collective-permute-start | bytes 417800 | tf_op jit(solution)/shard_map/ppermute | solution.py:592
  13.6 3.7 %shard_map.129 = (f32[3,16,32,256]{3,2,1,0:T(8,128)S(1)}, f32[6,16,32,256]{3,2,1,0:T(8,128)S(1)}, s32[16,32,256]{2,1,0:T(8,128)S(1)}, f32[1,16,32,256]{3,2,1,0:T...) custom-call(f32[3,16,32,256]{3,2,1,0:T(8,128)} %v_hbm.1, ...), custom_call_target="tpu_custom_call" | custom-call | tf_op jit(solution)/shard_map/pallas_call | solution.py:40
  17.4 1.3 %collective-permute-done.1.xo = f32[272,128]{1,0:T(8,128)S(1)} collective-permute-done((f32[272,128]{1,0:T(8,128)S(1)}, f32[272,128]{1,0:T(8,128)S(1)}, u32[]{:S(2)}, u32[]{:S(2)}) %collective-permute-start.1) | collective-permute-done | bytes 139296 | tf_op jit(solution)/shard_map/ppermute | solution.py:592
  18.7 1.4 %shard_map.131 = (f32[3,16,32,256]{3,2,1,0:T(8,128)S(1)}, f32[272,128]{1,0:T(8,128)S(1)}, f32[272,128]{1,0:T(8,128)S(1)}, f32[96,128]{1,0:T(8,128)S(1)}, f32[96,...) custom-call(f32[3,16,32,256]{3,2,1,0:T(8,128)S(1)} %get-tuple-elemen, ...), custom_call_target="tpu_custom_call", output_to_operand_aliasing={{0}: (0, {}), {7}: (9, {})} | custom-call | tf_op jit(solution)/shard_map/pallas_call | solution.py:40
  20.2 0.1 collective-permute-start.9
  20.3 0.1 collective-permute-start.5
  20.4 2.2 %collective-permute-start.6 = (f32[272,128]{1,0:T(8,128)S(1)}, f32[272,128]{1,0:T(8,128)S(1)}, u32[]{:S(2)}, u32[]{:S(2)}) collective-permute-start(f32[272,128]{1,0:T(8,128)S(1)} %get-tuple-element.86), channel_id=1, source_target_pairs={{16,32},{48,64},{80,96},{112,0},{32,16},{64,48},{96,80},{0,112},{1... | collective-permute-start | bytes 417800 | tf_op jit(solution)/shard_map/ppermute | solution.py:592
  22.5 2.4 %collective-permute-start.8 = (f32[96,128]{1,0:T(8,128)S(1)}, f32[96,128]{1,0:T(8,128)S(1)}, u32[]{:S(2)}, u32[]{:S(2)}) collective-permute-start(f32[96,128]{1,0:T(8,128)S(1)} %get-tuple-element.88), channel_id=1, source_target_pairs={{2,4},{6,8},{10,12},{14,0},{4,2},{8,6},{12,10},{0,14},{3,5},{7,9},... | collective-permute-start | bytes 147464 | tf_op jit(solution)/shard_map/ppermute | solution.py:592
  25.0 2.5 %shard_map.132 = (f32[2,16,32,256]{3,2,1,0:T(8,128)S(1)}, f32[3,16,32,256]{3,2,1,0:T(8,128)S(1)}) custom-call(f32[24,128]{1,0:T(8,128)S(1)} %broadcast_bitcast_fusion.tab, s32[16,32,256]{2,1,0:T(8,128)S(1)} %get-tuple-element.82.mat, f32[3,16,32,256]{3,2,1,0:T(8,128)S(1)} %get-tuple-element.79.v), custom_call_target="tpu_custom_call" | custom-call | tf_op jit(solution)/shard_map/pallas_call | solution.py:40
  27.5 2.8 %collective-permute-done.8.yo = f32[96,128]{1,0:T(8,128)S(1)} collective-permute-done((f32[96,128]{1,0:T(8,128)S(1)}, f32[96,128]{1,0:T(8,128)S(1)}, u32[]{:S(2)}, u32[]{:S(2)}) %collective-permute-start.8) | collective-permute-done | bytes 49184 | tf_op jit(solution)/shard_map/ppermute | solution.py:592
  30.3 1.5 %shard_map.133 = (f32[6,16,32,256]{3,2,1,0:T(8,128)S(1)}, f32[272,128]{1,0:T(8,128)S(1)}, f32[272,128]{1,0:T(8,128)S(1)}, f32[96,128]{1,0:T(8,128)S(1)}, f32[96,...) custom-call(f32[6,16,32,256]{3,2,1,0:T(8,128)S(1)} %get-tuple-elemen, ...), custom_call_target="tpu_custom_call", output_to_operand_aliasing={{0}: (0, {}), {6}: (9, {})} | custom-call | tf_op jit(solution)/shard_map/pallas_call | solution.py:40
  31.8 0.1 collective-permute-start.14
  31.9 1.3 %collective-permute-start.10 = (f32[272,128]{1,0:T(8,128)S(1)}, f32[272,128]{1,0:T(8,128)S(1)}, u32[]{:S(2)}, u32[]{:S(2)}) collective-permute-start(f32[272,128]{1,0:T(8,128)S(1)} %get-tuple-element.93), channel_id=1, source_target_pairs={{0,16},{32,48},{64,80},{96,112},{16,0},{48,32},{80,64},{112,96},{1... | collective-permute-start | bytes 417800 | tf_op jit(solution)/shard_map/ppermute | solution.py:592
  33.2 1.8 %collective-permute-start.11 = (f32[272,128]{1,0:T(8,128)S(1)}, f32[272,128]{1,0:T(8,128)S(1)}, u32[]{:S(2)}, u32[]{:S(2)}) collective-permute-start(f32[272,128]{1,0:T(8,128)S(1)} %get-tuple-element.94), channel_id=1, source_target_pairs={{16,32},{48,64},{80,96},{112,0},{32,16},{64,48},{96,80},{0,112},{1... | collective-permute-start | bytes 417800 | tf_op jit(solution)/shard_map/ppermute | solution.py:592
  35.0 2.0 %collective-permute-start.13 = (f32[96,128]{1,0:T(8,128)S(1)}, f32[96,128]{1,0:T(8,128)S(1)}, u32[]{:S(2)}, u32[]{:S(2)}) collective-permute-start(f32[96,128]{1,0:T(8,128)S(1)} %get-tuple-element.96), channel_id=1, source_target_pairs={{2,4},{6,8},{10,12},{14,0},{4,2},{8,6},{12,10},{0,14},{3,5},{7,9},... | collective-permute-start | bytes 147464 | tf_op jit(solution)/shard_map/ppermute | solution.py:592
  36.9 0.8 %shard_map.134.dzs = f32[3,16,32,256]{3,2,1,0:T(8,128)S(1)} custom-call(f32[6,16,32,256]{3,2,1,0:T(8,128)S(1)} %get-tuple-element.92.src.s), custom_call_target="tpu_custom_call" | custom-call | tf_op jit(solution)/shard_map/pallas_call | solution.py:40
  37.8 2.5 %shard_map.135 = (f32[8,512]{1,0:T(8,128)S(1)}, f32[512,128]{1,0:T(8,128)S(1)}, f32[8,128]{1,0:T(8,128)S(1)}, f32[2,16,32,256]{3,2,1,0:T(8,128)}, f32[6,8,32,256]{3,2,1,0:T(8,128)}) custom-call(s32[1,512]{1,0:T(1,128)S(1)} %get-tuple-element.98.owner, s32[8,512]{1,0:T(8,128)S(1)} %get-tuple-element.99.cell, f32[2,16,32,256]{3,2,1,0:T(8,128)S(1)} %get-tuple-element.83.coef, ...), custom_call_target="tpu_custom_call" | custom-call | tf_op jit(solution)/shard_map/pallas_call | solution.py:40
  40.3 2.4 %collective-permute-done.13.yo = f32[96,128]{1,0:T(8,128)S(1)} collective-permute-done((f32[96,128]{1,0:T(8,128)S(1)}, f32[96,128]{1,0:T(8,128)S(1)}, u32[]{:S(2)}, u32[]{:S(2)}) %collective-permute-start.13) | collective-permute-done | bytes 49184 | tf_op jit(solution)/shard_map/ppermute | solution.py:592
  42.7 2.0 %shard_map.136 = (f32[272,128]{1,0:T(8,128)S(1)}, f32[272,128]{1,0:T(8,128)S(1)}, f32[96,128]{1,0:T(8,128)S(1)}, f32[96,128]{1,0:T(8,128)S(1)}, f32[49,32,128]{2...) custom-call(f32[3,16,32,256]{3,2,1,0:T(8,128)S(1)} %get-tuple-element.79.v, ...), custom_call_target="tpu_custom_call" | custom-call | tf_op jit(solution)/shard_map/pallas_call | solution.py:40
  44.8 0.2 collective-permute-start.16
  44.9 2.5 %collective-permute-start.17 = (f32[272,128]{1,0:T(8,128)S(1)}, f32[272,128]{1,0:T(8,128)S(1)}, u32[]{:S(2)}, u32[]{:S(2)}) collective-permute-start(f32[272,128]{1,0:T(8,128)S(1)} %get-tuple-element.118), channel_id=1, source_target_pairs={{16,32},{48,64},{80,96},{112,0},{32,16},{64,48},{96,80},{0,112},{1... | collective-permute-start | bytes 417800 | tf_op jit(solution)/shard_map/ppermute | solution.py:592
  47.5 1.9 %collective-permute-start.19 = (f32[96,128]{1,0:T(8,128)S(1)}, f32[96,128]{1,0:T(8,128)S(1)}, u32[]{:S(2)}, u32[]{:S(2)}) collective-permute-start(f32[96,128]{1,0:T(8,128)S(1)} %get-tuple-element.120), channel_id=1, source_target_pairs={{2,4},{6,8},{10,12},{14,0},{4,2},{8,6},{12,10},{0,14},{3,5},{7,9},... | collective-permute-start | bytes 147464 | tf_op jit(solution)/shard_map/ppermute | solution.py:592
  49.4 1.0 %shard_map.138 = f32[64,128]{1,0:T(8,128)} custom-call(f32[32,128]{1,0:T(8,128)S(1)} %get-tuple-element.122.lift_here, f32[49,32,128]{2,1,0:T(8,128)S(1)} %collective-permute-done.15.zs_in.zs, f32[8,512]{1,0:T(8,128)S(1)} %get-tuple-element.123.group, f32[512,128]{1,0:T(8,128)S(1)} %get-tuple-element.124.slot, f32[8,128]{1,0:T(8,128)S(1)} %get-tuple-element.125.code), custom_call_target="tpu_custom_call" | custom-call | tf_op jit(solution)/shard_map/pallas_call | solution.py:40
  50.4 7.0 %all-to-all-start = ((f32[64,1,128]{2,1,0:T(1,128)}), f32[64,1,128]{2,1,0:T(1,128)S(1)}, u32[]{:S(2)}, u32[]{:S(2)}) async-start(f32[64,1,128]{2,1,0:T(1,128)} %bitcast.4), calls=%async_computation | async-start | bytes 65536 | tf_op jit(solution)/shard_map/all_to_all | solution.py:693
  57.4 4.2 %shard_map.137 = (f32[6,16,32,256]{3,2,1,0:T(8,128)}, f32[80,128]{1,0:T(8,128)}) custom-call(f32[6,8,32,256]{3,2,1,0:T(8,128)} %get-tuple-element.113.s_low, f32[6,8,32,256]{3,2,1,0:T(8,128)} %get-tuple-element.114.s_high, f32[3,16,32,256]{3,2,1,0:T(8,128)} %get-tuple-element.63.v_in, f32[2,16,32,256]{3,2,1,0:T(8,128)} %get-tuple-element.115.coef_in, ...), custom_call_target="tpu_custom_call" | custom-call | tf_op jit(solution)/shard_map/pallas_call | solution.py:40
  61.6 5.3 %all-to-all-done = f32[64,1,128]{2,1,0:T(1,128)S(1)} async-done(((f32[64,1,128]{2,1,0:T(1,128)}), f32[64,1,128]{2,1,0:T(1,128)S(1)}, u32[]{:S(2)}, u32[]{:S(2)}) %all-to-all-start) | async-done | bytes 32800 | tf_op jit(solution)/shard_map/all_to_all | solution.py:693
  66.9 2.2 %shard_map.139 = (f32[32,128]{1,0:T(8,128)}, f32[32,128]{1,0:T(8,128)}) custom-call(f32[64,128]{1,0:T(8,128)S(1)} %bitcast.9, f32[80,128]{1,0:T(8,128)} %get-tuple-element.126.far_in, f32[768,128]{1,0:T(8,128)} %get-tuple-element.127.bag_in, f32[32,128]{1,0:T(8,128)} %height_in.1, f32[32,128]{1,0:T(8,128)} %current_in.1, s32[32,128]{1,0:T(8,128)} %wet_in.1), custom_call_target="tpu_custom_call" | custom-call | tf_op jit(solution)/shard_map/pallas_call | solution.py:40
  (30 shorter events, 0.2 us)
Async XLA Ops:
  0.6 12.9 %copy-start.1 = (f32[16,3]{0,1:T(4,128)S(1)}, f32[16,3]{0,1:T(4,128)}, u32[]{:S(2)}) copy-start(f32[16,3]{0,1:T(4,128)} %param.13) | copy-start | bytes 580
  2.5 16.2 %collective-permute-start.4 = (f32[48,32,128]{2,1,0:T(8,128)S(1)}, f32[48,32,128]{2,1,0:T(8,128)S(1)}, u32[]{:S(2)}, u32[]{:S(2)}) collective-permute-start(f32[48,32,128]{2,1,0:T(8,128)S(1)} %get-tuple-element.76), channel_id=1, source_target_pairs={{0,1},{1,0},{2,3},{3,2},{4,5},{5,4},{6,7},{7,6},{8,9},{9,8},{10,11... | collective-permute-start | bytes 2359304 | tf_op jit(solution)/shard_map/ppermute | solution.py:592
  2.6 14.7 %collective-permute-start.2 = (f32[96,128]{1,0:T(8,128)S(1)}, f32[96,128]{1,0:T(8,128)S(1)}, u32[]{:S(2)}, u32[]{:S(2)}) collective-permute-start(f32[96,128]{1,0:T(8,128)S(1)} %get-tuple-element.74), channel_id=1, source_target_pairs={{0,2},{4,6},{8,10},{12,14},{2,0},{6,4},{10,8},{14,12},{1,3},{5,7},... | collective-permute-start | bytes 147464 | tf_op jit(solution)/shard_map/ppermute | solution.py:592
  4.3 13.1 %collective-permute-start.3 = (f32[96,128]{1,0:T(8,128)S(1)}, f32[96,128]{1,0:T(8,128)S(1)}, u32[]{:S(2)}, u32[]{:S(2)}) collective-permute-start(f32[96,128]{1,0:T(8,128)S(1)} %get-tuple-element.75), channel_id=1, source_target_pairs={{2,4},{6,8},{10,12},{14,0},{4,2},{8,6},{12,10},{0,14},{3,5},{7,9},... | collective-permute-start | bytes 147464 | tf_op jit(solution)/shard_map/ppermute | solution.py:592
  9.0 8.4 %collective-permute-start = (f32[272,128]{1,0:T(8,128)S(1)}, f32[272,128]{1,0:T(8,128)S(1)}, u32[]{:S(2)}, u32[]{:S(2)}) collective-permute-start(f32[272,128]{1,0:T(8,128)S(1)} %get-tuple-element.72), channel_id=1, source_target_pairs={{0,16},{32,48},{64,80},{96,112},{16,0},{48,32},{80,64},{112,96},{1... | collective-permute-start | bytes 417800 | tf_op jit(solution)/shard_map/ppermute | solution.py:592
  10.9 7.8 %collective-permute-start.1 = (f32[272,128]{1,0:T(8,128)S(1)}, f32[272,128]{1,0:T(8,128)S(1)}, u32[]{:S(2)}, u32[]{:S(2)}) collective-permute-start(f32[272,128]{1,0:T(8,128)S(1)} %get-tuple-element.73), channel_id=1, source_target_pairs={{16,32},{48,64},{80,96},{112,0},{32,16},{64,48},{96,80},{0,112},{1... | collective-permute-start | bytes 417800 | tf_op jit(solution)/shard_map/ppermute | solution.py:592
  20.2 10.1 %collective-permute-start.9 = (f32[48,32,128]{2,1,0:T(8,128)S(1)}, f32[48,32,128]{2,1,0:T(8,128)S(1)}, u32[]{:S(2)}, u32[]{:S(2)}) collective-permute-start(f32[48,32,128]{2,1,0:T(8,128)S(1)} %get-tuple-element.89), channel_id=1, source_target_pairs={{0,1},{1,0},{2,3},{3,2},{4,5},{5,4},{6,7},{7,6},{8,9},{9,8},{10,11... | collective-permute-start | bytes 2359304 | tf_op jit(solution)/shard_map/ppermute | solution.py:592
  20.3 10.0 %collective-permute-start.5 = (f32[272,128]{1,0:T(8,128)S(1)}, f32[272,128]{1,0:T(8,128)S(1)}, u32[]{:S(2)}, u32[]{:S(2)}) collective-permute-start(f32[272,128]{1,0:T(8,128)S(1)} %get-tuple-element.85), channel_id=1, source_target_pairs={{0,16},{32,48},{64,80},{96,112},{16,0},{48,32},{80,64},{112,96},{1... | collective-permute-start | bytes 417800 | tf_op jit(solution)/shard_map/ppermute | solution.py:592
  20.4 9.9 %collective-permute-start.6 = (f32[272,128]{1,0:T(8,128)S(1)}, f32[272,128]{1,0:T(8,128)S(1)}, u32[]{:S(2)}, u32[]{:S(2)}) collective-permute-start(f32[272,128]{1,0:T(8,128)S(1)} %get-tuple-element.86), channel_id=1, source_target_pairs={{16,32},{48,64},{80,96},{112,0},{32,16},{64,48},{96,80},{0,112},{1... | collective-permute-start | bytes 417800 | tf_op jit(solution)/shard_map/ppermute | solution.py:592
  22.5 4.9 %collective-permute-start.7 = (f32[96,128]{1,0:T(8,128)S(1)}, f32[96,128]{1,0:T(8,128)S(1)}, u32[]{:S(2)}, u32[]{:S(2)}) collective-permute-start(f32[96,128]{1,0:T(8,128)S(1)} %get-tuple-element.87), channel_id=1, source_target_pairs={{0,2},{4,6},{8,10},{12,14},{2,0},{6,4},{10,8},{14,12},{1,3},{5,7},... | collective-permute-start | bytes 147464 | tf_op jit(solution)/shard_map/ppermute | solution.py:592
  22.5 7.7 %collective-permute-start.8 = (f32[96,128]{1,0:T(8,128)S(1)}, f32[96,128]{1,0:T(8,128)S(1)}, u32[]{:S(2)}, u32[]{:S(2)}) collective-permute-start(f32[96,128]{1,0:T(8,128)S(1)} %get-tuple-element.88), channel_id=1, source_target_pairs={{2,4},{6,8},{10,12},{14,0},{4,2},{8,6},{12,10},{0,14},{3,5},{7,9},... | collective-permute-start | bytes 147464 | tf_op jit(solution)/shard_map/ppermute | solution.py:592
  31.8 10.9 %collective-permute-start.14 = (f32[48,32,128]{2,1,0:T(8,128)S(1)}, f32[48,32,128]{2,1,0:T(8,128)S(1)}, u32[]{:S(2)}, u32[]{:S(2)}) collective-permute-start(f32[48,32,128]{2,1,0:T(8,128)S(1)} %get-tuple-element.97), channel_id=1, source_target_pairs={{0,1},{1,0},{2,3},{3,2},{4,5},{5,4},{6,7},{7,6},{8,9},{9,8},{10,11... | collective-permute-start | bytes 2359304 | tf_op jit(solution)/shard_map/ppermute | solution.py:592
  31.9 10.8 %collective-permute-start.10 = (f32[272,128]{1,0:T(8,128)S(1)}, f32[272,128]{1,0:T(8,128)S(1)}, u32[]{:S(2)}, u32[]{:S(2)}) collective-permute-start(f32[272,128]{1,0:T(8,128)S(1)} %get-tuple-element.93), channel_id=1, source_target_pairs={{0,16},{32,48},{64,80},{96,112},{16,0},{48,32},{80,64},{112,96},{1... | collective-permute-start | bytes 417800 | tf_op jit(solution)/shard_map/ppermute | solution.py:592
  33.2 9.5 %collective-permute-start.11 = (f32[272,128]{1,0:T(8,128)S(1)}, f32[272,128]{1,0:T(8,128)S(1)}, u32[]{:S(2)}, u32[]{:S(2)}) collective-permute-start(f32[272,128]{1,0:T(8,128)S(1)} %get-tuple-element.94), channel_id=1, source_target_pairs={{16,32},{48,64},{80,96},{112,0},{32,16},{64,48},{96,80},{0,112},{1... | collective-permute-start | bytes 417800 | tf_op jit(solution)/shard_map/ppermute | solution.py:592
  34.9 5.3 %collective-permute-start.12 = (f32[96,128]{1,0:T(8,128)S(1)}, f32[96,128]{1,0:T(8,128)S(1)}, u32[]{:S(2)}, u32[]{:S(2)}) collective-permute-start(f32[96,128]{1,0:T(8,128)S(1)} %get-tuple-element.95), channel_id=1, source_target_pairs={{0,2},{4,6},{8,10},{12,14},{2,0},{6,4},{10,8},{14,12},{1,3},{5,7},... | collective-permute-start | bytes 147464 | tf_op jit(solution)/shard_map/ppermute | solution.py:592
  35.0 7.7 %collective-permute-start.13 = (f32[96,128]{1,0:T(8,128)S(1)}, f32[96,128]{1,0:T(8,128)S(1)}, u32[]{:S(2)}, u32[]{:S(2)}) collective-permute-start(f32[96,128]{1,0:T(8,128)S(1)} %get-tuple-element.96), channel_id=1, source_target_pairs={{2,4},{6,8},{10,12},{14,0},{4,2},{8,6},{12,10},{0,14},{3,5},{7,9},... | collective-permute-start | bytes 147464 | tf_op jit(solution)/shard_map/ppermute | solution.py:592
  44.7 4.7 %collective-permute-start.15 = (f32[49,32,128]{2,1,0:T(8,128)S(1)}, f32[49,32,128]{2,1,0:T(8,128)S(1)}, u32[]{:S(2)}, u32[]{:S(2)}) collective-permute-start(f32[49,32,128]{2,1,0:T(8,128)S(1)} %get-tuple-element.116), channel_id=1, source_target_pairs={{0,1},{1,0},{2,3},{3,2},{4,5},{5,4},{6,7},{7,6},{8,9},{9,8},{10,11... | collective-permute-start | bytes 2408456 | tf_op jit(solution)/shard_map/ppermute | solution.py:592
  44.8 12.6 %collective-permute-start.16 = (f32[272,128]{1,0:T(8,128)S(1)}, f32[272,128]{1,0:T(8,128)S(1)}, u32[]{:S(2)}, u32[]{:S(2)}) collective-permute-start(f32[272,128]{1,0:T(8,128)S(1)} %get-tuple-element.117), channel_id=1, source_target_pairs={{0,16},{32,48},{64,80},{96,112},{16,0},{48,32},{80,64},{112,96},{1... | collective-permute-start | bytes 417800 | tf_op jit(solution)/shard_map/ppermute | solution.py:592
  44.9 12.4 %collective-permute-start.17 = (f32[272,128]{1,0:T(8,128)S(1)}, f32[272,128]{1,0:T(8,128)S(1)}, u32[]{:S(2)}, u32[]{:S(2)}) collective-permute-start(f32[272,128]{1,0:T(8,128)S(1)} %get-tuple-element.118), channel_id=1, source_target_pairs={{16,32},{48,64},{80,96},{112,0},{32,16},{64,48},{96,80},{0,112},{1... | collective-permute-start | bytes 417800 | tf_op jit(solution)/shard_map/ppermute | solution.py:592
  47.5 9.9 %collective-permute-start.18 = (f32[96,128]{1,0:T(8,128)S(1)}, f32[96,128]{1,0:T(8,128)S(1)}, u32[]{:S(2)}, u32[]{:S(2)}) collective-permute-start(f32[96,128]{1,0:T(8,128)S(1)} %get-tuple-element.119), channel_id=1, source_target_pairs={{0,2},{4,6},{8,10},{12,14},{2,0},{6,4},{10,8},{14,12},{1,3},{5,7},... | collective-permute-start | bytes 147464 | tf_op jit(solution)/shard_map/ppermute | solution.py:592
  47.5 9.9 %collective-permute-start.19 = (f32[96,128]{1,0:T(8,128)S(1)}, f32[96,128]{1,0:T(8,128)S(1)}, u32[]{:S(2)}, u32[]{:S(2)}) collective-permute-start(f32[96,128]{1,0:T(8,128)S(1)} %get-tuple-element.120), channel_id=1, source_target_pairs={{2,4},{6,8},{10,12},{14,0},{4,2},{8,6},{12,10},{0,14},{3,5},{7,9},... | collective-permute-start | bytes 147464 | tf_op jit(solution)/shard_map/ppermute | solution.py:592
  49.4 8.0 %copy-start = (f32[49,32,128]{2,1,0:T(8,128)}, f32[49,32,128]{2,1,0:T(8,128)S(1)}, u32[]{:S(2)}) copy-start(f32[49,32,128]{2,1,0:T(8,128)S(1)} %collective-permute-done.15.zs_in.zs) | copy-start | bytes 2408452
  50.4 16.5 %all-to-all-start = ((f32[64,1,128]{2,1,0:T(1,128)}), f32[64,1,128]{2,1,0:T(1,128)S(1)}, u32[]{:S(2)}, u32[]{:S(2)}) async-start(f32[64,1,128]{2,1,0:T(1,128)} %bitcast.4), calls=%async_computation | async-start | bytes 65536 | tf_op jit(solution)/shard_map/all_to_all | solution.py:693

commit v5 on v4

--- a/solution.py
+++ b/solution.py
@@ -56,7 +56,7 @@
     return jax.ShapeDtypeStruct(dims, F32)
 
 
-PARTS = 3
+PARTS = 2
 HALF = 8
 def resident(*dims):
     return pltpu.VMEM(dims, F32)
@@ -481,7 +481,11 @@
     for x in range(CX):
         rows = slice(x * 32, x * 32 + 32)
         wide[rows, :] = slot[rows, :] * jnp.broadcast_to(lift[:, x : x + 1], (32, 128))
-    row = jnp.dot(group[...], wide[...], precision=HIGH, preferred_element_type=F32) + code[...]
+    row, rest = code[...], wide[...]
+    for _ in range(3):
+        part = rest.astype(jnp.bfloat16).astype(F32)
+        rest = rest - part
+        row = row + jnp.dot(group[...], part, preferred_element_type=F32)
     for i in range(8):
         out[i * 8 : i * 8 + 8, :] = row
 

time: 69.4 us -> 69.4 us (level)
  Pallas kernels: 23.7 us -> 22.9 us
  waiting for transfers between devices: 11.8 us -> 12.6 us
    pallas_call x11, Pallas kernels: 23.7 us -> 22.9 us  [call(): pl.pallas_call(body, out_shape=outs, in_specs=[VM] * len(args) if ins is...]
    ppermute x20, waiting for transfers between devices: 6.54 us -> 7.24 us  [swap(): return lax.ppermute(value, axis, pairs + [(j, i) for i, j in pairs])]
  transfers between devices with their start and end apart: 21 -> 21, of which waited for: 4 -> 4; matrix products, arithmetic and copies ran while one was open for 0% -> 0% of each run, Pallas kernels for 21% -> 20%
where the time goes in v5:
time: 69.4 us; the launch traced here: 69.2 us
  starting transfers between devices  32.6 us (47%)
  Pallas kernels  22.9 us (33%)
  waiting for transfers between devices  12.6 us (18%)
  between operations  1.04 us (1%)
    ppermute x20, starting transfers between devices, swap(): return lax.ppermute(value, axis, pairs + [(j, i) for i, j in pairs])  25.3 us
    pallas_call x11, Pallas kernels, call(): pl.pallas_call(body, out_shape=outs, in_specs=[VM] * len(args) if ins is...  22.9 us
    all_to_all x1, starting transfers between devices, local(): lax.all_to_all(out, ('gx', 'gy'), split_axis=0, concat_axis=0, tiled=True)  7.36 us
    ppermute x20, waiting for transfers between devices, swap(): return lax.ppermute(value, axis, pairs + [(j, i) for i, j in pairs])  7.24 us
    all_to_all x1, waiting for transfers between devices, local(): lax.all_to_all(out, ('gx', 'gy'), split_axis=0, concat_axis=0, tiled=True)  5.33 us
  transfers between devices with their start and end apart: 21, of which 4 were waited for; matrix products, arithmetic and copies ran while one was open for 0% of the time, Pallas kernels for 20%

profile of v5, /device:TPU:0, one launch (start us, length us, event | category | flops | bytes accessed | tf_op | source)
XLA Modules:
  0.0 69.2 jit_solution(18037165431461717007)
XLA Ops:
  0.6 1.9 %shard_map.130 = (f32[272,128]{1,0:T(8,128)S(1)}, f32[272,128]{1,0:T(8,128)S(1)}, f32[96,128]{1,0:T(8,128)S(1)}, f32[96,128]{1,0:T(8,128)S(1)}, f32[48,32,128]{2,1,0:T(8,128)S(1)}, /*index=5*/f32[768,128]{1,0:T(8,128)S(1)}) custom-call(f32[6,16,32,256]{3,2,1,0:T(8,128)} %s.1, f32[32,128]{1,0:T(8,128)} %depth.1, f32[32,128]{1,0:T(8,128)} %height_in.1, ...), custom_call_target="tpu_custom_call" | custom-call | tf_op jit(solution)/shard_map/pallas_call | solution.py:40
  2.5 0.1 collective-permute-start.4
  2.6 1.7 %collective-permute-start.2 = (f32[96,128]{1,0:T(8,128)S(1)}, f32[96,128]{1,0:T(8,128)S(1)}, u32[]{:S(2)}, u32[]{:S(2)}) collective-permute-start(f32[96,128]{1,0:T(8,128)S(1)} %get-tuple-element.74), channel_id=1, source_target_pairs={{0,2},{4,6},{8,10},{12,14},{2,0},{6,4},{10,8},{14,12},{1,3},{5,7},... | collective-permute-start | bytes 147464 | tf_op jit(solution)/shard_map/ppermute | solution.py:596
  4.3 4.7 %collective-permute-start.3 = (f32[96,128]{1,0:T(8,128)S(1)}, f32[96,128]{1,0:T(8,128)S(1)}, u32[]{:S(2)}, u32[]{:S(2)}) collective-permute-start(f32[96,128]{1,0:T(8,128)S(1)} %get-tuple-element.75), channel_id=1, source_target_pairs={{2,4},{6,8},{10,12},{14,0},{4,2},{8,6},{12,10},{0,14},{3,5},{7,9},... | collective-permute-start | bytes 147464 | tf_op jit(solution)/shard_map/ppermute | solution.py:596
  9.0 1.9 %collective-permute-start = (f32[272,128]{1,0:T(8,128)S(1)}, f32[272,128]{1,0:T(8,128)S(1)}, u32[]{:S(2)}, u32[]{:S(2)}) collective-permute-start(f32[272,128]{1,0:T(8,128)S(1)} %get-tuple-element.72), channel_id=1, source_target_pairs={{0,16},{32,48},{64,80},{96,112},{16,0},{48,32},{80,64},{112,96},{1... | collective-permute-start | bytes 417800 | tf_op jit(solution)/shard_map/ppermute | solution.py:596
  10.9 2.6 %collective-permute-start.1 = (f32[272,128]{1,0:T(8,128)S(1)}, f32[272,128]{1,0:T(8,128)S(1)}, u32[]{:S(2)}, u32[]{:S(2)}) collective-permute-start(f32[272,128]{1,0:T(8,128)S(1)} %get-tuple-element.73), channel_id=1, source_target_pairs={{16,32},{48,64},{80,96},{112,0},{32,16},{64,48},{96,80},{0,112},{1... | collective-permute-start | bytes 417800 | tf_op jit(solution)/shard_map/ppermute | solution.py:596
  13.6 3.5 %shard_map.129 = (f32[3,16,32,256]{3,2,1,0:T(8,128)S(1)}, f32[6,16,32,256]{3,2,1,0:T(8,128)S(1)}, s32[16,32,256]{2,1,0:T(8,128)S(1)}, f32[1,16,32,256]{3,2,1,0:T...) custom-call(f32[3,16,32,256]{3,2,1,0:T(8,128)} %v_hbm.1, ...), custom_call_target="tpu_custom_call" | custom-call | tf_op jit(solution)/shard_map/pallas_call | solution.py:40
  17.2 1.6 %collective-permute-done.1.xo = f32[272,128]{1,0:T(8,128)S(1)} collective-permute-done((f32[272,128]{1,0:T(8,128)S(1)}, f32[272,128]{1,0:T(8,128)S(1)}, u32[]{:S(2)}, u32[]{:S(2)}) %collective-permute-start.1) | collective-permute-done | bytes 139296 | tf_op jit(solution)/shard_map/ppermute | solution.py:596
  18.7 1.4 %shard_map.131 = (f32[3,16,32,256]{3,2,1,0:T(8,128)S(1)}, f32[272,128]{1,0:T(8,128)S(1)}, f32[272,128]{1,0:T(8,128)S(1)}, f32[96,128]{1,0:T(8,128)S(1)}, f32[96,...) custom-call(f32[3,16,32,256]{3,2,1,0:T(8,128)S(1)} %get-tuple-elemen, ...), custom_call_target="tpu_custom_call", output_to_operand_aliasing={{0}: (0, {}), {7}: (9, {})} | custom-call | tf_op jit(solution)/shard_map/pallas_call | solution.py:40
  20.2 0.1 collective-permute-start.9
  20.3 0.1 collective-permute-start.5
  20.4 2.2 %collective-permute-start.6 = (f32[272,128]{1,0:T(8,128)S(1)}, f32[272,128]{1,0:T(8,128)S(1)}, u32[]{:S(2)}, u32[]{:S(2)}) collective-permute-start(f32[272,128]{1,0:T(8,128)S(1)} %get-tuple-element.86), channel_id=1, source_target_pairs={{16,32},{48,64},{80,96},{112,0},{32,16},{64,48},{96,80},{0,112},{1... | collective-permute-start | bytes 417800 | tf_op jit(solution)/shard_map/ppermute | solution.py:596
  22.5 2.4 %collective-permute-start.8 = (f32[96,128]{1,0:T(8,128)S(1)}, f32[96,128]{1,0:T(8,128)S(1)}, u32[]{:S(2)}, u32[]{:S(2)}) collective-permute-start(f32[96,128]{1,0:T(8,128)S(1)} %get-tuple-element.88), channel_id=1, source_target_pairs={{2,4},{6,8},{10,12},{14,0},{4,2},{8,6},{12,10},{0,14},{3,5},{7,9},... | collective-permute-start | bytes 147464 | tf_op jit(solution)/shard_map/ppermute | solution.py:596
  25.0 2.2 %shard_map.132 = (f32[2,16,32,256]{3,2,1,0:T(8,128)S(1)}, f32[3,16,32,256]{3,2,1,0:T(8,128)S(1)}) custom-call(f32[24,128]{1,0:T(8,128)S(1)} %broadcast_bitcast_fusion.tab, s32[16,32,256]{2,1,0:T(8,128)S(1)} %get-tuple-element.82.mat, f32[3,16,32,256]{3,2,1,0:T(8,128)S(1)} %get-tuple-element.79.v), custom_call_target="tpu_custom_call" | custom-call | tf_op jit(solution)/shard_map/pallas_call | solution.py:40
  27.2 3.0 %collective-permute-done.8.yo = f32[96,128]{1,0:T(8,128)S(1)} collective-permute-done((f32[96,128]{1,0:T(8,128)S(1)}, f32[96,128]{1,0:T(8,128)S(1)}, u32[]{:S(2)}, u32[]{:S(2)}) %collective-permute-start.8) | collective-permute-done | bytes 49184 | tf_op jit(solution)/shard_map/ppermute | solution.py:596
  30.3 1.5 %shard_map.133 = (f32[6,16,32,256]{3,2,1,0:T(8,128)S(1)}, f32[272,128]{1,0:T(8,128)S(1)}, f32[272,128]{1,0:T(8,128)S(1)}, f32[96,128]{1,0:T(8,128)S(1)}, f32[96,...) custom-call(f32[6,16,32,256]{3,2,1,0:T(8,128)S(1)} %get-tuple-elemen, ...), custom_call_target="tpu_custom_call", output_to_operand_aliasing={{0}: (0, {}), {6}: (9, {})} | custom-call | tf_op jit(solution)/shard_map/pallas_call | solution.py:40
  31.8 0.1 collective-permute-start.14
  31.9 1.3 %collective-permute-start.10 = (f32[272,128]{1,0:T(8,128)S(1)}, f32[272,128]{1,0:T(8,128)S(1)}, u32[]{:S(2)}, u32[]{:S(2)}) collective-permute-start(f32[272,128]{1,0:T(8,128)S(1)} %get-tuple-element.93), channel_id=1, source_target_pairs={{0,16},{32,48},{64,80},{96,112},{16,0},{48,32},{80,64},{112,96},{1... | collective-permute-start | bytes 417800 | tf_op jit(solution)/shard_map/ppermute | solution.py:596
  33.2 1.8 %collective-permute-start.11 = (f32[272,128]{1,0:T(8,128)S(1)}, f32[272,128]{1,0:T(8,128)S(1)}, u32[]{:S(2)}, u32[]{:S(2)}) collective-permute-start(f32[272,128]{1,0:T(8,128)S(1)} %get-tuple-element.94), channel_id=1, source_target_pairs={{16,32},{48,64},{80,96},{112,0},{32,16},{64,48},{96,80},{0,112},{1... | collective-permute-start | bytes 417800 | tf_op jit(solution)/shard_map/ppermute | solution.py:596
  35.0 2.0 %collective-permute-start.13 = (f32[96,128]{1,0:T(8,128)S(1)}, f32[96,128]{1,0:T(8,128)S(1)}, u32[]{:S(2)}, u32[]{:S(2)}) collective-permute-start(f32[96,128]{1,0:T(8,128)S(1)} %get-tuple-element.96), channel_id=1, source_target_pairs={{2,4},{6,8},{10,12},{14,0},{4,2},{8,6},{12,10},{0,14},{3,5},{7,9},... | collective-permute-start | bytes 147464 | tf_op jit(solution)/shard_map/ppermute | solution.py:596
  36.9 0.6 shard_map.134.dzs
  37.5 2.5 %shard_map.135 = (f32[8,512]{1,0:T(8,128)S(1)}, f32[512,128]{1,0:T(8,128)S(1)}, f32[8,128]{1,0:T(8,128)S(1)}, f32[2,16,32,256]{3,2,1,0:T(8,128)}, f32[6,8,32,256]{3,2,1,0:T(8,128)}) custom-call(s32[1,512]{1,0:T(1,128)S(1)} %get-tuple-element.98.owner, s32[8,512]{1,0:T(8,128)S(1)} %get-tuple-element.99.cell, f32[2,16,32,256]{3,2,1,0:T(8,128)S(1)} %get-tuple-element.83.coef, ...), custom_call_target="tpu_custom_call" | custom-call | tf_op jit(solution)/shard_map/pallas_call | solution.py:40
  40.1 2.6 %collective-permute-done.13.yo = f32[96,128]{1,0:T(8,128)S(1)} collective-permute-done((f32[96,128]{1,0:T(8,128)S(1)}, f32[96,128]{1,0:T(8,128)S(1)}, u32[]{:S(2)}, u32[]{:S(2)}) %collective-permute-start.13) | collective-permute-done | bytes 49184 | tf_op jit(solution)/shard_map/ppermute | solution.py:596
  42.7 2.0 %shard_map.136 = (f32[272,128]{1,0:T(8,128)S(1)}, f32[272,128]{1,0:T(8,128)S(1)}, f32[96,128]{1,0:T(8,128)S(1)}, f32[96,128]{1,0:T(8,128)S(1)}, f32[49,32,128]{2...) custom-call(f32[3,16,32,256]{3,2,1,0:T(8,128)S(1)} %get-tuple-element.79.v, ...), custom_call_target="tpu_custom_call" | custom-call | tf_op jit(solution)/shard_map/pallas_call | solution.py:40
  44.8 0.2 collective-permute-start.16
  44.9 2.3 %collective-permute-start.17 = (f32[272,128]{1,0:T(8,128)S(1)}, f32[272,128]{1,0:T(8,128)S(1)}, u32[]{:S(2)}, u32[]{:S(2)}) collective-permute-start(f32[272,128]{1,0:T(8,128)S(1)} %get-tuple-element.118), channel_id=1, source_target_pairs={{16,32},{48,64},{80,96},{112,0},{32,16},{64,48},{96,80},{0,112},{1... | collective-permute-start | bytes 417800 | tf_op jit(solution)/shard_map/ppermute | solution.py:596
  47.3 1.7 %collective-permute-start.19 = (f32[96,128]{1,0:T(8,128)S(1)}, f32[96,128]{1,0:T(8,128)S(1)}, u32[]{:S(2)}, u32[]{:S(2)}) collective-permute-start(f32[96,128]{1,0:T(8,128)S(1)} %get-tuple-element.120), channel_id=1, source_target_pairs={{2,4},{6,8},{10,12},{14,0},{4,2},{8,6},{12,10},{0,14},{3,5},{7,9},... | collective-permute-start | bytes 147464 | tf_op jit(solution)/shard_map/ppermute | solution.py:596
  49.0 0.9 %shard_map.138 = f32[64,128]{1,0:T(8,128)} custom-call(f32[32,128]{1,0:T(8,128)S(1)} %get-tuple-element.122.lift_here, f32[49,32,128]{2,1,0:T(8,128)S(1)} %collective-permute-done.15.zs_in.zs, f32[8,512]{1,0:T(8,128)S(1)} %get-tuple-element.123.group, f32[512,128]{1,0:T(8,128)S(1)} %get-tuple-element.124.slot, f32[8,128]{1,0:T(8,128)S(1)} %get-tuple-element.125.code), custom_call_target="tpu_custom_call" | custom-call | tf_op jit(solution)/shard_map/pallas_call | solution.py:40
  50.0 7.4 %all-to-all-start = ((f32[64,1,128]{2,1,0:T(1,128)}), f32[64,1,128]{2,1,0:T(1,128)S(1)}, u32[]{:S(2)}, u32[]{:S(2)}) async-start(f32[64,1,128]{2,1,0:T(1,128)} %bitcast.4), calls=%async_computation | async-start | bytes 65536 | tf_op jit(solution)/shard_map/all_to_all | solution.py:697
  57.4 4.1 %shard_map.137 = (f32[6,16,32,256]{3,2,1,0:T(8,128)}, f32[80,128]{1,0:T(8,128)}) custom-call(f32[6,8,32,256]{3,2,1,0:T(8,128)} %get-tuple-element.113.s_low, f32[6,8,32,256]{3,2,1,0:T(8,128)} %get-tuple-element.114.s_high, f32[3,16,32,256]{3,2,1,0:T(8,128)} %get-tuple-element.63.v_in, f32[2,16,32,256]{3,2,1,0:T(8,128)} %get-tuple-element.115.coef_in, ...), custom_call_target="tpu_custom_call" | custom-call | tf_op jit(solution)/shard_map/pallas_call | solution.py:40
  61.5 5.3 %all-to-all-done = f32[64,1,128]{2,1,0:T(1,128)S(1)} async-done(((f32[64,1,128]{2,1,0:T(1,128)}), f32[64,1,128]{2,1,0:T(1,128)S(1)}, u32[]{:S(2)}, u32[]{:S(2)}) %all-to-all-start) | async-done | bytes 32800 | tf_op jit(solution)/shard_map/all_to_all | solution.py:697
  66.8 2.2 %shard_map.139 = (f32[32,128]{1,0:T(8,128)}, f32[32,128]{1,0:T(8,128)}) custom-call(f32[64,128]{1,0:T(8,128)S(1)} %bitcast.9, f32[80,128]{1,0:T(8,128)} %get-tuple-element.126.far_in, f32[768,128]{1,0:T(8,128)} %get-tuple-element.127.bag_in, f32[32,128]{1,0:T(8,128)} %height_in.1, f32[32,128]{1,0:T(8,128)} %current_in.1, s32[32,128]{1,0:T(8,128)} %wet_in.1), custom_call_target="tpu_custom_call" | custom-call | tf_op jit(solution)/shard_map/pallas_call | solution.py:40
  (30 shorter events, 0.2 us)
Async XLA Ops:
  0.6 12.9 %copy-start.1 = (f32[16,3]{0,1:T(4,128)S(1)}, f32[16,3]{0,1:T(4,128)}, u32[]{:S(2)}) copy-start(f32[16,3]{0,1:T(4,128)} %param.13) | copy-start | bytes 580
  2.5 16.2 %collective-permute-start.4 = (f32[48,32,128]{2,1,0:T(8,128)S(1)}, f32[48,32,128]{2,1,0:T(8,128)S(1)}, u32[]{:S(2)}, u32[]{:S(2)}) collective-permute-start(f32[48,32,128]{2,1,0:T(8,128)S(1)} %get-tuple-element.76), channel_id=1, source_target_pairs={{0,1},{1,0},{2,3},{3,2},{4,5},{5,4},{6,7},{7,6},{8,9},{9,8},{10,11... | collective-permute-start | bytes 2359304 | tf_op jit(solution)/shard_map/ppermute | solution.py:596
  2.6 14.5 %collective-permute-start.2 = (f32[96,128]{1,0:T(8,128)S(1)}, f32[96,128]{1,0:T(8,128)S(1)}, u32[]{:S(2)}, u32[]{:S(2)}) collective-permute-start(f32[96,128]{1,0:T(8,128)S(1)} %get-tuple-element.74), channel_id=1, source_target_pairs={{0,2},{4,6},{8,10},{12,14},{2,0},{6,4},{10,8},{14,12},{1,3},{5,7},... | collective-permute-start | bytes 147464 | tf_op jit(solution)/shard_map/ppermute | solution.py:596
  4.3 12.9 %collective-permute-start.3 = (f32[96,128]{1,0:T(8,128)S(1)}, f32[96,128]{1,0:T(8,128)S(1)}, u32[]{:S(2)}, u32[]{:S(2)}) collective-permute-start(f32[96,128]{1,0:T(8,128)S(1)} %get-tuple-element.75), channel_id=1, source_target_pairs={{2,4},{6,8},{10,12},{14,0},{4,2},{8,6},{12,10},{0,14},{3,5},{7,9},... | collective-permute-start | bytes 147464 | tf_op jit(solution)/shard_map/ppermute | solution.py:596
  9.0 8.1 %collective-permute-start = (f32[272,128]{1,0:T(8,128)S(1)}, f32[272,128]{1,0:T(8,128)S(1)}, u32[]{:S(2)}, u32[]{:S(2)}) collective-permute-start(f32[272,128]{1,0:T(8,128)S(1)} %get-tuple-element.72), channel_id=1, source_target_pairs={{0,16},{32,48},{64,80},{96,112},{16,0},{48,32},{80,64},{112,96},{1... | collective-permute-start | bytes 417800 | tf_op jit(solution)/shard_map/ppermute | solution.py:596
  10.9 7.8 %collective-permute-start.1 = (f32[272,128]{1,0:T(8,128)S(1)}, f32[272,128]{1,0:T(8,128)S(1)}, u32[]{:S(2)}, u32[]{:S(2)}) collective-permute-start(f32[272,128]{1,0:T(8,128)S(1)} %get-tuple-element.73), channel_id=1, source_target_pairs={{16,32},{48,64},{80,96},{112,0},{32,16},{64,48},{96,80},{0,112},{1... | collective-permute-start | bytes 417800 | tf_op jit(solution)/shard_map/ppermute | solution.py:596
  20.2 10.1 %collective-permute-start.9 = (f32[48,32,128]{2,1,0:T(8,128)S(1)}, f32[48,32,128]{2,1,0:T(8,128)S(1)}, u32[]{:S(2)}, u32[]{:S(2)}) collective-permute-start(f32[48,32,128]{2,1,0:T(8,128)S(1)} %get-tuple-element.89), channel_id=1, source_target_pairs={{0,1},{1,0},{2,3},{3,2},{4,5},{5,4},{6,7},{7,6},{8,9},{9,8},{10,11... | collective-permute-start | bytes 2359304 | tf_op jit(solution)/shard_map/ppermute | solution.py:596
  20.3 10.0 %collective-permute-start.5 = (f32[272,128]{1,0:T(8,128)S(1)}, f32[272,128]{1,0:T(8,128)S(1)}, u32[]{:S(2)}, u32[]{:S(2)}) collective-permute-start(f32[272,128]{1,0:T(8,128)S(1)} %get-tuple-element.85), channel_id=1, source_target_pairs={{0,16},{32,48},{64,80},{96,112},{16,0},{48,32},{80,64},{112,96},{1... | collective-permute-start | bytes 417800 | tf_op jit(solution)/shard_map/ppermute | solution.py:596
  20.4 9.9 %collective-permute-start.6 = (f32[272,128]{1,0:T(8,128)S(1)}, f32[272,128]{1,0:T(8,128)S(1)}, u32[]{:S(2)}, u32[]{:S(2)}) collective-permute-start(f32[272,128]{1,0:T(8,128)S(1)} %get-tuple-element.86), channel_id=1, source_target_pairs={{16,32},{48,64},{80,96},{112,0},{32,16},{64,48},{96,80},{0,112},{1... | collective-permute-start | bytes 417800 | tf_op jit(solution)/shard_map/ppermute | solution.py:596
  22.5 4.7 %collective-permute-start.7 = (f32[96,128]{1,0:T(8,128)S(1)}, f32[96,128]{1,0:T(8,128)S(1)}, u32[]{:S(2)}, u32[]{:S(2)}) collective-permute-start(f32[96,128]{1,0:T(8,128)S(1)} %get-tuple-element.87), channel_id=1, source_target_pairs={{0,2},{4,6},{8,10},{12,14},{2,0},{6,4},{10,8},{14,12},{1,3},{5,7},... | collective-permute-start | bytes 147464 | tf_op jit(solution)/shard_map/ppermute | solution.py:596
  22.5 7.7 %collective-permute-start.8 = (f32[96,128]{1,0:T(8,128)S(1)}, f32[96,128]{1,0:T(8,128)S(1)}, u32[]{:S(2)}, u32[]{:S(2)}) collective-permute-start(f32[96,128]{1,0:T(8,128)S(1)} %get-tuple-element.88), channel_id=1, source_target_pairs={{2,4},{6,8},{10,12},{14,0},{4,2},{8,6},{12,10},{0,14},{3,5},{7,9},... | collective-permute-start | bytes 147464 | tf_op jit(solution)/shard_map/ppermute | solution.py:596
  31.8 10.9 %collective-permute-start.14 = (f32[48,32,128]{2,1,0:T(8,128)S(1)}, f32[48,32,128]{2,1,0:T(8,128)S(1)}, u32[]{:S(2)}, u32[]{:S(2)}) collective-permute-start(f32[48,32,128]{2,1,0:T(8,128)S(1)} %get-tuple-element.97), channel_id=1, source_target_pairs={{0,1},{1,0},{2,3},{3,2},{4,5},{5,4},{6,7},{7,6},{8,9},{9,8},{10,11... | collective-permute-start | bytes 2359304 | tf_op jit(solution)/shard_map/ppermute | solution.py:596
  31.9 10.8 %collective-permute-start.10 = (f32[272,128]{1,0:T(8,128)S(1)}, f32[272,128]{1,0:T(8,128)S(1)}, u32[]{:S(2)}, u32[]{:S(2)}) collective-permute-start(f32[272,128]{1,0:T(8,128)S(1)} %get-tuple-element.93), channel_id=1, source_target_pairs={{0,16},{32,48},{64,80},{96,112},{16,0},{48,32},{80,64},{112,96},{1... | collective-permute-start | bytes 417800 | tf_op jit(solution)/shard_map/ppermute | solution.py:596
  33.2 9.5 %collective-permute-start.11 = (f32[272,128]{1,0:T(8,128)S(1)}, f32[272,128]{1,0:T(8,128)S(1)}, u32[]{:S(2)}, u32[]{:S(2)}) collective-permute-start(f32[272,128]{1,0:T(8,128)S(1)} %get-tuple-element.94), channel_id=1, source_target_pairs={{16,32},{48,64},{80,96},{112,0},{32,16},{64,48},{96,80},{0,112},{1... | collective-permute-start | bytes 417800 | tf_op jit(solution)/shard_map/ppermute | solution.py:596
  34.9 5.1 %collective-permute-start.12 = (f32[96,128]{1,0:T(8,128)S(1)}, f32[96,128]{1,0:T(8,128)S(1)}, u32[]{:S(2)}, u32[]{:S(2)}) collective-permute-start(f32[96,128]{1,0:T(8,128)S(1)} %get-tuple-element.95), channel_id=1, source_target_pairs={{0,2},{4,6},{8,10},{12,14},{2,0},{6,4},{10,8},{14,12},{1,3},{5,7},... | collective-permute-start | bytes 147464 | tf_op jit(solution)/shard_map/ppermute | solution.py:596
  35.0 7.7 %collective-permute-start.13 = (f32[96,128]{1,0:T(8,128)S(1)}, f32[96,128]{1,0:T(8,128)S(1)}, u32[]{:S(2)}, u32[]{:S(2)}) collective-permute-start(f32[96,128]{1,0:T(8,128)S(1)} %get-tuple-element.96), channel_id=1, source_target_pairs={{2,4},{6,8},{10,12},{14,0},{4,2},{8,6},{12,10},{0,14},{3,5},{7,9},... | collective-permute-start | bytes 147464 | tf_op jit(solution)/shard_map/ppermute | solution.py:596
  44.7 4.3 %collective-permute-start.15 = (f32[49,32,128]{2,1,0:T(8,128)S(1)}, f32[49,32,128]{2,1,0:T(8,128)S(1)}, u32[]{:S(2)}, u32[]{:S(2)}) collective-permute-start(f32[49,32,128]{2,1,0:T(8,128)S(1)} %get-tuple-element.116), channel_id=1, source_target_pairs={{0,1},{1,0},{2,3},{3,2},{4,5},{5,4},{6,7},{7,6},{8,9},{9,8},{10,11... | collective-permute-start | bytes 2408456 | tf_op jit(solution)/shard_map/ppermute | solution.py:596
  44.8 12.6 %collective-permute-start.16 = (f32[272,128]{1,0:T(8,128)S(1)}, f32[272,128]{1,0:T(8,128)S(1)}, u32[]{:S(2)}, u32[]{:S(2)}) collective-permute-start(f32[272,128]{1,0:T(8,128)S(1)} %get-tuple-element.117), channel_id=1, source_target_pairs={{0,16},{32,48},{64,80},{96,112},{16,0},{48,32},{80,64},{112,96},{1... | collective-permute-start | bytes 417800 | tf_op jit(solution)/shard_map/ppermute | solution.py:596
  44.9 12.4 %collective-permute-start.17 = (f32[272,128]{1,0:T(8,128)S(1)}, f32[272,128]{1,0:T(8,128)S(1)}, u32[]{:S(2)}, u32[]{:S(2)}) collective-permute-start(f32[272,128]{1,0:T(8,128)S(1)} %get-tuple-element.118), channel_id=1, source_target_pairs={{16,32},{48,64},{80,96},{112,0},{32,16},{64,48},{96,80},{0,112},{1... | collective-permute-start | bytes 417800 | tf_op jit(solution)/shard_map/ppermute | solution.py:596
  47.3 10.0 %collective-permute-start.18 = (f32[96,128]{1,0:T(8,128)S(1)}, f32[96,128]{1,0:T(8,128)S(1)}, u32[]{:S(2)}, u32[]{:S(2)}) collective-permute-start(f32[96,128]{1,0:T(8,128)S(1)} %get-tuple-element.119), channel_id=1, source_target_pairs={{0,2},{4,6},{8,10},{12,14},{2,0},{6,4},{10,8},{14,12},{1,3},{5,7},... | collective-permute-start | bytes 147464 | tf_op jit(solution)/shard_map/ppermute | solution.py:596
  47.3 10.0 %collective-permute-start.19 = (f32[96,128]{1,0:T(8,128)S(1)}, f32[96,128]{1,0:T(8,128)S(1)}, u32[]{:S(2)}, u32[]{:S(2)}) collective-permute-start(f32[96,128]{1,0:T(8,128)S(1)} %get-tuple-element.120), channel_id=1, source_target_pairs={{2,4},{6,8},{10,12},{14,0},{4,2},{8,6},{12,10},{0,14},{3,5},{7,9},... | collective-permute-start | bytes 147464 | tf_op jit(solution)/shard_map/ppermute | solution.py:596
  49.0 8.4 %copy-start = (f32[49,32,128]{2,1,0:T(8,128)}, f32[49,32,128]{2,1,0:T(8,128)S(1)}, u32[]{:S(2)}) copy-start(f32[49,32,128]{2,1,0:T(8,128)S(1)} %collective-permute-done.15.zs_in.zs) | copy-start | bytes 2408452
  50.0 16.9 %all-to-all-start = ((f32[64,1,128]{2,1,0:T(1,128)}), f32[64,1,128]{2,1,0:T(1,128)S(1)}, u32[]{:S(2)}, u32[]{:S(2)}) async-start(f32[64,1,128]{2,1,0:T(1,128)} %bitcast.4), calls=%async_computation | async-start | bytes 65536 | tf_op jit(solution)/shard_map/all_to_all | solution.py:697
